TPU v7x, 256 devices: a whole 4x4x8 slice. The times are simulated.
256 devices in a mesh: ty: 16 (over z_hi, y, core), tx: 16 (over x, z_lo).
Axes of the slice: x: 4, y: 4, z: 8 (z_hi: 2, z_lo: 4; z = z_hi * 4 + z_lo), core: 2. Of those that a mesh axis runs over, the one named last changes fastest.
Arguments:
- object_field: float32 [2, 8192, 8192], P(None, 'ty', 'tx'), may hold values from -5 to 5
- probe: float32 [2, 256, 256], replicated, may hold values from -5 to 5
- intensity: float32 [16, 16, 8, 256, 256], P('ty', 'tx'), may hold values from 0.05 to 4
- positions: int32 [2, 16, 16, 8], P(None, 'ty', 'tx'), may hold values from -128 to 384
- counts: int32 [16, 16], P('ty', 'tx'), may hold values from 1 to 8, as said below
Outputs:
- object_new: float32 [2, 8192, 8192], P(None, 'ty', 'tx')
- probe_new: float32 [2, 256, 256], replicated
Inputs may be any that keep to these rules, and one draw needn't show every extreme that they name: counts are skewed over tiles; some tile has 8.
All inputs are finite; a program needn't handle non-finite values.
Results may differ from a plain program's by a relative error of at most 0.00013.
Values sent between devices are 32-bit elements; how exact they have to be, the bound alone decides.
No kernel may reach another device: no remote copies, remote signals or barrier semaphores. Data moves between devices by JAX's collectives and lax.ppermute only.
A program may use at most 128 MiB of HBM per device.

v0:
```python
import jax
import jax.numpy as jnp
from jax import lax
from jax.sharding import PartitionSpec as P


def with_halo(block, sides, width):
    for axis, dim in sides:
        count = lax.axis_size(axis)
        forward = [(i, i + 1) for i in range(count - 1)]
        backward = [(target, source) for source, target in forward]
        low = lax.ppermute(
            lax.slice_in_dim(block, block.shape[dim] - width, None, axis=dim), axis, forward
        )
        high = lax.ppermute(lax.slice_in_dim(block, 0, width, axis=dim), axis, backward)
        block = jnp.concatenate([low, block, high], axis=dim)
    return block


def from_behind(value, axis, steps):
    count = lax.axis_size(axis)
    initial, last = (max(0, -steps), min(count, count - steps))
    return lax.ppermute(value, axis, [(source, source + steps) for source in range(initial, last)])


def dft_tables(size):
    index = jnp.arange(size, dtype=jnp.int32)
    product = index[:, None] * index[None, :] % size
    angle = product.astype(jnp.float32) * (2.0 * jnp.pi / size)
    scale = 1.0 / jnp.sqrt(jnp.float32(size))
    return (jnp.cos(angle) * scale, -jnp.sin(angle) * scale)


def matmul(left, right):
    return jnp.dot(left, right, precision=lax.Precision.HIGHEST, preferred_element_type=jnp.float32)


def transform(real, imag, table_re, table_im):
    first_re = matmul(table_re, real) - matmul(table_im, imag)
    first_im = matmul(table_re, imag) + matmul(table_im, real)
    out_re = matmul(first_re, table_re) - matmul(first_im, table_im)
    out_im = matmul(first_re, table_im) + matmul(first_im, table_re)
    return (out_re, out_im)


def slot_terms(patch_re, patch_im, probe_re, probe_im, measured, table_re, table_im):
    exit_re = probe_re * patch_re - probe_im * patch_im
    exit_im = probe_re * patch_im + probe_im * patch_re
    wave_re, wave_im = transform(exit_re, exit_im, table_re, table_im)
    excess = wave_re * wave_re + wave_im * wave_im - measured
    chi_re, chi_im = transform(excess * wave_re, excess * wave_im, table_re, -table_im)
    obj_re = probe_re * chi_re + probe_im * chi_im
    obj_im = probe_re * chi_im - probe_im * chi_re
    obj_wt = probe_re * probe_re + probe_im * probe_im
    prb_re = patch_re * chi_re + patch_im * chi_im
    prb_im = patch_re * chi_im - patch_im * chi_re
    prb_wt = patch_re * patch_re + patch_im * patch_im
    return (jnp.stack([obj_re, obj_im, obj_wt]), jnp.stack([prb_re, prb_im, prb_wt]))


def per_device(object_field, probe, intensity, positions, counts):
    tile = object_field.shape[1]
    patch = probe.shape[1]
    half = patch // 2
    table_re, table_im = dft_tables(patch)
    canvas = with_halo(object_field, (("ty", 1), ("tx", 2)), half)
    side = tile + 2 * half
    row_at = positions[0, 0, 0, :] + half
    col_at = positions[1, 0, 0, :] + half
    live_count = counts[0, 0]
    measured_all = intensity[0, 0]

    def step(slot, carry):
        grid, acc = carry
        zero = jnp.zeros((), jnp.int32)
        row_pos = row_at[slot]
        col_pos = col_at[slot]
        window = lax.dynamic_slice(canvas, (zero, row_pos, col_pos), (2, patch, patch))
        obj_terms, prb_terms = slot_terms(
            window[0], window[1], probe[0], probe[1], measured_all[slot], table_re, table_im
        )
        old = lax.dynamic_slice(grid, (zero, row_pos, col_pos), (3, patch, patch))
        grid = lax.dynamic_update_slice(grid, old + obj_terms, (zero, row_pos, col_pos))
        return (grid, acc + prb_terms)

    grid = jnp.zeros((3, side, side), jnp.float32)
    probe_acc = jnp.zeros((3, patch, patch), jnp.float32)
    grid, probe_acc = lax.fori_loop(0, live_count, step, (grid, probe_acc))
    from_right = from_behind(grid[:, :, :half], "tx", -1)
    from_left = from_behind(grid[:, :, tile + half :], "tx", 1)
    grid = grid.at[:, :, tile : tile + half].add(from_right)
    grid = grid.at[:, :, half : 2 * half].add(from_left)
    middle = grid[:, :, half : half + tile]
    from_below = from_behind(middle[:, :half, :], "ty", -1)
    from_above = from_behind(middle[:, tile + half :, :], "ty", 1)
    middle = middle.at[:, tile : tile + half, :].add(from_below)
    middle = middle.at[:, half : 2 * half, :].add(from_above)
    inner = middle[:, half : half + tile, :]
    object_new = object_field - inner[:2] / (inner[2] + 1.0)
    totals = lax.psum(probe_acc, ("ty", "tx"))
    probe_new = probe - totals[:2] / jnp.sqrt(totals[2] + 1.0)
    return (object_new, probe_new)


def solution(mesh):
    in_specs = (
        P(None, "ty", "tx"),
        P(),
        P("ty", "tx", None, None, None),
        P(None, "ty", "tx", None),
        P("ty", "tx"),
    )
    out_specs = (P(None, "ty", "tx"), P())
    return jax.shard_map(
        per_device, mesh=mesh, in_specs=in_specs, out_specs=out_specs, check_vma=False
    )
```

profile of v0, /device:TPU:1, one launch (start us, length us, event | category | flops | bytes accessed | tf_op | source)
XLA Modules:
  0.0 718.3 jit_solution(2394600600357687286)
XLA Ops:
  8.7 4.6 collective-permute-start
  13.3 1.9 collective-permute-start.1
  15.2 4.2 collective-permute-done
  19.6 4.1 collective-permute-done.1
  23.8 1.6 copy-done.4
  26.4 3.6 collective-permute-start.2
  31.4 15.6 %collective-permute-done.2 = f32[2,768,128]{2,1,0:T(8,128)S(1)} collective-permute-done((f32[2,768,128]{2,1,0:T(8,128)}, f32[2,768,128]{2,1,0:T(8,128)S(1)}, u32[]{:S(2)}, u32[]{:S(2)}) %collective-permute-start.2) | collective-permute-done | bytes 786464 | tf_op jit(solution)/shard_map/ppermute | solution.py:12
  47.0 14.1 %collective-permute-done.3 = f32[2,768,128]{2,1,0:T(8,128)S(1)} collective-permute-done((f32[2,768,128]{2,1,0:T(8,128)S(1)}, f32[2,768,128]{2,1,0:T(8,128)S(1)}, u32[]{:S(2)}, u32[]{:S(2)}) %collective-permute-start.3) | collective-permute-done | bytes 786464 | tf_op jit(solution)/shard_map/ppermute | solution.py:15
  61.1 4.4 pad_maximum_fusion
  65.6 3.4 broadcast_in_dim.4
  69.0 90.9 %while.20 = (s32[]{:T(128)}, f32[3,768,768]{2,1,0:T(8,128)}, f32[3,256,256]{2,1,0:T(8,128)S(1)}, s32[]{:T(128)}, s32[8]{0:T(128)S(1)}, /*index=5*/s32[8]{0:T(128...) while((s32[]{:T(128)}, f32[3,768,768]{2,1,0:T(8,128)}, ...), condition=%wide.region_1.2_spmd.clone.clone, body=%wide.region_0.1_spmd.clone.clone.sunk | while | flops 3241213952 | bytes 22020436 | solution.py:88
  78.9 1.5 convolution_subtract_fusion.7
  80.4 1.5 fusion.200
  81.9 1.5 convolution_add_fusion.7
  83.4 1.5 fusion.201
  86.3 1.5 convolution_subtract_fusion.8
  87.8 2.4 fusion.202
  90.2 1.5 fusion.203
  91.7 1.5 convolution_subtract_fusion.9
  94.6 1.5 convolution_add_fusion.8
  97.6 1.5 fusion.204
  100.6 2.7 fusion.207
  103.3 1.8 maximum_add_fusion.3
  105.1 9.4 %dynamic_update_slice.8 = f32[3,768,768]{2,1,0:T(8,128)} dynamic-update-slice(f32[3,768,768]{2,1,0:T(8,128)} %get-tuple-element.446, f32[3,256,256]{2,1,0:T(8,128)S(1)} %get-tuple-element.428, s32[]{:T(128)} %constant.143.clone.1..sunk, s32[]{:T(128)S(6)} %select_n.150, s32[]{:T(128)S(6)} %select_n.151) | dynamic-update-slice | bytes 1572868 | tf_op jit(solution)/shard_map/while/body/dynamic_update_slice | solution.py:83
  122.9 1.5 fusion.198
  124.3 1.5 convolution_subtract_fusion.7
  127.3 1.5 convolution_add_fusion.7
  128.8 1.5 fusion.201
  131.7 1.5 convolution_subtract_fusion.8
  133.2 2.4 fusion.202
  137.1 1.5 convolution_subtract_fusion.9
  140.1 1.5 convolution_add_fusion.8
  143.0 1.5 fusion.204
  146.0 2.7 fusion.207
  148.7 1.8 maximum_add_fusion.3
  150.5 8.6 %dynamic_update_slice.8 = f32[3,768,768]{2,1,0:T(8,128)} dynamic-update-slice(f32[3,768,768]{2,1,0:T(8,128)} %get-tuple-element.446, f32[3,256,256]{2,1,0:T(8,128)S(1)} %get-tuple-element.428, s32[]{:T(128)} %constant.143.clone.1..sunk, s32[]{:T(128)S(6)} %select_n.150, s32[]{:T(128)S(6)} %select_n.151) | dynamic-update-slice | bytes 1572868 | tf_op jit(solution)/shard_map/while/body/dynamic_update_slice | solution.py:83
  159.9 3.6 fusion.125
  164.8 4.1 collective-permute-start.5
  168.9 18.3 %collective-permute-done.4 = f32[3,768,128]{2,1,0:T(8,128)} collective-permute-done((f32[3,768,128]{2,1,0:T(8,128)}, f32[3,768,128]{2,1,0:T(8,128)}, u32[]{:S(2)}, u32[]{:S(2)}) %collective-permute-start.4) | collective-permute-done | bytes 1179680 | tf_op jit(solution)/shard_map/ppermute | solution.py:23
  187.2 2.8 add_dynamic-update-slice_fusion
  190.1 2.5 fusion.117
  192.6 2.4 fusion.124
  195.0 8.8 %collective-permute-start.6 = (f32[3,128,512]{2,1,0:T(8,128)}, f32[3,128,512]{2,1,0:T(8,128)S(1)}, u32[]{:S(2)}, u32[]{:S(2)}) collective-permute-start(f32[3,128,512]{2,1,0:T(8,128)} %get-tuple-element.339), channel_id=1, source_target_pairs={{16,0},{32,16},{48,32},{64,48},{80,64},{96,80},{112,96},{128,112},... | collective-permute-start | bytes 2359304 | tf_op jit(solution)/shard_map/ppermute | solution.py:23
  203.8 97.8 %collective-permute-start.7 = (f32[3,128,512]{2,1,0:T(8,128)S(1)}, f32[3,128,512]{2,1,0:T(8,128)S(1)}, u32[]{:S(2)}, u32[]{:S(2)}) collective-permute-start(f32[3,128,512]{2,1,0:T(8,128)S(1)} %get-tuple-element.338), channel_id=1, source_target_pairs={{0,16},{16,32},{32,48},{48,64},{64,80},{80,96},{96,112},{112,128},... | collective-permute-start | bytes 2359304 | tf_op jit(solution)/shard_map/ppermute | solution.py:23
  301.6 400.3 %all-reduce.2.cloned.1.call-done = f32[3,256,256]{2,1,0:T(8,128)} async-done(((f32[3,256,256]{2,1,0:T(8,128)}), f32[3,256,256]{2,1,0:T(8,128)}) %all-reduce.2.cloned.1.call-update) | async-done | bytes 786448 | tf_op jit(solution)/shard_map/psum | solution.py:100
  702.9 1.9 fusion.121
  704.8 2.8 slice.205
  709.5 2.0 fusion.116
  (49 shorter events, 32.0 us)
Async XLA Ops:
  7.2 12.2 %copy-start.2 = (f32[2,512,512]{2,1,0:T(8,128)S(1)}, f32[2,512,512]{2,1,0:T(8,128)}, u32[]{:S(2)}) copy-start(f32[2,512,512]{2,1,0:T(8,128)} %param.15) | copy-start | bytes 6291460
  7.2 694.7 %all-reduce.2.cloned.1.call-start = ((), (), s32[]{:S(2)}) async-start(), calls=%async_computation | async-start | bytes 1572864 | tf_op jit(solution)/shard_map/psum | solution.py:100
  8.7 10.7 %collective-permute-start = (f32[2,128,512]{2,1,0:T(8,128)S(1)}, f32[2,128,512]{2,1,0:T(8,128)S(1)}, u32[]{:S(2)}, u32[]{:S(2)}) collective-permute-start(f32[2,128,512]{2,1,0:T(8,128)S(1)} %get-tuple-element.345), channel_id=1, source_target_pairs={{0,16},{16,32},{32,48},{48,64},{64,80},{80,96},{96,112},{112,128},... | collective-permute-start | bytes 1572872 | tf_op jit(solution)/shard_map/ppermute | solution.py:12
  13.3 10.5 %collective-permute-start.1 = (f32[2,128,512]{2,1,0:T(8,128)S(1)}, f32[2,128,512]{2,1,0:T(8,128)S(1)}, u32[]{:S(2)}, u32[]{:S(2)}) collective-permute-start(f32[2,128,512]{2,1,0:T(8,128)S(1)} %get-tuple-element.344), channel_id=1, source_target_pairs={{16,0},{32,16},{48,32},{64,48},{80,64},{96,80},{112,96},{128,112},... | collective-permute-start | bytes 1572872 | tf_op jit(solution)/shard_map/ppermute | solution.py:15
  19.6 11.7 %copy-start.5 = (s32[2,1,1,8]{3,2,1,0:T(1,128)S(1)}, s32[2,1,1,8]{3,2,1,0:T(1,128)}, u32[]{:S(2)}) copy-start(s32[2,1,1,8]{3,2,1,0:T(1,128)} %param.18) | copy-start | bytes 196
  19.6 11.7 %copy-start = (f32[2,256,256]{2,1,0:T(8,128)S(1)}, f32[2,256,256]{2,1,0:T(8,128)}, u32[]{:S(2)}) copy-start(f32[2,256,256]{2,1,0:T(8,128)} %param.16) | copy-start | bytes 1572868
  23.8 1.6 copy-start.4
  26.4 20.6 %collective-permute-start.2 = (f32[2,768,128]{2,1,0:T(8,128)}, f32[2,768,128]{2,1,0:T(8,128)S(1)}, u32[]{:S(2)}, u32[]{:S(2)}) collective-permute-start(f32[2,768,128]{2,1,0:T(8,128)} %get-tuple-element.342), channel_id=1, source_target_pairs={{0,1},{1,2},{2,3},{3,4},{4,5},{5,6},{6,7},{7,8},{8,9},{9,10},{10,1... | collective-permute-start | bytes 2359304 | tf_op jit(solution)/shard_map/ppermute | solution.py:12
  30.0 31.1 %collective-permute-start.3 = (f32[2,768,128]{2,1,0:T(8,128)S(1)}, f32[2,768,128]{2,1,0:T(8,128)S(1)}, u32[]{:S(2)}, u32[]{:S(2)}) collective-permute-start(f32[2,768,128]{2,1,0:T(8,128)S(1)} %get-tuple-element.343), channel_id=1, source_target_pairs={{1,0},{2,1},{3,2},{4,3},{5,4},{6,5},{7,6},{8,7},{9,8},{10,9},{11,1... | collective-permute-start | bytes 2359304 | tf_op jit(solution)/shard_map/ppermute | solution.py:15
  159.9 8.9 %copy-start.1 = (f32[3,256,256]{2,1,0:T(8,128)}, f32[3,256,256]{2,1,0:T(8,128)S(1)}, u32[]{:S(2)}) copy-start(f32[3,256,256]{2,1,0:T(8,128)S(1)} %get-tuple-element.233) | copy-start | bytes 2359300
  163.5 23.7 %collective-permute-start.4 = (f32[3,768,128]{2,1,0:T(8,128)}, f32[3,768,128]{2,1,0:T(8,128)}, u32[]{:S(2)}, u32[]{:S(2)}) collective-permute-start(f32[3,768,128]{2,1,0:T(8,128)} %get-tuple-element.341), channel_id=1, source_target_pairs={{1,0},{2,1},{3,2},{4,3},{5,4},{6,5},{7,6},{8,7},{9,8},{10,9},{11,1... | collective-permute-start | bytes 3538952 | tf_op jit(solution)/shard_map/ppermute | solution.py:23
  164.8 25.3 %collective-permute-start.5 = (f32[3,768,128]{2,1,0:T(8,128)}, f32[3,768,128]{2,1,0:T(8,128)S(1)}, u32[]{:S(2)}, u32[]{:S(2)}) collective-permute-start(f32[3,768,128]{2,1,0:T(8,128)} %get-tuple-element.340), channel_id=1, source_target_pairs={{0,1},{1,2},{2,3},{3,4},{4,5},{5,6},{6,7},{7,8},{8,9},{9,10},{10,1... | collective-permute-start | bytes 3538952 | tf_op jit(solution)/shard_map/ppermute | solution.py:23
  195.0 512.7 %collective-permute-start.6 = (f32[3,128,512]{2,1,0:T(8,128)}, f32[3,128,512]{2,1,0:T(8,128)S(1)}, u32[]{:S(2)}, u32[]{:S(2)}) collective-permute-start(f32[3,128,512]{2,1,0:T(8,128)} %get-tuple-element.339), channel_id=1, source_target_pairs={{16,0},{32,16},{48,32},{64,48},{80,64},{96,80},{112,96},{128,112},... | collective-permute-start | bytes 2359304 | tf_op jit(solution)/shard_map/ppermute | solution.py:23
  203.8 505.4 %collective-permute-start.7 = (f32[3,128,512]{2,1,0:T(8,128)S(1)}, f32[3,128,512]{2,1,0:T(8,128)S(1)}, u32[]{:S(2)}, u32[]{:S(2)}) collective-permute-start(f32[3,128,512]{2,1,0:T(8,128)S(1)} %get-tuple-element.338), channel_id=1, source_target_pairs={{0,16},{16,32},{32,48},{48,64},{64,80},{80,96},{96,112},{112,128},... | collective-permute-start | bytes 2359304 | tf_op jit(solution)/shard_map/ppermute | solution.py:23
  707.7 1.8 copy-start.3
Sparse Core Ops, SparseCore 0:
  169.0 532.8 all-reduce.1
where the time goes:
time: 723 us; the launch traced here: 718 us
  waiting for transfers between devices  457 us (63%)
  starting transfers between devices  123 us (17%)
  matrix products  51.4 us (7%)
  local copies, waits for them, and re-layouts  37 us (5%)
  other arithmetic  25.4 us (4%)
  between operations  14.3 us (2%)
  loops' own time  10.2 us (1%)
    psum x1, waiting for transfers between devices, per_device(): totals = lax.psum(probe_acc, ('ty', 'tx'))  400 us
    ppermute x4, starting transfers between devices, from_behind(): lax.ppermute(value, axis, [(source, source + steps) for source in range(i...  112 us
    dot_general x32, matrix products, matmul(): jnp.dot(left, right, precision=lax.Precision.HIGHEST, preferred_element_t...  51.4 us
    ppermute x2, waiting for transfers between devices, with_halo(): lax.ppermute(lax.slice_in_dim(block, block.shape[dim] - width, None, axis...  19.8 us
    ppermute x4, waiting for transfers between devices, from_behind(): lax.ppermute(value, axis, [(source, source + steps) for source in range(i...  18.3 us
    ppermute x2, waiting for transfers between devices, with_halo(): lax.ppermute(lax.slice_in_dim(block, 0, width, axis=dim), axis, backward)  18.3 us
    dynamic_update_slice x2, local copies, waits for them, and re-layouts, step(): lax.dynamic_update_slice(grid, old + obj_terms, (zero, row_pos, col_pos))  17.9 us
  transfers between devices with their start and end apart: 9, of which 6 were waited for; matrix products, arithmetic and copies ran while one was open for 2% of the time, Pallas kernels for 0%

commit v1 on v0

v1 whole, which is shorter than its diff:
```python
import numpy as np
import ml_dtypes
import jax
import jax.numpy as jnp
from jax import lax
from jax.experimental import pallas as pl
from jax.experimental.pallas import tpu as pltpu
from jax.sharding import PartitionSpec as P

BF16 = jnp.bfloat16
F32 = jnp.float32
LANES = 128
VMEM = pl.BlockSpec(memory_space=pltpu.VMEM)
SMEM = pl.BlockSpec(memory_space=pltpu.SMEM)
ANY = pl.BlockSpec(memory_space=pl.ANY)
AROUND = ((-1, 0), (1, 0), (0, -1), (0, 1), (-1, -1), (-1, 1), (1, -1), (1, 1))


def split_host(table):
    high = table.astype(ml_dtypes.bfloat16)
    low = (table - high.astype(np.float64)).astype(ml_dtypes.bfloat16)
    return high, low


def half_tables(size):
    half = size // 2
    left, right = [], []
    for parity in range(2):
        product = (2 * np.arange(half)[:, None] + parity) * np.arange(half)[None, :] % size
        angle = 2.0 * np.pi * product / size
        cos, sin = np.cos(angle) / np.sqrt(size), np.sin(angle) / np.sqrt(size)
        base = np.block([[cos, sin], [-sin, cos]])
        for table in (base, base.T):
            high, low = split_host(table)
            left.append(np.concatenate([high, high, low], axis=1))
            right.append(np.concatenate([high, high, low], axis=0))
    return np.stack(left), np.stack(right)


def parity_tables(size):
    order = np.concatenate([np.arange(0, size, 2), np.arange(1, size, 2)])
    gather = np.eye(size)[order].astype(ml_dtypes.bfloat16)
    return np.concatenate([gather] * 3, axis=1), np.concatenate([gather.T] * 3, axis=0)


def matmul(left, right):
    return jnp.dot(left, right, preferred_element_type=F32)


def split(value):
    high = value.astype(BF16)
    return high, (value - high.astype(F32)).astype(BF16)


def put_rows(ref, start, columns, value):
    rows = value.shape[0]
    high, low = split(value)
    third = ref.shape[0] // 3
    ref[start : start + rows, columns] = high
    ref[third + start : third + start + rows, columns] = low
    ref[2 * third + start : 2 * third + start + rows, columns] = high


def put_columns(ref, rows, start, value):
    width = value.shape[1]
    high, low = split(value)
    third = ref.shape[1] // 3
    ref[rows, start : start + width] = high
    ref[rows, third + start : third + start + width] = low
    ref[rows, 2 * third + start : 2 * third + start + width] = high


def place(position, slot, half):
    row = position[0, slot] + half
    col = position[1, slot] + half
    tile = jnp.minimum(lax.shift_right_logical(col, 7), 3)
    return row, tile, col - tile * LANES


def add_window(accumulate, row, tile, offset, first, second):
    rows = first.shape[0]
    turn = jnp.bitwise_and(offset, LANES - 1)
    kept = lax.broadcasted_iota(jnp.int32, first.shape, 1) >= offset
    first = pltpu.roll(first, turn, 1)
    second = pltpu.roll(second, turn, 1)
    where = pl.ds(row, rows)
    accumulate[tile, where, :] += jnp.where(kept, first, 0.0)
    accumulate[tile + 1, where, :] += jnp.where(kept, second, first)
    accumulate[tile + 2, where, :] += jnp.where(kept, 0.0, second)


def early_kernel(position, count, probe, measured, gather_left, gather_right, folded, weight, parts):
    size = probe.shape[1]
    half = size // 2
    weight[...] = jnp.zeros_like(weight)

    def step(slot, carry):
        row, tile, offset = place(position, slot, half)
        pieces = []
        for start in (0, LANES):
            columns = slice(start, start + LANES)
            pieces.append(probe[0, :, columns] * probe[0, :, columns] + probe[1, :, columns] * probe[1, :, columns])
        add_window(weight, row, tile, offset, *pieces)

        def three(value):
            high = value.astype(BF16)
            rest = value - high.astype(F32)
            middle = rest.astype(BF16)
            return high, middle, (rest - middle.astype(F32)).astype(BF16)

        for index, part in enumerate(three(measured[slot])):
            parts[:, index * size : (index + 1) * size] = part
        value = matmul(parts[...], gather_right[...])
        value = jnp.concatenate(three(value), axis=0)
        folded[slot] = matmul(gather_left[...], value)
        return carry

    lax.fori_loop(0, count[0], step, 0)


def slot_kernel(
    position, count, probe, folded, left, right, tile_ref, top, bottom, low, high, top_low, top_high, bottom_low,
    bottom_high, grad, probe_sum, canvas, patch, rhs, lhs, sems,
):
    size = probe.shape[1]
    half = size // 2
    side = tile_ref.shape[1]
    tiles = side // LANES
    inner = slice(half, half + side)
    copies = []

    def fetch(source, target):
        copy = pltpu.make_async_copy(source, target, sems.at[len(copies)])
        copy.start()
        copies.append(copy)

    for index in range(tiles):
        columns = slice(index * LANES, (index + 1) * LANES)
        fetch(tile_ref.at[:, :, columns], canvas.at[:, 1 + index, inner, :])
        fetch(top.at[:, :, columns], canvas.at[:, 1 + index, :half, :])
        fetch(bottom.at[:, :, columns], canvas.at[:, 1 + index, half + side :, :])
    fetch(low, canvas.at[:, 0, inner, :])
    fetch(high, canvas.at[:, 1 + tiles, inner, :])
    fetch(top_low, canvas.at[:, 0, :half, :])
    fetch(top_high, canvas.at[:, 1 + tiles, :half, :])
    fetch(bottom_low, canvas.at[:, 0, half + side :, :])
    fetch(bottom_high, canvas.at[:, 1 + tiles, half + side :, :])
    grad[...] = jnp.zeros_like(grad)
    probe_sum[...] = jnp.zeros_like(probe_sum)
    for copy in copies:
        copy.wait()
    near, far = slice(0, half), slice(half, size)

    def step(slot, carry):
        row, tile, offset = place(position, slot, half)
        turn = jnp.bitwise_and(LANES - offset, LANES - 1)
        kept = lax.broadcasted_iota(jnp.int32, (size, LANES), 1) < LANES - offset
        for plane in range(2):
            raw = [pltpu.roll(canvas[plane, tile + index, pl.ds(row, size), :], turn, 1) for index in range(3)]
            patch[plane, :, near] = jnp.where(kept, raw[0], raw[1])
            patch[plane, :, far] = jnp.where(kept, raw[1], raw[2])
        for columns in (near, far):
            probe_re, probe_im = probe[0, :, columns], probe[1, :, columns]
            patch_re, patch_im = patch[0, :, columns], patch[1, :, columns]
            exit_re = probe_re * patch_re - probe_im * patch_im
            exit_im = probe_re * patch_im + probe_im * patch_re
            probe_sum[2, :, columns] += patch_re * patch_re + patch_im * patch_im
            put_rows(rhs.at[0], 0, columns, exit_re[:half] + exit_re[half:])
            put_rows(rhs.at[0], half, columns, exit_im[:half] + exit_im[half:])
            put_rows(rhs.at[1], 0, columns, exit_re[:half] - exit_re[half:])
            put_rows(rhs.at[1], half, columns, exit_im[:half] - exit_im[half:])
        for parity in range(2):
            value = matmul(left[2 * parity], rhs[parity])
            rows = slice(parity * half, (parity + 1) * half)
            put_columns(lhs.at[0], rows, 0, value[:half, near] + value[:half, far])
            put_columns(lhs.at[0], rows, half, value[half:, near] + value[half:, far])
            put_columns(lhs.at[1], rows, 0, value[:half, near] - value[:half, far])
            put_columns(lhs.at[1], rows, half, value[half:, near] - value[half:, far])
        everything = slice(0, size)
        back = []
        for parity in range(2):
            value = matmul(lhs[parity], right[2 * parity + 1])
            wave_re, wave_im = value[:, near], value[:, far]
            columns = slice(parity * half, (parity + 1) * half)
            excess = wave_re * wave_re + wave_im * wave_im - folded[slot, :, columns]
            put_columns(lhs.at[parity], everything, 0, excess * wave_re)
            put_columns(lhs.at[parity], everything, half, excess * wave_im)
            back.append(matmul(lhs[parity], right[2 * parity]))
        for parity in range(2):
            rows = slice(parity * half, (parity + 1) * half)
            put_rows(rhs.at[parity], 0, near, back[0][rows, near] + back[1][rows, near])
            put_rows(rhs.at[parity], half, near, back[0][rows, far] + back[1][rows, far])
            put_rows(rhs.at[parity], 0, far, back[0][rows, near] - back[1][rows, near])
            put_rows(rhs.at[parity], half, far, back[0][rows, far] - back[1][rows, far])
        even = matmul(left[1], rhs[0])
        odd = matmul(left[3], rhs[1])
        pieces = []
        for columns in (near, far):
            chi_re = jnp.concatenate([even[:half, columns] + odd[:half, columns], even[:half, columns] - odd[:half, columns]], axis=0)
            chi_im = jnp.concatenate([even[half:, columns] + odd[half:, columns], even[half:, columns] - odd[half:, columns]], axis=0)
            probe_re, probe_im = probe[0, :, columns], probe[1, :, columns]
            patch_re, patch_im = patch[0, :, columns], patch[1, :, columns]
            probe_sum[0, :, columns] += patch_re * chi_re + patch_im * chi_im
            probe_sum[1, :, columns] += patch_re * chi_im - patch_im * chi_re
            pieces.append((probe_re * chi_re + probe_im * chi_im, probe_re * chi_im - probe_im * chi_re))
        for plane in range(2):
            add_window(grad.at[plane], row, tile, offset, pieces[0][plane], pieces[1][plane])
        return carry

    lax.fori_loop(0, count[0], step, 0)


def final_kernel(tile_ref, grad, weight, *refs):
    grads, weights, out = refs[:8], refs[8:16], refs[16]
    half = LANES
    tiles = tile_ref.shape[2] // LANES
    side = tile_ref.shape[1]
    for index in range(tiles):
        columns = slice(index * LANES, (index + 1) * LANES)
        for start in range(0, side, half):
            rows = slice(start, start + half)
            inner = slice(half + start, 2 * half + start)

            def total(planes, pieces, own):
                value = own
                side_rows = rows
                if start == 0:
                    value = value + pieces[0][planes, index]
                if start + half == side:
                    value = value + pieces[1][planes, index]
                if index == 0:
                    value = value + pieces[2][planes, side_rows, :]
                if index == tiles - 1:
                    value = value + pieces[3][planes, side_rows, :]
                for corner, (first_row, first_col) in enumerate(((True, True), (True, False), (False, True), (False, False))):
                    if start == (0 if first_row else side - half) and index == (0 if first_col else tiles - 1):
                        value = value + pieces[4 + corner][planes]
                return value

            scale = 1.0 / (total(0, weights, weight[0, index + 1, inner, :]) + 1.0)
            for plane in range(2):
                value = total(plane, grads, grad[plane, index + 1, inner, :])
                out[plane, rows, columns] = tile_ref[plane, rows, columns] - value * scale


def to_neighbour(value, step, shape):
    rows, cols = shape
    down, across = step
    pairs = [
        (row * cols + col, (row + down) * cols + col + across)
        for row in range(rows)
        for col in range(cols)
        if 0 <= row + down < rows and 0 <= col + across < cols
    ]
    return lax.ppermute(value, ("ty", "tx"), pairs)


def edges_of_tile(value, half):
    pick = {-1: slice(0, half), 0: slice(None), 1: slice(-half, None)}
    return [value[:, pick[down], pick[across]] for down, across in AROUND]


def margins_of_grid(grid, half):
    side = grid.shape[2] - 2 * half
    rows = {-1: slice(0, half), 0: slice(half, half + side), 1: slice(half + side, None)}
    out = []
    for down, across in AROUND:
        if across == 0:
            out.append(grid[:, 1:-1, rows[down], :])
        else:
            out.append(grid[:, 0 if across < 0 else -1, rows[down], :])
    return out


def exchange(pieces, shape):
    arrived = [to_neighbour(piece, step, shape) for piece, step in zip(pieces, AROUND)]
    order = [AROUND.index((-down, -across)) for down, across in AROUND]
    return [arrived[index] for index in order]


def solution(mesh):
    shape = (mesh.shape["ty"], mesh.shape["tx"])

    def per_device(object_field, probe, intensity, positions, counts):
        side = object_field.shape[1]
        size = probe.shape[1]
        half = size // 2
        slots = intensity.shape[2]
        tiles = side // LANES
        position = positions[:, 0, 0, :]
        count = counts[0]
        left, right = half_tables(size)
        gather_left, gather_right = parity_tables(size)
        halo = exchange(edges_of_tile(object_field, half), shape)
        folded, weight = pl.pallas_call(
            early_kernel,
            out_shape=(
                jax.ShapeDtypeStruct((slots, size, size), F32),
                jax.ShapeDtypeStruct((tiles + 2, side + size, LANES), F32),
            ),
            in_specs=[SMEM, SMEM, VMEM, VMEM, VMEM, VMEM],
            out_specs=(VMEM, VMEM),
            scratch_shapes=[pltpu.VMEM((size, 3 * size), BF16)],
            compiler_params=pltpu.CompilerParams(vmem_limit_bytes=24 * 2**20),
            name="early",
        )(position, count, probe, intensity[0, 0], jnp.asarray(gather_left), jnp.asarray(gather_right))
        weight = weight[None]
        weights = exchange(margins_of_grid(weight, half), shape)
        grad, probe_sum = pl.pallas_call(
            slot_kernel,
            out_shape=(
                jax.ShapeDtypeStruct((2, tiles + 2, side + size, LANES), F32),
                jax.ShapeDtypeStruct((3, size, size), F32),
            ),
            in_specs=[SMEM, SMEM, VMEM, VMEM, VMEM, VMEM] + [ANY] * 9,
            out_specs=(VMEM, VMEM),
            scratch_shapes=[
                pltpu.VMEM((2, tiles + 2, side + size, LANES), F32),
                pltpu.VMEM((2, size, size), F32),
                pltpu.VMEM((2, 3 * size, size), BF16),
                pltpu.VMEM((2, size, 3 * size), BF16),
                pltpu.SemaphoreType.DMA((3 * tiles + 6,)),
            ],
            compiler_params=pltpu.CompilerParams(vmem_limit_bytes=48 * 2**20),
            name="slots",
        )(position, count, probe, folded, jnp.asarray(left), jnp.asarray(right), object_field, *halo)
        totals = lax.psum(probe_sum, ("ty", "tx"))
        grads = exchange(margins_of_grid(grad, half), shape)
        object_new = pl.pallas_call(
            final_kernel,
            out_shape=jax.ShapeDtypeStruct(object_field.shape, F32),
            in_specs=[VMEM] * 19,
            out_specs=VMEM,
            compiler_params=pltpu.CompilerParams(vmem_limit_bytes=48 * 2**20),
            name="final",
        )(object_field, grad, weight, *grads, *weights)
        probe_new = probe - totals[:2] / jnp.sqrt(totals[2] + 1.0)
        return (object_new, probe_new)

    in_specs = (
        P(None, "ty", "tx"),
        P(),
        P("ty", "tx", None, None, None),
        P(None, "ty", "tx", None),
        P("ty", "tx"),
    )
    out_specs = (P(None, "ty", "tx"), P())
    return jax.shard_map(per_device, mesh=mesh, in_specs=in_specs, out_specs=out_specs, check_vma=False)
```

time: 723 us -> 421 us (0.58)
  waiting for transfers between devices: 457 us -> 266 us
  matrix products: 51.4 us -> 0 us
  other arithmetic: 25.4 us -> 3.03 us
  starting transfers between devices: 123 us -> 101 us
  local copies, waits for them, and re-layouts: 37 us -> 15.8 us
  Pallas kernels: 0 us -> 15.2 us
  loops' own time: 10.2 us -> 0 us
    psum x1, waiting for transfers between devices: 400 us -> 241 us  [per_device(): totals = lax.psum(probe_sum, ('ty', 'tx'))]
    dot_general x32 -> x0, matrix products: 51.4 us -> none  [matmul(): jnp.dot(left, right, precision=lax.Precision.HIGHEST, preferred_element_t...]
    ppermute x8 -> x24, waiting for transfers between devices: 56.4 us -> 25 us  [to_neighbour(): return lax.ppermute(value, ('ty', 'tx'), pairs)]
    ppermute x8 -> x24, starting transfers between devices: 123 us -> 101 us  [to_neighbour(): return lax.ppermute(value, ('ty', 'tx'), pairs)]
    dynamic_update_slice x2 -> x0, local copies, waits for them, and re-layouts: 17.9 us -> none  [step(): lax.dynamic_update_slice(grid, old + obj_terms, (zero, row_pos, col_pos))]
    pallas_call x0 -> x3, Pallas kernels: none -> 15.2 us  [the longest x1 8.55 us: per_device(): pl.pallas_call(slot_kernel, out_shape=(jax.ShapeDtypeStruct((2, tiles + 2...]
    another operation x1 -> x0, loops' own time: 10.2 us -> none  [per_device(): grid, probe_acc = lax.fori_loop(0, live_count, step, (grid, probe_acc))]
    add x8 -> x0, other arithmetic: 9.02 us -> none  [the longest x2 3.61 us: step(): old + obj_terms]
  transfers between devices with their start and end apart: 9 -> 25, of which waited for: 6 -> 4; matrix products, arithmetic and copies ran while one was open for 2% -> 3% of each run, Pallas kernels for 0% -> 2%
where the time goes in v1:
time: 421 us; the launch traced here: 417 us
  waiting for transfers between devices  266 us (63%)
  starting transfers between devices  101 us (24%)
  local copies, waits for them, and re-layouts  15.8 us (4%)
  between operations  15.3 us (4%)
  Pallas kernels  15.2 us (4%)
    psum x1, waiting for transfers between devices, per_device(): totals = lax.psum(probe_sum, ('ty', 'tx'))  241 us
    ppermute x24, starting transfers between devices, to_neighbour(): return lax.ppermute(value, ('ty', 'tx'), pairs)  101 us
    ppermute x24, waiting for transfers between devices, to_neighbour(): return lax.ppermute(value, ('ty', 'tx'), pairs)  25 us
    pallas_call x1, Pallas kernels, per_device(): pl.pallas_call(slot_kernel, out_shape=(jax.ShapeDtypeStruct((2, tiles + 2...  8.55 us
  transfers between devices with their start and end apart: 25, of which 4 were waited for; matrix products, arithmetic and copies ran while one was open for 3% of the time, Pallas kernels for 2%

profile of v1, /device:TPU:1, one launch (start us, length us, event | category | flops | bytes accessed | tf_op | source)
XLA Modules:
  0.0 416.5 jit_solution(18184159226019394573)
XLA Ops:
  7.2 1.3 fusion.5
  8.6 6.2 %collective-permute-start.4 = (f32[2,128,128]{2,1,0:T(8,128)S(1)}, f32[2,128,128]{2,1,0:T(8,128)S(1)}, u32[]{:S(2)}, u32[]{:S(2)}) collective-permute-start(f32[2,128,128]{2,1,0:T(8,128)S(1)} %get-tuple-element.29), channel_id=1, source_target_pairs={{0,17},{1,18},{2,19},{3,20},{4,21},{5,22},{6,23},{7,24},{8,25},{9,... | collective-permute-start | bytes 393224 | tf_op jit(solution)/shard_map/ppermute | solution.py:255
  14.8 1.3 collective-permute-start.5
  16.1 1.3 fusion.7
  17.4 1.9 collective-permute-start
  19.3 2.4 collective-permute-start.1
  21.8 0.1 fusion.6
  21.8 5.1 %collective-permute-start.2 = (f32[2,512,128]{2,1,0:T(8,128)S(1)}, f32[2,512,128]{2,1,0:T(8,128)S(1)}, u32[]{:S(2)}, u32[]{:S(2)}) collective-permute-start(f32[2,512,128]{2,1,0:T(8,128)S(1)} %get-tuple-element.31), channel_id=1, source_target_pairs={{0,1},{1,2},{2,3},{3,4},{4,5},{5,6},{6,7},{7,8},{8,9},{9,10},{10,1... | collective-permute-start | bytes 1572872 | tf_op jit(solution)/shard_map/ppermute | solution.py:255
  27.6 1.0 copy-done.8
  28.6 1.4 early.1
  30.0 1.3 collective-permute-start.3
  31.3 0.9 fusion.4
  32.2 6.1 %collective-permute-start.6 = (f32[2,128,128]{2,1,0:T(8,128)S(1)}, f32[2,128,128]{2,1,0:T(8,128)S(1)}, u32[]{:S(2)}, u32[]{:S(2)}) collective-permute-start(f32[2,128,128]{2,1,0:T(8,128)S(1)} %get-tuple-element.27), channel_id=1, source_target_pairs={{16,1},{17,2},{18,3},{19,4},{20,5},{21,6},{22,7},{23,8},{24,9},{25... | collective-permute-start | bytes 393224 | tf_op jit(solution)/shard_map/ppermute | solution.py:255
  38.3 0.8 slice_bitcast_fusion.2
  39.2 1.5 collective-permute-done.6.bottom_low
  40.7 1.3 collective-permute-start.7
  42.0 0.6 slice_bitcast_fusion.8
  42.6 19.2 %collective-permute-done.7.bottom_high = f32[2,128,128]{2,1,0:T(8,128)S(1)} collective-permute-done((f32[2,128,128]{2,1,0:T(8,128)S(1)}, f32[2,128,128]{2,1,0:T(8,128)S(1)}, u32[]{:S(2)}, u32[]{:S(2)}) %collective-permute-start.7) | collective-permute-done | bytes 131104 | tf_op jit(solution)/shard_map/ppermute | solution.py:255
  61.9 2.7 collective-permute-start.20
  64.5 1.3 collective-permute-start.21
  65.8 4.3 %collective-permute-start.22 = (f32[1,128,128]{2,1,0:T(8,128)S(1)}, f32[1,128,128]{2,1,0:T(8,128)S(1)}, u32[]{:S(2)}, u32[]{:S(2)}) collective-permute-start(f32[1,128,128]{2,1,0:T(8,128)S(1)} %get-tuple-element.19), channel_id=1, source_target_pairs={{16,1},{17,2},{18,3},{19,4},{20,5},{21,6},{22,7},{23,8},{24,9},{25... | collective-permute-start | bytes 196616 | tf_op jit(solution)/shard_map/ppermute | solution.py:255
  70.1 1.3 collective-permute-start.23
  71.4 4.9 %collective-permute-start.16 = (f32[1,4,128,128]{3,2,1,0:T(8,128)}, f32[1,4,128,128]{3,2,1,0:T(8,128)S(1)}, u32[]{:S(2)}, u32[]{:S(2)}) collective-permute-start(f32[1,4,128,128]{3,2,1,0:T(8,128)} %get-tuple-element.25), channel_id=1, source_target_pairs={{0,16},{1,17},{2,18},{3,19},{4,20},{5,21},{6,22},{7,23},{8,24},{9,... | collective-permute-start | bytes 786440 | tf_op jit(solution)/shard_map/ppermute | solution.py:255
  76.4 8.6 %slots.1 = (f32[2,6,768,128]{3,2,1,0:T(8,128)}, f32[3,256,256]{2,1,0:T(8,128)}) custom-call(s32[2,8]{1,0:T(2,128)S(1)} %bitcast.38, s32[1]{0:T(128)} %bitcast.31.count, f32[2,256,256]{2,1,0:T(8,128)S(1)} %copy-done.3, f32[8,256,256]{2,1,0:T(8,128)} %copy-done.5, bf16[4,256,768]{2,1,0:T(8,128)(2,1)S(1)} %copy-done.6, ...), custom_call_target="tpu_custom_call" | custom-call | tf_op jit(solution)/shard_map/slots/pallas_call | solution.py:309
  84.9 2.2 slice_bitcast_fusion
  87.2 1.8 slice_bitcast_fusion.4
  89.0 0.6 copy-done.17
  89.7 2.0 collective-permute-start.17
  91.7 17.6 %collective-permute-start.18 = (f32[1,512,128]{2,1,0:T(8,128)}, f32[1,512,128]{2,1,0:T(8,128)S(1)}, u32[]{:S(2)}, u32[]{:S(2)}) collective-permute-start(f32[1,512,128]{2,1,0:T(8,128)} %get-tuple-element.23), channel_id=1, source_target_pairs={{0,1},{1,2},{2,3},{3,4},{4,5},{5,6},{6,7},{7,8},{8,9},{9,10},{10,1... | collective-permute-start | bytes 786440 | tf_op jit(solution)/shard_map/ppermute | solution.py:255
  109.4 1.3 collective-permute-start.19
  110.7 1.3 collective-permute-start.12
  112.0 1.3 collective-permute-start.13
  113.3 2.3 fusion.3
  115.6 0.7 copy-done.9
  116.3 11.9 %collective-permute-start.10 = (f32[2,512,128]{2,1,0:T(8,128)}, f32[2,512,128]{2,1,0:T(8,128)S(1)}, u32[]{:S(2)}, u32[]{:S(2)}) collective-permute-start(f32[2,512,128]{2,1,0:T(8,128)} %get-tuple-element.15), channel_id=1, source_target_pairs={{0,1},{1,2},{2,3},{3,4},{4,5},{5,6},{6,7},{7,8},{8,9},{9,10},{10,1... | collective-permute-start | bytes 1572872 | tf_op jit(solution)/shard_map/ppermute | solution.py:255
  128.3 0.7 copy-done.11
  129.0 1.3 collective-permute-start.11
  130.3 0.7 copy-done.13
  131.0 19.4 %collective-permute-start.8 = (f32[2,4,128,128]{3,2,1,0:T(8,128)}, f32[2,4,128,128]{3,2,1,0:T(8,128)}, u32[]{:S(2)}, u32[]{:S(2)}) collective-permute-start(f32[2,4,128,128]{3,2,1,0:T(8,128)} %get-tuple-element.17), channel_id=1, source_target_pairs={{0,16},{1,17},{2,18},{3,19},{4,20},{5,21},{6,22},{7,23},{8,24},{9,... | collective-permute-start | bytes 1572872 | tf_op jit(solution)/shard_map/ppermute | solution.py:255
  150.4 1.9 collective-permute-start.9
  152.4 0.6 copy-done.15
  153.0 1.9 collective-permute-start.14
  154.9 240.8 %all-reduce.2.cloned.1.call-done = f32[3,256,256]{2,1,0:T(8,128)} async-done(((f32[3,256,256]{2,1,0:T(8,128)}), f32[3,256,256]{2,1,0:T(8,128)}) %all-reduce.2.cloned.1.call-update) | async-done | bytes 786448 | tf_op jit(solution)/shard_map/psum | solution.py:327
  395.8 1.1 fusion.2
  396.9 1.3 collective-permute-start.15
  398.2 1.9 fusion
  400.1 4.2 %collective-permute-done.15.refs_7_ = f32[2,128,128]{2,1,0:T(8,128)S(1)} collective-permute-done((f32[2,128,128]{2,1,0:T(8,128)}, f32[2,128,128]{2,1,0:T(8,128)S(1)}, u32[]{:S(2)}, u32[]{:S(2)}) %collective-permute-start.15) | collective-permute-done | bytes 131104 | tf_op jit(solution)/shard_map/ppermute | solution.py:255
  404.4 5.3 %final.1 = f32[2,512,512]{2,1,0:T(8,128)} custom-call(f32[2,512,512]{2,1,0:T(8,128)S(1)} %copy-done.1, f32[2,6,768,128]{3,2,1,0:T(8,128)} %get-tuple-element.7.grad, f32[1,6,768,128]{3,2,1,0:T(8,128)} %bitcast.35, f32[2,4,128,128]{3,2,1,0:T(8,128)} %collective-permute-done.8.refs_0_, f32[2,4,128,128]{3,2,1,0:T(8,128)} %collective-permute-done.9.refs_1_, ...), custom_call_target="tpu_custom_call" | custom-call | tf_op jit(solution)/shard_map/final/pallas_call | solution.py:329
  (69 shorter events, 0.2 us)
Async XLA Ops:
  7.2 14.6 %copy-start = (f32[2,512,512]{2,1,0:T(8,128)S(1)}, f32[2,512,512]{2,1,0:T(8,128)}, u32[]{:S(2)}) copy-start(f32[2,512,512]{2,1,0:T(8,128)} %tile_ref.3) | copy-start | bytes 6291460
  7.2 388.6 %all-reduce.2.cloned.1.call-start = ((), (), s32[]{:S(2)}) async-start(), calls=%async_computation | async-start | bytes 1572864 | tf_op jit(solution)/shard_map/psum | solution.py:327
  8.5 19.0 %copy-start.3 = (f32[2,256,256]{2,1,0:T(8,128)S(1)}, f32[2,256,256]{2,1,0:T(8,128)}, u32[]{:S(2)}) copy-start(f32[2,256,256]{2,1,0:T(8,128)} %probe.3) | copy-start | bytes 1572868
  8.5 19.0 %copy-start.4 = (f32[1,1,8,256,256]{4,3,2,1,0:T(8,128)S(1)}, f32[1,1,8,256,256]{4,3,2,1,0:T(8,128)}, u32[]{:S(2)}) copy-start(f32[1,1,8,256,256]{4,3,2,1,0:T(8,128)} %param.11) | copy-start | bytes 6291460
  8.5 19.0 %copy-start.7 = (bf16[256,768]{1,0:T(8,128)(2,1)S(1)}, bf16[256,768]{1,0:T(8,128)(2,1)}, u32[]{:S(2)}) copy-start(bf16[256,768]{1,0:T(8,128)(2,1)} %constant.10.clone.gather_left) | copy-start | bytes 1179652
  8.5 19.0 %copy-start.25 = (s32[2,1,1,8]{3,2,1,0:T(1,128)S(1)}, s32[2,1,1,8]{3,2,1,0:T(1,128)}, u32[]{:S(2)}) copy-start(s32[2,1,1,8]{3,2,1,0:T(1,128)} %param.12) | copy-start | bytes 196
  8.6 21.4 %collective-permute-start.4 = (f32[2,128,128]{2,1,0:T(8,128)S(1)}, f32[2,128,128]{2,1,0:T(8,128)S(1)}, u32[]{:S(2)}, u32[]{:S(2)}) collective-permute-start(f32[2,128,128]{2,1,0:T(8,128)S(1)} %get-tuple-element.29), channel_id=1, source_target_pairs={{0,17},{1,18},{2,19},{3,20},{4,21},{5,22},{6,23},{7,24},{8,25},{9,... | collective-permute-start | bytes 393224 | tf_op jit(solution)/shard_map/ppermute | solution.py:255
  14.8 17.4 %collective-permute-start.5 = (f32[2,128,128]{2,1,0:T(8,128)S(1)}, f32[2,128,128]{2,1,0:T(8,128)S(1)}, u32[]{:S(2)}, u32[]{:S(2)}) collective-permute-start(f32[2,128,128]{2,1,0:T(8,128)S(1)} %get-tuple-element.28), channel_id=1, source_target_pairs={{1,16},{2,17},{3,18},{4,19},{5,20},{6,21},{7,22},{8,23},{9,24},{10... | collective-permute-start | bytes 393224 | tf_op jit(solution)/shard_map/ppermute | solution.py:255
  17.4 47.2 %collective-permute-start = (f32[2,128,512]{2,1,0:T(8,128)S(1)}, f32[2,128,512]{2,1,0:T(8,128)S(1)}, u32[]{:S(2)}, u32[]{:S(2)}) collective-permute-start(f32[2,128,512]{2,1,0:T(8,128)S(1)} %get-tuple-element.33), channel_id=1, source_target_pairs={{0,16},{1,17},{2,18},{3,19},{4,20},{5,21},{6,22},{7,23},{8,24},{9,... | collective-permute-start | bytes 1572872 | tf_op jit(solution)/shard_map/ppermute | solution.py:255
  19.3 46.5 %collective-permute-start.1 = (f32[2,128,512]{2,1,0:T(8,128)S(1)}, f32[2,128,512]{2,1,0:T(8,128)S(1)}, u32[]{:S(2)}, u32[]{:S(2)}) collective-permute-start(f32[2,128,512]{2,1,0:T(8,128)S(1)} %get-tuple-element.32), channel_id=1, source_target_pairs={{16,0},{17,1},{18,2},{19,3},{20,4},{21,5},{22,6},{23,7},{24,8},{25... | collective-permute-start | bytes 1572872 | tf_op jit(solution)/shard_map/ppermute | solution.py:255
  21.8 48.3 %collective-permute-start.2 = (f32[2,512,128]{2,1,0:T(8,128)S(1)}, f32[2,512,128]{2,1,0:T(8,128)S(1)}, u32[]{:S(2)}, u32[]{:S(2)}) collective-permute-start(f32[2,512,128]{2,1,0:T(8,128)S(1)} %get-tuple-element.31), channel_id=1, source_target_pairs={{0,1},{1,2},{2,3},{3,4},{4,5},{5,6},{6,7},{7,8},{8,9},{9,10},{10,1... | collective-permute-start | bytes 1572872 | tf_op jit(solution)/shard_map/ppermute | solution.py:255
  27.6 1.0 copy-start.8
  28.6 47.8 %copy-start.6 = (bf16[4,256,768]{2,1,0:T(8,128)(2,1)S(1)}, bf16[4,256,768]{2,1,0:T(8,128)(2,1)}, u32[]{:S(2)}) copy-start(bf16[4,256,768]{2,1,0:T(8,128)(2,1)} %constant.12.clone.left) | copy-start | bytes 4718596
  30.0 12.0 %copy-start.2 = (f32[6,768,128]{2,1,0:T(8,128)}, f32[6,768,128]{2,1,0:T(8,128)S(1)}, u32[]{:S(2)}) copy-start(f32[6,768,128]{2,1,0:T(8,128)S(1)} %get-tuple-element.8) | copy-start | bytes 7077892
  30.0 12.6 %copy-start.5 = (f32[8,256,256]{2,1,0:T(8,128)}, f32[8,256,256]{2,1,0:T(8,128)S(1)}, u32[]{:S(2)}) copy-start(f32[8,256,256]{2,1,0:T(8,128)S(1)} %get-tuple-element.6.folded) | copy-start | bytes 6291460
  30.0 41.4 %collective-permute-start.3 = (f32[2,512,128]{2,1,0:T(8,128)S(1)}, f32[2,512,128]{2,1,0:T(8,128)S(1)}, u32[]{:S(2)}, u32[]{:S(2)}) collective-permute-start(f32[2,512,128]{2,1,0:T(8,128)S(1)} %get-tuple-element.30), channel_id=1, source_target_pairs={{1,0},{2,1},{3,2},{4,3},{5,4},{6,5},{7,6},{8,7},{9,8},{10,9},{11,1... | collective-permute-start | bytes 1572872 | tf_op jit(solution)/shard_map/ppermute | solution.py:255
  32.2 8.4 %collective-permute-start.6 = (f32[2,128,128]{2,1,0:T(8,128)S(1)}, f32[2,128,128]{2,1,0:T(8,128)S(1)}, u32[]{:S(2)}, u32[]{:S(2)}) collective-permute-start(f32[2,128,128]{2,1,0:T(8,128)S(1)} %get-tuple-element.27), channel_id=1, source_target_pairs={{16,1},{17,2},{18,3},{19,4},{20,5},{21,6},{22,7},{23,8},{24,9},{25... | collective-permute-start | bytes 393224 | tf_op jit(solution)/shard_map/ppermute | solution.py:255
  40.7 21.2 %collective-permute-start.7 = (f32[2,128,128]{2,1,0:T(8,128)S(1)}, f32[2,128,128]{2,1,0:T(8,128)S(1)}, u32[]{:S(2)}, u32[]{:S(2)}) collective-permute-start(f32[2,128,128]{2,1,0:T(8,128)S(1)} %get-tuple-element.26), channel_id=1, source_target_pairs={{17,0},{18,1},{19,2},{20,3},{21,4},{22,5},{23,6},{24,7},{25,8},{26... | collective-permute-start | bytes 393224 | tf_op jit(solution)/shard_map/ppermute | solution.py:255
  61.9 27.2 %collective-permute-start.20 = (f32[1,128,128]{2,1,0:T(8,128)S(1)}, f32[1,128,128]{2,1,0:T(8,128)S(1)}, u32[]{:S(2)}, u32[]{:S(2)}) collective-permute-start(f32[1,128,128]{2,1,0:T(8,128)S(1)} %get-tuple-element.21), channel_id=1, source_target_pairs={{0,17},{1,18},{2,19},{3,20},{4,21},{5,22},{6,23},{7,24},{8,25},{9,... | collective-permute-start | bytes 196616 | tf_op jit(solution)/shard_map/ppermute | solution.py:255
  64.5 27.2 %collective-permute-start.21 = (f32[1,128,128]{2,1,0:T(8,128)}, f32[1,128,128]{2,1,0:T(8,128)S(1)}, u32[]{:S(2)}, u32[]{:S(2)}) collective-permute-start(f32[1,128,128]{2,1,0:T(8,128)} %get-tuple-element.20), channel_id=1, source_target_pairs={{1,16},{2,17},{3,18},{4,19},{5,20},{6,21},{7,22},{8,23},{9,24},{10... | collective-permute-start | bytes 196616 | tf_op jit(solution)/shard_map/ppermute | solution.py:255
  65.8 43.5 %collective-permute-start.22 = (f32[1,128,128]{2,1,0:T(8,128)S(1)}, f32[1,128,128]{2,1,0:T(8,128)S(1)}, u32[]{:S(2)}, u32[]{:S(2)}) collective-permute-start(f32[1,128,128]{2,1,0:T(8,128)S(1)} %get-tuple-element.19), channel_id=1, source_target_pairs={{16,1},{17,2},{18,3},{19,4},{20,5},{21,6},{22,7},{23,8},{24,9},{25... | collective-permute-start | bytes 196616 | tf_op jit(solution)/shard_map/ppermute | solution.py:255
  70.1 40.6 %collective-permute-start.23 = (f32[1,128,128]{2,1,0:T(8,128)S(1)}, f32[1,128,128]{2,1,0:T(8,128)S(1)}, u32[]{:S(2)}, u32[]{:S(2)}) collective-permute-start(f32[1,128,128]{2,1,0:T(8,128)S(1)} %get-tuple-element.18), channel_id=1, source_target_pairs={{17,0},{18,1},{19,2},{20,3},{21,4},{22,5},{23,6},{24,7},{25,8},{26... | collective-permute-start | bytes 196616 | tf_op jit(solution)/shard_map/ppermute | solution.py:255
  71.4 40.6 %collective-permute-start.16 = (f32[1,4,128,128]{3,2,1,0:T(8,128)}, f32[1,4,128,128]{3,2,1,0:T(8,128)S(1)}, u32[]{:S(2)}, u32[]{:S(2)}) collective-permute-start(f32[1,4,128,128]{3,2,1,0:T(8,128)} %get-tuple-element.25), channel_id=1, source_target_pairs={{0,16},{1,17},{2,18},{3,19},{4,20},{5,21},{6,22},{7,23},{8,24},{9,... | collective-permute-start | bytes 786440 | tf_op jit(solution)/shard_map/ppermute | solution.py:255
  89.0 315.3 %copy-start.1 = (f32[2,512,512]{2,1,0:T(8,128)S(1)}, f32[2,512,512]{2,1,0:T(8,128)}, u32[]{:S(2)}) copy-start(f32[2,512,512]{2,1,0:T(8,128)} %tile_ref.3) | copy-start | bytes 6291460
  89.7 26.0 %collective-permute-start.17 = (f32[1,4,128,128]{3,2,1,0:T(8,128)}, f32[1,4,128,128]{3,2,1,0:T(8,128)S(1)}, u32[]{:S(2)}, u32[]{:S(2)}) collective-permute-start(f32[1,4,128,128]{3,2,1,0:T(8,128)} %get-tuple-element.24), channel_id=1, source_target_pairs={{16,0},{17,1},{18,2},{19,3},{20,4},{21,5},{22,6},{23,7},{24,8},{25... | collective-permute-start | bytes 786440 | tf_op jit(solution)/shard_map/ppermute | solution.py:255
  91.7 23.9 %copy-start.19 = (f32[1,128,128]{2,1,0:T(8,128)}, f32[1,128,128]{2,1,0:T(8,128)S(1)}, u32[]{:S(2)}) copy-start(f32[1,128,128]{2,1,0:T(8,128)S(1)} %collective-permute-done.21.refs_13_) | copy-start | bytes 196612
  91.7 36.6 %collective-permute-start.18 = (f32[1,512,128]{2,1,0:T(8,128)}, f32[1,512,128]{2,1,0:T(8,128)S(1)}, u32[]{:S(2)}, u32[]{:S(2)}) collective-permute-start(f32[1,512,128]{2,1,0:T(8,128)} %get-tuple-element.23), channel_id=1, source_target_pairs={{0,1},{1,2},{2,3},{3,4},{4,5},{5,6},{6,7},{7,8},{8,9},{9,10},{10,1... | collective-permute-start | bytes 786440 | tf_op jit(solution)/shard_map/ppermute | solution.py:255
  109.4 6.2 %copy-start.21 = (f32[1,128,128]{2,1,0:T(8,128)}, f32[1,128,128]{2,1,0:T(8,128)S(1)}, u32[]{:S(2)}) copy-start(f32[1,128,128]{2,1,0:T(8,128)S(1)} %collective-permute-done.22.refs_14_) | copy-start | bytes 196612
  109.4 20.9 %collective-permute-start.19 = (f32[1,512,128]{2,1,0:T(8,128)}, f32[1,512,128]{2,1,0:T(8,128)S(1)}, u32[]{:S(2)}, u32[]{:S(2)}) collective-permute-start(f32[1,512,128]{2,1,0:T(8,128)} %get-tuple-element.22), channel_id=1, source_target_pairs={{1,0},{2,1},{3,2},{4,3},{5,4},{6,5},{7,6},{8,7},{9,8},{10,9},{11,1... | collective-permute-start | bytes 786440 | tf_op jit(solution)/shard_map/ppermute | solution.py:255
  110.7 4.9 %copy-start.23 = (f32[1,128,128]{2,1,0:T(8,128)}, f32[1,128,128]{2,1,0:T(8,128)S(1)}, u32[]{:S(2)}) copy-start(f32[1,128,128]{2,1,0:T(8,128)S(1)} %collective-permute-done.23.refs_15_) | copy-start | bytes 196612
  110.7 39.7 %collective-permute-start.12 = (f32[2,128,128]{2,1,0:T(8,128)S(1)}, f32[2,128,128]{2,1,0:T(8,128)S(1)}, u32[]{:S(2)}, u32[]{:S(2)}) collective-permute-start(f32[2,128,128]{2,1,0:T(8,128)S(1)} %get-tuple-element.13), channel_id=1, source_target_pairs={{0,17},{1,18},{2,19},{3,20},{4,21},{5,22},{6,23},{7,24},{8,25},{9,... | collective-permute-start | bytes 393224 | tf_op jit(solution)/shard_map/ppermute | solution.py:255
  112.0 40.3 %collective-permute-start.13 = (f32[2,128,128]{2,1,0:T(8,128)S(1)}, f32[2,128,128]{2,1,0:T(8,128)S(1)}, u32[]{:S(2)}, u32[]{:S(2)}) collective-permute-start(f32[2,128,128]{2,1,0:T(8,128)S(1)} %get-tuple-element.12), channel_id=1, source_target_pairs={{1,16},{2,17},{3,18},{4,19},{5,20},{6,21},{7,22},{8,23},{9,24},{10... | collective-permute-start | bytes 393224 | tf_op jit(solution)/shard_map/ppermute | solution.py:255
  115.6 0.7 copy-start.9
  116.3 288.0 %collective-permute-start.10 = (f32[2,512,128]{2,1,0:T(8,128)}, f32[2,512,128]{2,1,0:T(8,128)S(1)}, u32[]{:S(2)}, u32[]{:S(2)}) collective-permute-start(f32[2,512,128]{2,1,0:T(8,128)} %get-tuple-element.15), channel_id=1, source_target_pairs={{0,1},{1,2},{2,3},{3,4},{4,5},{5,6},{6,7},{7,8},{8,9},{9,10},{10,1... | collective-permute-start | bytes 1572872 | tf_op jit(solution)/shard_map/ppermute | solution.py:255
  128.3 0.7 copy-start.11
  129.0 275.3 %collective-permute-start.11 = (f32[2,512,128]{2,1,0:T(8,128)}, f32[2,512,128]{2,1,0:T(8,128)}, u32[]{:S(2)}, u32[]{:S(2)}) collective-permute-start(f32[2,512,128]{2,1,0:T(8,128)} %get-tuple-element.14), channel_id=1, source_target_pairs={{1,0},{2,1},{3,2},{4,3},{5,4},{6,5},{7,6},{8,7},{9,8},{10,9},{11,1... | collective-permute-start | bytes 1572872 | tf_op jit(solution)/shard_map/ppermute | solution.py:255
  131.0 273.3 %collective-permute-start.8 = (f32[2,4,128,128]{3,2,1,0:T(8,128)}, f32[2,4,128,128]{3,2,1,0:T(8,128)}, u32[]{:S(2)}, u32[]{:S(2)}) collective-permute-start(f32[2,4,128,128]{3,2,1,0:T(8,128)} %get-tuple-element.17), channel_id=1, source_target_pairs={{0,16},{1,17},{2,18},{3,19},{4,20},{5,21},{6,22},{7,23},{8,24},{9,... | collective-permute-start | bytes 1572872 | tf_op jit(solution)/shard_map/ppermute | solution.py:255
  150.4 253.9 %collective-permute-start.9 = (f32[2,4,128,128]{3,2,1,0:T(8,128)}, f32[2,4,128,128]{3,2,1,0:T(8,128)}, u32[]{:S(2)}, u32[]{:S(2)}) collective-permute-start(f32[2,4,128,128]{3,2,1,0:T(8,128)} %get-tuple-element.16), channel_id=1, source_target_pairs={{16,0},{17,1},{18,2},{19,3},{20,4},{21,5},{22,6},{23,7},{24,8},{25... | collective-permute-start | bytes 1572872 | tf_op jit(solution)/shard_map/ppermute | solution.py:255
  153.0 243.9 %collective-permute-start.14 = (f32[2,128,128]{2,1,0:T(8,128)}, f32[2,128,128]{2,1,0:T(8,128)}, u32[]{:S(2)}, u32[]{:S(2)}) collective-permute-start(f32[2,128,128]{2,1,0:T(8,128)} %get-tuple-element.11), channel_id=1, source_target_pairs={{16,1},{17,2},{18,3},{19,4},{20,5},{21,6},{22,7},{23,8},{24,9},{25... | collective-permute-start | bytes 393224 | tf_op jit(solution)/shard_map/ppermute | solution.py:255
  395.7 8.6 %copy-start.10 = (f32[1,4,128,128]{3,2,1,0:T(8,128)S(1)}, f32[1,4,128,128]{3,2,1,0:T(8,128)}, u32[]{:S(2)}) copy-start(f32[1,4,128,128]{3,2,1,0:T(8,128)} %copy-done.9) | copy-start | bytes 786436
  395.7 8.6 %copy-start.12 = (f32[1,512,128]{2,1,0:T(8,128)S(1)}, f32[1,512,128]{2,1,0:T(8,128)}, u32[]{:S(2)}) copy-start(f32[1,512,128]{2,1,0:T(8,128)} %copy-done.11) | copy-start | bytes 786436
  395.7 8.6 %copy-start.14 = (f32[1,512,128]{2,1,0:T(8,128)S(1)}, f32[1,512,128]{2,1,0:T(8,128)}, u32[]{:S(2)}) copy-start(f32[1,512,128]{2,1,0:T(8,128)} %copy-done.13) | copy-start | bytes 786436
  395.8 8.6 %copy-start.16 = (f32[2,128,128]{2,1,0:T(8,128)S(1)}, f32[2,128,128]{2,1,0:T(8,128)}, u32[]{:S(2)}) copy-start(f32[2,128,128]{2,1,0:T(8,128)} %copy-done.15) | copy-start | bytes 393220
  395.8 8.6 %copy-start.18 = (f32[1,128,128]{2,1,0:T(8,128)S(1)}, f32[1,128,128]{2,1,0:T(8,128)}, u32[]{:S(2)}) copy-start(f32[1,128,128]{2,1,0:T(8,128)} %copy-done.17) | copy-start | bytes 196612
  395.8 8.6 %copy-start.20 = (f32[1,128,128]{2,1,0:T(8,128)S(1)}, f32[1,128,128]{2,1,0:T(8,128)}, u32[]{:S(2)}) copy-start(f32[1,128,128]{2,1,0:T(8,128)} %copy-done.19) | copy-start | bytes 196612
  395.8 8.6 %copy-start.22 = (f32[1,128,128]{2,1,0:T(8,128)S(1)}, f32[1,128,128]{2,1,0:T(8,128)}, u32[]{:S(2)}) copy-start(f32[1,128,128]{2,1,0:T(8,128)} %copy-done.21) | copy-start | bytes 196612
  395.8 8.6 %copy-start.24 = (f32[1,128,128]{2,1,0:T(8,128)S(1)}, f32[1,128,128]{2,1,0:T(8,128)}, u32[]{:S(2)}) copy-start(f32[1,128,128]{2,1,0:T(8,128)} %copy-done.23) | copy-start | bytes 196612
  396.9 7.4 %collective-permute-start.15 = (f32[2,128,128]{2,1,0:T(8,128)}, f32[2,128,128]{2,1,0:T(8,128)S(1)}, u32[]{:S(2)}, u32[]{:S(2)}) collective-permute-start(f32[2,128,128]{2,1,0:T(8,128)} %get-tuple-element.10), channel_id=1, source_target_pairs={{17,0},{18,1},{19,2},{20,3},{21,4},{22,5},{23,6},{24,7},{25,8},{26... | collective-permute-start | bytes 393224 | tf_op jit(solution)/shard_map/ppermute | solution.py:255
  (3 other events, 2.0 us)
Sparse Core Ops, SparseCore 0:
  87.3 308.3 all-reduce.1

commit v2 on v1

v2 whole, which is shorter than its diff:
```python
import numpy as np
import ml_dtypes
import jax
import jax.numpy as jnp
from jax import lax
from jax.experimental import pallas as pl
from jax.experimental.pallas import tpu as pltpu
from jax.sharding import PartitionSpec as P

BF16 = jnp.bfloat16
F32 = jnp.float32
LANES = 128
VMEM = pl.BlockSpec(memory_space=pltpu.VMEM)
SMEM = pl.BlockSpec(memory_space=pltpu.SMEM)
ANY = pl.BlockSpec(memory_space=pl.ANY)
def split_host(table):
    high = table.astype(ml_dtypes.bfloat16)
    low = (table - high.astype(np.float64)).astype(ml_dtypes.bfloat16)
    return high, low


def half_tables(size):
    half = size // 2
    left, right = [], []
    for parity in range(2):
        product = (2 * np.arange(half)[:, None] + parity) * np.arange(half)[None, :] % size
        angle = 2.0 * np.pi * product / size
        cos, sin = np.cos(angle) / np.sqrt(size), np.sin(angle) / np.sqrt(size)
        base = np.block([[cos, sin], [-sin, cos]])
        for table in (base, base.T):
            high, low = split_host(table)
            left.append(np.concatenate([high, high, low], axis=1))
            right.append(np.concatenate([high, high, low], axis=0))
    return np.stack(left), np.stack(right)


def parity_tables(size):
    order = np.concatenate([np.arange(0, size, 2), np.arange(1, size, 2)])
    gather = np.eye(size)[order].astype(ml_dtypes.bfloat16)
    return np.concatenate([gather] * 3, axis=1), np.concatenate([gather.T] * 3, axis=0)


def matmul(left, right):
    return jnp.dot(left, right, preferred_element_type=F32)


def split(value):
    high = value.astype(BF16)
    return high, (value - high.astype(F32)).astype(BF16)


def put_rows(ref, start, columns, value):
    rows = value.shape[0]
    high, low = split(value)
    third = ref.shape[0] // 3
    ref[start : start + rows, columns] = high
    ref[third + start : third + start + rows, columns] = low
    ref[2 * third + start : 2 * third + start + rows, columns] = high


def put_columns(ref, rows, start, value):
    width = value.shape[1]
    high, low = split(value)
    third = ref.shape[1] // 3
    ref[rows, start : start + width] = high
    ref[rows, third + start : third + start + width] = low
    ref[rows, 2 * third + start : 2 * third + start + width] = high


def place(row, col, last):
    tile = jnp.minimum(lax.shift_right_logical(col, 7), last)
    return row, tile, col - tile * LANES


def add_window(accumulate, row, tile, offset, first, second):
    rows = first.shape[0]
    turn = jnp.bitwise_and(offset, LANES - 1)
    kept = lax.broadcasted_iota(jnp.int32, first.shape, 1) >= offset
    first = pltpu.roll(first, turn, 1)
    second = pltpu.roll(second, turn, 1)
    where = pl.ds(row, rows)
    accumulate[tile, where, :] += jnp.where(kept, first, 0.0)
    accumulate[tile + 1, where, :] += jnp.where(kept, second, first)
    accumulate[tile + 2, where, :] += jnp.where(kept, 0.0, second)


def fold_kernel(count, measured, gather_left, gather_right, folded, parts):
    size = measured.shape[1]

    def three(value):
        high = value.astype(BF16)
        rest = value - high.astype(F32)
        middle = rest.astype(BF16)
        return high, middle, (rest - middle.astype(F32)).astype(BF16)

    def step(slot, carry):
        for index, part in enumerate(three(measured[slot])):
            parts[:, index * size : (index + 1) * size] = part
        value = matmul(parts[...], gather_right[...])
        folded[slot] = matmul(gather_left[...], jnp.concatenate(three(value), axis=0))
        return carry

    lax.fori_loop(0, count[0], step, 0)


def ends_kernel(tile_ref, low, high, notes, top, bottom):
    half = LANES
    side = tile_ref.shape[1]
    tiles = side // LANES
    for out, start in ((top, 0), (bottom, side - half)):
        rows = slice(start, start + half)
        for index in range(tiles):
            out[:, 1 + index, :half, :] = tile_ref[:, rows, index * LANES : (index + 1) * LANES]
        for index, strip in ((0, low), (1 + tiles, high)):
            out[:, index, :half, :] = strip[:, rows, :]
            out[:, index, half:, :] = strip[:, side:, :]
        out[:, 1, half:, :] = notes[...]
        out[:, 2 : 1 + tiles, half:, :] = jnp.zeros((2, tiles - 1, 8, LANES), F32)


def slot_kernel(
    position, count, probe, folded, left, right, tile_ref, low, high, top, bottom,
    margin_top, margin_bottom, side_low, side_high, middle, sums, canvas, grad, probe_sum, patch, rhs, lhs,
):
    size = probe.shape[1]
    half = size // 2
    side = tile_ref.shape[1]
    tiles = side // LANES
    inner = slice(half, half + side)
    for index in range(tiles):
        canvas[:, 1 + index, inner, :] = tile_ref[:, :, index * LANES : (index + 1) * LANES]
    canvas[:, 0, inner, :] = low[:, :side, :]
    canvas[:, 1 + tiles, inner, :] = high[:, :side, :]
    canvas[:, :, :half, :] = top[:, :, :half, :]
    canvas[:, :, half + side :, :] = bottom[:, :, :half, :]
    grad[...] = jnp.zeros_like(grad)
    probe_sum[...] = jnp.zeros_like(probe_sum)
    near, far = slice(0, half), slice(half, size)

    def step(slot, carry):
        row, tile, offset = place(position[0, slot] + half, position[1, slot] + half, tiles - 1)
        turn = jnp.bitwise_and(LANES - offset, LANES - 1)
        kept = lax.broadcasted_iota(jnp.int32, (size, LANES), 1) < LANES - offset
        for plane in range(2):
            raw = [pltpu.roll(canvas[plane, tile + index, pl.ds(row, size), :], turn, 1) for index in range(3)]
            patch[plane, 0] = jnp.where(kept, raw[0], raw[1])
            patch[plane, 1] = jnp.where(kept, raw[1], raw[2])
        for index, columns in enumerate((near, far)):
            probe_re, probe_im = probe[0, :, columns], probe[1, :, columns]
            patch_re, patch_im = patch[0, index], patch[1, index]
            exit_re = probe_re * patch_re - probe_im * patch_im
            exit_im = probe_re * patch_im + probe_im * patch_re
            probe_sum[2, index] += patch_re * patch_re + patch_im * patch_im
            put_rows(rhs.at[0], 0, columns, exit_re[:half] + exit_re[half:])
            put_rows(rhs.at[0], half, columns, exit_im[:half] + exit_im[half:])
            put_rows(rhs.at[1], 0, columns, exit_re[:half] - exit_re[half:])
            put_rows(rhs.at[1], half, columns, exit_im[:half] - exit_im[half:])
        for parity_ in range(2):
            value = matmul(left[2 * parity_], rhs[parity_])
            rows = slice(parity_ * half, (parity_ + 1) * half)
            put_columns(lhs.at[0], rows, 0, value[:half, near] + value[:half, far])
            put_columns(lhs.at[0], rows, half, value[half:, near] + value[half:, far])
            put_columns(lhs.at[1], rows, 0, value[:half, near] - value[:half, far])
            put_columns(lhs.at[1], rows, half, value[half:, near] - value[half:, far])
        everything = slice(0, size)
        back = []
        for parity_ in range(2):
            value = matmul(lhs[parity_], right[2 * parity_ + 1])
            wave_re, wave_im = value[:, near], value[:, far]
            columns = slice(parity_ * half, (parity_ + 1) * half)
            excess = wave_re * wave_re + wave_im * wave_im - folded[slot, :, columns]
            put_columns(lhs.at[parity_], everything, 0, excess * wave_re)
            put_columns(lhs.at[parity_], everything, half, excess * wave_im)
            back.append(matmul(lhs[parity_], right[2 * parity_]))
        for parity_ in range(2):
            rows = slice(parity_ * half, (parity_ + 1) * half)
            put_rows(rhs.at[parity_], 0, near, back[0][rows, near] + back[1][rows, near])
            put_rows(rhs.at[parity_], half, near, back[0][rows, far] + back[1][rows, far])
            put_rows(rhs.at[parity_], 0, far, back[0][rows, near] - back[1][rows, near])
            put_rows(rhs.at[parity_], half, far, back[0][rows, far] - back[1][rows, far])
        even = matmul(left[1], rhs[0])
        odd = matmul(left[3], rhs[1])
        pieces = []
        for index, columns in enumerate((near, far)):
            chi_re, chi_im = (
                jnp.concatenate([even[rows, columns] + odd[rows, columns], even[rows, columns] - odd[rows, columns]], axis=0)
                for rows in (near, far)
            )
            probe_re, probe_im = probe[0, :, columns], probe[1, :, columns]
            patch_re, patch_im = patch[0, index], patch[1, index]
            probe_sum[0, index] += patch_re * chi_re + patch_im * chi_im
            probe_sum[1, index] += patch_re * chi_im - patch_im * chi_re
            pieces.append((probe_re * chi_re + probe_im * chi_im, probe_re * chi_im - probe_im * chi_re))
        for plane in range(2):
            add_window(grad.at[plane], row, tile, offset, pieces[0][plane], pieces[1][plane])
        return carry

    lax.fori_loop(0, count[0], step, 0)
    margin_top[...] = grad[:, :, :half, :]
    margin_bottom[...] = grad[:, :, half + side :, :]
    side_low[...] = grad[:, 0, inner, :]
    side_high[...] = grad[:, 1 + tiles, inner, :]
    middle[...] = grad[:, 1 : 1 + tiles, inner, :]
    for plane in range(3):
        for index in range(2):
            sums[:, 2 * plane + index] = probe_sum[plane, index].reshape(size // 8, 8, LANES)


def sides_kernel(first, last, above_first, above_last, below_first, below_last, low, high):
    half = LANES
    side = first.shape[1]
    for out, own, above, below in ((low, first, above_first, below_first), (high, last, above_last, below_last)):
        out[...] = own[...]
        out[:, :half, :] += above[:, 0]
        out[:, side - half :, :] += below[:, 0]


def weight_kernel(probe, notes, low, high, top, bottom, scale, power, weight, numbers, sems):
    half = LANES
    side = scale.shape[1]
    tiles = side // LANES
    sources = (
        top.at[0, 0, half:, :], top.at[0, 1, half:, :], top.at[0, 1 + tiles, half:, :],
        low.at[0, side:, :], notes.at[0], high.at[0, side:, :],
        bottom.at[0, 0, half:, :], bottom.at[0, 1, half:, :], bottom.at[0, 1 + tiles, half:, :],
    )
    copies = [pltpu.make_async_copy(source, numbers.at[index], sems.at[index]) for index, source in enumerate(sources)]
    for copy in copies:
        copy.start()
    weight[...] = jnp.zeros_like(weight)
    for index in range(2):
        columns = slice(index * LANES, (index + 1) * LANES)
        power[index] = probe[0, :, columns] * probe[0, :, columns] + probe[1, :, columns] * probe[1, :, columns]
    for copy in copies:
        copy.wait()
    for index in range(9):
        down, across = index // 3 - 1, index % 3 - 1

        def step(slot, carry):
            row = numbers[index, 0, slot].astype(jnp.int32) + (2 * half + down * side)
            col = numbers[index, 1, slot].astype(jnp.int32) + (2 * half + across * side)
            reach = side + 2 * half

            @pl.when((row > 0) & (row < reach) & (col > 0) & (col < reach))
            def add():
                at, tile, offset = place(row, col, tiles + 1)
                add_window(weight, at, tile, offset, power[0], power[1])

            return carry

        lax.fori_loop(0, numbers[index, 2, 0].astype(jnp.int32), step, 0)
    for index in range(tiles):
        scale[index] = 1.0 / (weight[2 + index, 2 * half : 2 * half + side, :] + 1.0)


def final_kernel(tile_ref, middle, above, below, low, high, scale, out):
    half = LANES
    side = tile_ref.shape[1]
    index = pl.program_id(0)
    is_first = (index == 0).astype(F32)
    is_last = (index == pl.num_programs(0) - 1).astype(F32)
    for plane in range(2):
        for start in range(0, side, half):
            rows = slice(start, start + half)
            value = middle[plane, 0, rows, :]
            if start == 0:
                value = value + above[plane, 0]
            if start + half == side:
                value = value + below[plane, 0]
            value = value + low[plane, rows, :] * is_first + high[plane, rows, :] * is_last
            out[plane, rows, :] = tile_ref[plane, rows, :] - value * scale[0, rows, :]


def plane_kernel(parts, out):
    out[...] = jnp.broadcast_to(jnp.sum(parts[...], axis=0)[None], out.shape)


def probe_kernel(index, parts, probe, out):
    total = jnp.sum(parts[...], axis=0)
    rows = pl.ds(pl.multiple_of(index[0] * 8, 8), 8)
    for tile in range(2):
        root = jnp.sqrt(total[4 + tile] + 1.0)
        for plane in range(2):
            new = probe[plane, rows, tile * LANES : (tile + 1) * LANES] - total[2 * plane + tile] / root
            out[:, 2 * plane + tile] = jnp.broadcast_to(new[None], (out.shape[0], 8, LANES))


def join_kernel(pieces, out):
    for plane in range(2):
        for tile in range(2):
            value = pieces[:, 2 * plane + tile]
            out[plane, :, tile * LANES : (tile + 1) * LANES] = value.reshape(out.shape[1], LANES)


def both_ways(low, high, axis):
    count = lax.axis_size(axis)
    up = [(index, index + 1) for index in range(count - 1)]
    down = [(index + 1, index) for index in range(count - 1)]
    return lax.ppermute(high, axis, up), lax.ppermute(low, axis, down)


def block(shape, *where):
    return pl.BlockSpec(shape, lambda *_: where)


def params(mib):
    return pltpu.CompilerParams(vmem_limit_bytes=mib * 2**20)


def solution(mesh):
    rows, cols = mesh.shape["ty"], mesh.shape["tx"]
    near_y, near_z = 8, 4
    planes = [
        [(8 * high + row) * cols + near_z * x + low for row in range(near_y) for x in range(cols // near_z)]
        for high in range(rows // near_y)
        for low in range(near_z)
    ]
    lines = [list(line) for line in zip(*planes)]

    def trade(pieces, groups):
        return lax.all_to_all(pieces, ("ty", "tx"), 0, 0, axis_index_groups=groups, tiled=True)

    def per_device(object_field, probe, intensity, positions, counts):
        side = object_field.shape[1]
        size = probe.shape[1]
        half = size // 2
        slots = intensity.shape[2]
        tiles = side // LANES
        position = positions[:, 0, 0, :]
        count = counts[0]
        row, col = lax.axis_index("ty"), lax.axis_index("tx")
        piece = jnp.bitwise_and(row, near_y - 1) * (cols // near_z) + lax.shift_right_logical(col, 2)
        piece = piece.reshape(1).astype(jnp.int32)
        left, right = (jnp.asarray(table) for table in half_tables(size))
        gather_left, gather_right = (jnp.asarray(table) for table in parity_tables(size))

        notes = jnp.zeros((8, LANES), F32).at[:2, :slots].set(position.astype(F32))
        notes = notes.at[2, 0].set(counts[0, 0].astype(F32))
        notes = jnp.stack([notes, jnp.zeros_like(notes)])
        low, high = both_ways(
            jnp.concatenate([object_field[:, :, :half], notes], axis=1),
            jnp.concatenate([object_field[:, :, side - half :], notes], axis=1),
            "tx",
        )
        folded = pl.pallas_call(
            fold_kernel,
            out_shape=jax.ShapeDtypeStruct((slots, size, size), F32),
            in_specs=[SMEM, VMEM, VMEM, VMEM],
            out_specs=VMEM,
            scratch_shapes=[pltpu.VMEM((size, 3 * size), BF16)],
            compiler_params=params(16),
            name="fold",
        )(count, intensity[0, 0], gather_left, gather_right)
        end = jax.ShapeDtypeStruct((2, tiles + 2, half + 8, LANES), F32)
        first_rows, last_rows = pl.pallas_call(
            ends_kernel,
            out_shape=(end, end),
            in_specs=[VMEM] * 4,
            out_specs=(VMEM, VMEM),
            compiler_params=params(16),
            name="ends",
        )(object_field, low, high, notes)
        top, bottom = both_ways(first_rows, last_rows, "ty")

        margin = jax.ShapeDtypeStruct((2, tiles + 2, half, LANES), F32)
        strip = jax.ShapeDtypeStruct((2, side, LANES), F32)
        members = len(planes[0])
        margin_top, margin_bottom, side_low, side_high, middle, sums = pl.pallas_call(
            slot_kernel,
            out_shape=(
                margin, margin, strip, strip,
                jax.ShapeDtypeStruct((2, tiles, side, LANES), F32),
                jax.ShapeDtypeStruct((members, 6, 8, LANES), F32),
            ),
            in_specs=[SMEM] * 2 + [VMEM] * 9,
            out_specs=(VMEM,) * 6,
            scratch_shapes=[
                pltpu.VMEM((2, tiles + 2, side + size, LANES), F32),
                pltpu.VMEM((2, tiles + 2, side + size, LANES), F32),
                pltpu.VMEM((3, 2, size, LANES), F32),
                pltpu.VMEM((2, 2, size, LANES), F32),
                pltpu.VMEM((2, 3 * size, size), BF16),
                pltpu.VMEM((2, size, 3 * size), BF16),
            ],
            compiler_params=params(48),
            name="slots",
        )(position, count, probe, folded, left, right, object_field, low, high, top, bottom)

        above, below = both_ways(margin_top, margin_bottom, "ty")
        parts = trade(sums, planes)
        tall = (2, 1, side, LANES)
        flat = (2, 1, half, LANES)
        whole = block((2, side, LANES), 0, 0, 0)
        margin_low, margin_high = pl.pallas_call(
            sides_kernel,
            out_shape=(strip, strip),
            grid=(1,),
            in_specs=[
                whole, whole,
                block(flat, 0, 0, 0, 0), block(flat, 0, tiles + 1, 0, 0),
                block(flat, 0, 0, 0, 0), block(flat, 0, tiles + 1, 0, 0),
            ],
            out_specs=(whole, whole),
            name="sides",
        )(side_low, side_high, above, above, below, below)
        from_low, from_high = both_ways(margin_low, margin_high, "tx")

        parts = pl.pallas_call(
            plane_kernel,
            out_shape=jax.ShapeDtypeStruct((len(lines[0]), 6, 8, LANES), F32),
            in_specs=[VMEM],
            out_specs=VMEM,
            name="plane_sum",
        )(parts)
        parts = trade(parts, lines)
        pieces = pl.pallas_call(
            probe_kernel,
            out_shape=jax.ShapeDtypeStruct((members, 4, 8, LANES), F32),
            in_specs=[SMEM, VMEM, VMEM],
            out_specs=VMEM,
            name="probe_rows",
        )(piece, parts, probe)
        probe_new = pl.pallas_call(
            join_kernel,
            out_shape=jax.ShapeDtypeStruct(probe.shape, F32),
            in_specs=[VMEM],
            out_specs=VMEM,
            name="join",
        )(trade(pieces, planes))

        scale = pl.pallas_call(
            weight_kernel,
            out_shape=jax.ShapeDtypeStruct((tiles, side, LANES), F32),
            in_specs=[VMEM] + [ANY] * 5,
            out_specs=VMEM,
            scratch_shapes=[
                pltpu.VMEM((2, size, LANES), F32),
                pltpu.VMEM((tiles + 4, side + 2 * size, LANES), F32),
                pltpu.SMEM((9, 8, LANES), F32),
                pltpu.SemaphoreType.DMA((9,)),
            ],
            compiler_params=params(16),
            name="weights",
        )(probe, notes, low, high, top, bottom)
        object_new = pl.pallas_call(
            final_kernel,
            out_shape=jax.ShapeDtypeStruct(object_field.shape, F32),
            grid=(tiles,),
            in_specs=[
                pl.BlockSpec((2, side, LANES), lambda index: (0, 0, index)),
                pl.BlockSpec(tall, lambda index: (0, index, 0, 0)),
                pl.BlockSpec(flat, lambda index: (0, index + 1, 0, 0)),
                pl.BlockSpec(flat, lambda index: (0, index + 1, 0, 0)),
                block((2, side, LANES), 0, 0, 0),
                block((2, side, LANES), 0, 0, 0),
                pl.BlockSpec((1, side, LANES), lambda index: (index, 0, 0)),
            ],
            out_specs=pl.BlockSpec((2, side, LANES), lambda index: (0, 0, index)),
            compiler_params=params(24),
            name="final",
        )(object_field, middle, above, below, from_low, from_high, scale)
        return (object_new, probe_new)

    in_specs = (
        P(None, "ty", "tx"),
        P(),
        P("ty", "tx", None, None, None),
        P(None, "ty", "tx", None),
        P("ty", "tx"),
    )
    out_specs = (P(None, "ty", "tx"), P())
    return jax.shard_map(per_device, mesh=mesh, in_specs=in_specs, out_specs=out_specs, check_vma=False)
```

time: 421 us -> 161 us (0.38)
  waiting for transfers between devices: 266 us -> 53.8 us
  starting transfers between devices: 101 us -> 69.4 us
  between operations: 15.3 us -> 1.57 us
  Pallas kernels: 15.2 us -> 23 us
  local copies, waits for them, and re-layouts: 15.8 us -> 10 us
    psum x1 -> x0, waiting for transfers between devices: 241 us -> none  [per_device(): totals = lax.psum(probe_sum, ('ty', 'tx'))]
    ppermute x24 -> x8, starting transfers between devices: 101 us -> 21.8 us  [both_ways(): return (lax.ppermute(high, axis, up), lax.ppermute(low, axis, down))]
    all_to_all x0 -> x3, starting transfers between devices: none -> 47.7 us  [trade(): lax.all_to_all(pieces, ('ty', 'tx'), 0, 0, axis_index_groups=groups, tile...]
    ppermute x24 -> x8, waiting for transfers between devices: 25 us -> 44.4 us  [both_ways(): return (lax.ppermute(high, axis, up), lax.ppermute(low, axis, down))]
    pallas_call x2 -> x8, Pallas kernels: 9.93 us -> 19.6 us  [the longest x1 8.23 us: per_device(): pl.pallas_call(slot_kernel, out_shape=(margin, margin, strip, strip, jax....]
    all_to_all x0 -> x3, waiting for transfers between devices: none -> 9.42 us  [trade(): lax.all_to_all(pieces, ('ty', 'tx'), 0, 0, axis_index_groups=groups, tile...]
    squeeze x4 -> x0, local copies, waits for them, and re-layouts: 5.53 us -> none  [margins_of_grid(): out.append(grid[:, 0 if across < 0 else -1, rows[down], :])]
    slice x5 -> x1, local copies, waits for them, and re-layouts: 5.83 us -> 1.43 us  [per_device(): object_field[:, :, :half]]
  transfers between devices with their start and end apart: 25 -> 11, of which waited for: 4 -> 7; matrix products, arithmetic and copies ran while one was open for 3% -> 0% of each run, Pallas kernels for 2% -> 8%
where the time goes in v2:
time: 161 us; the launch traced here: 159 us
  starting transfers between devices  69.4 us (43%)
  waiting for transfers between devices  53.8 us (33%)
  Pallas kernels  23 us (14%)
  local copies, waits for them, and re-layouts  10 us (6%)
    all_to_all x3, starting transfers between devices, trade(): lax.all_to_all(pieces, ('ty', 'tx'), 0, 0, axis_index_groups=groups, tile...  47.7 us
    ppermute x8, waiting for transfers between devices, both_ways(): return (lax.ppermute(high, axis, up), lax.ppermute(low, axis, down))  44.4 us
    ppermute x8, starting transfers between devices, both_ways(): return (lax.ppermute(high, axis, up), lax.ppermute(low, axis, down))  21.8 us
    all_to_all x3, waiting for transfers between devices, trade(): lax.all_to_all(pieces, ('ty', 'tx'), 0, 0, axis_index_groups=groups, tile...  9.42 us
    unnamed x42, local copies, waits for them, and re-layouts  8.52 us
    pallas_call x1, Pallas kernels, per_device(): pl.pallas_call(slot_kernel, out_shape=(margin, margin, strip, strip, jax....  8.23 us
    pallas_call x1, Pallas kernels, per_device(): pl.pallas_call(final_kernel, out_shape=jax.ShapeDtypeStruct(object_field....  3.44 us
  transfers between devices with their start and end apart: 11, of which 7 were waited for; matrix products, arithmetic and copies ran while one was open for 0% of the time, Pallas kernels for 8%

profile of v2, /device:TPU:1, one launch (start us, length us, event | category | flops | bytes accessed | tf_op | source)
XLA Modules:
  0.0 158.6 jit_solution(6659901490583958702)
XLA Ops:
  1.3 0.7 convert_element_type.7
  2.0 1.4 fusion
  3.4 0.1 scatter.9
  3.5 0.1 pad_maximum_fusion
  3.6 0.0 copy-start.14
  3.6 0.0 copy-start.17
  3.6 0.0 copy-start.18
  3.6 4.7 %collective-permute-start = (f32[2,520,128]{2,1,0:T(8,128)S(1)}, f32[2,520,128]{2,1,0:T(8,128)S(1)}, u32[]{:S(2)}, u32[]{:S(2)}) collective-permute-start(f32[2,520,128]{2,1,0:T(8,128)S(1)} %get-tuple-element.49), channel_id=1, source_target_pairs={{0,1},{1,2},{2,3},{3,4},{4,5},{5,6},{6,7},{7,8},{8,9},{9,10},{10,1... | collective-permute-start | bytes 1597448 | tf_op jit(solution)/shard_map/ppermute | solution.py:299
  8.3 1.3 collective-permute-start.1
  9.6 9.4 %collective-permute-done.low = f32[2,520,128]{2,1,0:T(8,128)S(1)} collective-permute-done((f32[2,520,128]{2,1,0:T(8,128)S(1)}, f32[2,520,128]{2,1,0:T(8,128)S(1)}, u32[]{:S(2)}, u32[]{:S(2)}) %collective-permute-start) | collective-permute-done | bytes 532512 | tf_op jit(solution)/shard_map/ppermute | solution.py:299
  19.0 15.9 %collective-permute-done.1.high = f32[2,520,128]{2,1,0:T(8,128)S(1)} collective-permute-done((f32[2,520,128]{2,1,0:T(8,128)S(1)}, f32[2,520,128]{2,1,0:T(8,128)S(1)}, u32[]{:S(2)}, u32[]{:S(2)}) %collective-permute-start.1) | collective-permute-done | bytes 532512 | tf_op jit(solution)/shard_map/ppermute | solution.py:299
  34.9 0.1 ends.1
  35.0 3.6 %collective-permute-start.2 = (f32[2,6,136,128]{3,2,1,0:T(8,128)S(1)}, f32[2,6,136,128]{3,2,1,0:T(8,128)S(1)}, u32[]{:S(2)}, u32[]{:S(2)}) collective-permute-start(f32[2,6,136,128]{3,2,1,0:T(8,128)S(1)} %get-tuple-element.36), channel_id=1, source_target_pairs={{0,16},{16,32},{32,48},{48,64},{64,80},{80,96},{96,112},{112,128},... | collective-permute-start | bytes 2506760 | tf_op jit(solution)/shard_map/ppermute | solution.py:299
  38.6 1.9 %collective-permute-start.3 = (f32[2,6,136,128]{3,2,1,0:T(8,128)S(1)}, f32[2,6,136,128]{3,2,1,0:T(8,128)S(1)}, u32[]{:S(2)}, u32[]{:S(2)}) collective-permute-start(f32[2,6,136,128]{3,2,1,0:T(8,128)S(1)} %get-tuple-element.37), channel_id=1, source_target_pairs={{16,0},{32,16},{48,32},{64,48},{80,64},{96,80},{112,96},{128,112},... | collective-permute-start | bytes 2506760 | tf_op jit(solution)/shard_map/ppermute | solution.py:299
  40.6 0.0 copy-start.7
  40.6 0.0 copy-start.19
  40.6 0.7 fold.1.folded
  41.3 0.0 copy-start.2
  41.3 1.3 copy-done.2
  42.6 5.5 %collective-permute-done.2.top = f32[2,6,136,128]{3,2,1,0:T(8,128)S(1)} collective-permute-done((f32[2,6,136,128]{3,2,1,0:T(8,128)S(1)}, f32[2,6,136,128]{3,2,1,0:T(8,128)S(1)}, u32[]{:S(2)}, u32[]{:S(2)}) %collective-permute-start.2) | collective-permute-done | bytes 835616 | tf_op jit(solution)/shard_map/ppermute | solution.py:299
  48.1 4.4 %collective-permute-done.3.bottom = f32[2,6,136,128]{3,2,1,0:T(8,128)S(1)} collective-permute-done((f32[2,6,136,128]{3,2,1,0:T(8,128)S(1)}, f32[2,6,136,128]{3,2,1,0:T(8,128)S(1)}, u32[]{:S(2)}, u32[]{:S(2)}) %collective-permute-start.3) | collective-permute-done | bytes 835616 | tf_op jit(solution)/shard_map/ppermute | solution.py:299
  52.5 0.9 copy-done.11
  53.4 8.2 %slots.1 = (f32[2,6,128,128]{3,2,1,0:T(8,128)S(1)}, f32[2,6,128,128]{3,2,1,0:T(8,128)}, f32[2,512,128]{2,1,0:T(8,128)S(1)}, f32[2,512,128]{2,1,0:T(8,128)S(1)}, ...) custom-call(s32[2,8]{1,0:T(2,128)S(1)} %bitcast.11, s32[1]{0:T(128)} %bitcast.8.count, ...), custom_call_target="tpu_custom_call" | custom-call | tf_op jit(solution)/shard_map/slots/pallas_call | solution.py:368
  61.6 0.8 copy-done.15
  62.4 0.8 copy-done.16
  63.2 24.9 %all-to-all-start = ((f32[32,6,8,128]{3,2,1,0:T(8,128)}), f32[32,6,8,128]{3,2,1,0:T(8,128)}, u32[]{:S(2)}, u32[]{:S(2)}) async-start(f32[32,6,8,128]{3,2,1,0:T(8,128)} %get-tuple-element.45), calls=%async_computation | async-start | bytes 1572864 | tf_op jit(solution)/shard_map/all_to_all | solution.py:321
  88.1 3.5 %collective-permute-start.4 = (f32[2,6,128,128]{3,2,1,0:T(8,128)}, f32[2,6,128,128]{3,2,1,0:T(8,128)S(1)}, u32[]{:S(2)}, u32[]{:S(2)}) collective-permute-start(f32[2,6,128,128]{3,2,1,0:T(8,128)} %get-tuple-element.39), channel_id=1, source_target_pairs={{0,16},{16,32},{32,48},{48,64},{64,80},{80,96},{96,112},{112,128},... | collective-permute-start | bytes 2359304 | tf_op jit(solution)/shard_map/ppermute | solution.py:299
  91.7 1.9 %collective-permute-start.5 = (f32[2,6,128,128]{3,2,1,0:T(8,128)S(1)}, f32[2,6,128,128]{3,2,1,0:T(8,128)S(1)}, u32[]{:S(2)}, u32[]{:S(2)}) collective-permute-start(f32[2,6,128,128]{3,2,1,0:T(8,128)S(1)} %get-tuple-element.40), channel_id=1, source_target_pairs={{16,0},{32,16},{48,32},{64,48},{80,64},{96,80},{112,96},{128,112},... | collective-permute-start | bytes 2359304 | tf_op jit(solution)/shard_map/ppermute | solution.py:299
  93.6 8.3 %all-to-all-done.parts = f32[32,6,8,128]{3,2,1,0:T(8,128)} async-done(((f32[32,6,8,128]{3,2,1,0:T(8,128)}), f32[32,6,8,128]{3,2,1,0:T(8,128)}, u32[]{:S(2)}, u32[]{:S(2)}) %all-to-all-start) | async-done | bytes 786464 | tf_op jit(solution)/shard_map/all_to_all | solution.py:321
  101.8 1.9 %plane_sum.1 = f32[8,6,8,128]{3,2,1,0:T(8,128)} custom-call(f32[32,6,8,128]{3,2,1,0:T(8,128)} %all-to-all-done.parts), custom_call_target="tpu_custom_call" | custom-call | tf_op jit(solution)/shard_map/plane_sum/pallas_call | solution.py:408
  103.7 14.2 %all-to-all-start.1 = ((f32[8,6,8,128]{3,2,1,0:T(8,128)}), f32[8,6,8,128]{3,2,1,0:T(8,128)}, u32[]{:S(2)}, u32[]{:S(2)}) async-start(f32[8,6,8,128]{3,2,1,0:T(8,128)} %plane_sum.1), calls=%async_computation.1 | async-start | bytes 393216 | tf_op jit(solution)/shard_map/all_to_all | solution.py:321
  117.9 0.0 copy-start.3
  118.0 0.8 copy-done.3
  118.8 0.3 copy-done.5
  119.1 2.4 %sides.1 = (f32[2,512,128]{2,1,0:T(8,128)}, f32[2,512,128]{2,1,0:T(8,128)}) custom-call(f32[2,512,128]{2,1,0:T(8,128)} %copy-done.15, f32[2,512,128]{2,1,0:T(8,128)} %copy-done.16, f32[2,6,128,128]{3,2,1,0:T(8,128)} %copy-done.3, f32[2,6,128,128]{3,2,1,0:T(8,128)} %copy-done.3, f32[2,6,128,128]{3,2,1,0:T(8,128)} %copy-done.5, f32[2,6,128,128]{3,2,1,0:T(8,128)} %copy-done.5), custom_call_target="tpu_custom_call" | custom-call | tf_op jit(solution)/shard_map/sides/pallas_call | solution.py:394
  121.5 3.5 %collective-permute-start.6 = (f32[2,512,128]{2,1,0:T(8,128)}, f32[2,512,128]{2,1,0:T(8,128)S(1)}, u32[]{:S(2)}, u32[]{:S(2)}) collective-permute-start(f32[2,512,128]{2,1,0:T(8,128)} %get-tuple-element.43), channel_id=1, source_target_pairs={{0,1},{1,2},{2,3},{3,4},{4,5},{5,6},{6,7},{7,8},{8,9},{9,10},{10,1... | collective-permute-start | bytes 1572872 | tf_op jit(solution)/shard_map/ppermute | solution.py:299
  125.0 1.3 collective-permute-start.7
  126.3 1.2 all-to-all-done.1.parts
  127.5 2.0 %probe_rows.1 = f32[32,4,8,128]{3,2,1,0:T(8,128)} custom-call(s32[1]{0:T(128)} %bitcast.5.index, f32[8,6,8,128]{3,2,1,0:T(8,128)} %all-to-all-done.1.parts, f32[2,256,256]{2,1,0:T(8,128)} %probe.5), custom_call_target="tpu_custom_call" | custom-call | tf_op jit(solution)/shard_map/probe_rows/pallas_call | solution.py:416
  129.5 8.6 %all-to-all-start.2 = ((f32[32,4,8,128]{3,2,1,0:T(8,128)}), f32[32,4,8,128]{3,2,1,0:T(8,128)S(1)}, u32[]{:S(2)}, u32[]{:S(2)}) async-start(f32[32,4,8,128]{3,2,1,0:T(8,128)} %probe_rows.1), calls=%async_computation.2 | async-start | bytes 1048576 | tf_op jit(solution)/shard_map/all_to_all | solution.py:321
  138.1 1.1 copy-done.12
  139.2 2.5 %weights.1.scale = f32[4,512,128]{2,1,0:T(8,128)S(1)} custom-call(f32[2,256,256]{2,1,0:T(8,128)S(1)} %copy-done.8, f32[2,8,128]{2,1,0:T(8,128)S(1)} %stack.10.notes, f32[2,520,128]{2,1,0:T(8,128)S(1)} %collective-permute-done.low, f32[2,520,128]{2,1,0:T(8,128)S(1)} %collective-permute-done.1.high, f32[2,6,136,128]{3,2,1,0:T(8,128)S(1)} %copy-done.10, ...), custom_call_target="tpu_custom_call" | custom-call | tf_op jit(solution)/shard_map/weights/pallas_call | solution.py:431
  141.7 0.0 collective-permute-done.6.low
  141.7 9.2 %collective-permute-done.7.high = f32[2,512,128]{2,1,0:T(8,128)} collective-permute-done((f32[2,512,128]{2,1,0:T(8,128)}, f32[2,512,128]{2,1,0:T(8,128)}, u32[]{:S(2)}, u32[]{:S(2)}) %collective-permute-start.7) | collective-permute-done | bytes 524320 | tf_op jit(solution)/shard_map/ppermute | solution.py:299
  150.9 1.6 copy-done.13
  152.5 3.4 %final.1 = f32[2,512,512]{2,1,0:T(8,128)} custom-call(f32[2,512,512]{2,1,0:T(8,128)S(1)} %copy-done.1, f32[2,4,512,128]{3,2,1,0:T(8,128)S(1)} %copy-done.13, f32[2,6,128,128]{3,2,1,0:T(8,128)S(1)} %copy-done.4, f32[2,6,128,128]{3,2,1,0:T(8,128)S(1)} %copy-done.6, f32[2,512,128]{2,1,0:T(8,128)S(1)} %collective-permute-done.6.low, ...), custom_call_target="tpu_custom_call" | custom-call | tf_op jit(solution)/shard_map/final/pallas_call | solution.py:445
  155.9 0.8 copy-done.20
  156.7 1.9 %join.1 = f32[2,256,256]{2,1,0:T(8,128)} custom-call(f32[32,4,8,128]{3,2,1,0:T(8,128)} %copy-done.20), custom_call_target="tpu_custom_call" | custom-call | tf_op jit(solution)/shard_map/join/pallas_call | solution.py:423
  (31 shorter events, 0.1 us)
Async XLA Ops:
  2.0 33.0 %copy-start = (f32[2,512,512]{2,1,0:T(8,128)S(1)}, f32[2,512,512]{2,1,0:T(8,128)}, u32[]{:S(2)}) copy-start(f32[2,512,512]{2,1,0:T(8,128)} %tile_ref.5) | copy-start | bytes 6291460
  3.6 37.0 %copy-start.14 = (f32[1,1,8,256,256]{4,3,2,1,0:T(8,128)S(1)}, f32[1,1,8,256,256]{4,3,2,1,0:T(8,128)}, u32[]{:S(2)}) copy-start(f32[1,1,8,256,256]{4,3,2,1,0:T(8,128)} %param.15) | copy-start | bytes 6291460
  3.6 37.0 %copy-start.17 = (bf16[256,768]{1,0:T(8,128)(2,1)S(1)}, bf16[256,768]{1,0:T(8,128)(2,1)}, u32[]{:S(2)}) copy-start(bf16[256,768]{1,0:T(8,128)(2,1)} %constant.81.clone.gather_left) | copy-start | bytes 1179652
  3.6 37.0 %copy-start.18 = (bf16[768,256]{1,0:T(8,128)(2,1)S(1)}, bf16[768,256]{1,0:T(8,128)(2,1)}, u32[]{:S(2)}) copy-start(bf16[768,256]{1,0:T(8,128)(2,1)} %constant.82.clone.gather_right) | copy-start | bytes 1179652
  3.6 15.4 %collective-permute-start = (f32[2,520,128]{2,1,0:T(8,128)S(1)}, f32[2,520,128]{2,1,0:T(8,128)S(1)}, u32[]{:S(2)}, u32[]{:S(2)}) collective-permute-start(f32[2,520,128]{2,1,0:T(8,128)S(1)} %get-tuple-element.49), channel_id=1, source_target_pairs={{0,1},{1,2},{2,3},{3,4},{4,5},{5,6},{6,7},{7,8},{8,9},{9,10},{10,1... | collective-permute-start | bytes 1597448 | tf_op jit(solution)/shard_map/ppermute | solution.py:299
  8.3 26.6 %collective-permute-start.1 = (f32[2,520,128]{2,1,0:T(8,128)S(1)}, f32[2,520,128]{2,1,0:T(8,128)S(1)}, u32[]{:S(2)}, u32[]{:S(2)}) collective-permute-start(f32[2,520,128]{2,1,0:T(8,128)S(1)} %get-tuple-element.48), channel_id=1, source_target_pairs={{1,0},{2,1},{3,2},{4,3},{5,4},{6,5},{7,6},{8,7},{9,8},{10,9},{11,1... | collective-permute-start | bytes 1597448 | tf_op jit(solution)/shard_map/ppermute | solution.py:299
  35.0 13.0 %collective-permute-start.2 = (f32[2,6,136,128]{3,2,1,0:T(8,128)S(1)}, f32[2,6,136,128]{3,2,1,0:T(8,128)S(1)}, u32[]{:S(2)}, u32[]{:S(2)}) collective-permute-start(f32[2,6,136,128]{3,2,1,0:T(8,128)S(1)} %get-tuple-element.36), channel_id=1, source_target_pairs={{0,16},{16,32},{32,48},{48,64},{64,80},{80,96},{96,112},{112,128},... | collective-permute-start | bytes 2506760 | tf_op jit(solution)/shard_map/ppermute | solution.py:299
  38.6 13.8 %collective-permute-start.3 = (f32[2,6,136,128]{3,2,1,0:T(8,128)S(1)}, f32[2,6,136,128]{3,2,1,0:T(8,128)S(1)}, u32[]{:S(2)}, u32[]{:S(2)}) collective-permute-start(f32[2,6,136,128]{3,2,1,0:T(8,128)S(1)} %get-tuple-element.37), channel_id=1, source_target_pairs={{16,0},{32,16},{48,32},{64,48},{80,64},{96,80},{112,96},{128,112},... | collective-permute-start | bytes 2506760 | tf_op jit(solution)/shard_map/ppermute | solution.py:299
  40.6 12.8 %copy-start.7 = (f32[2,256,256]{2,1,0:T(8,128)S(1)}, f32[2,256,256]{2,1,0:T(8,128)}, u32[]{:S(2)}) copy-start(f32[2,256,256]{2,1,0:T(8,128)} %probe.5) | copy-start | bytes 1572868
  40.6 12.8 %copy-start.19 = (s32[2,1,1,8]{3,2,1,0:T(1,128)S(1)}, s32[2,1,1,8]{3,2,1,0:T(1,128)}, u32[]{:S(2)}) copy-start(s32[2,1,1,8]{3,2,1,0:T(1,128)} %param.16) | copy-start | bytes 196
  41.3 1.3 copy-start.2
  48.1 13.5 %copy-start.9 = (f32[2,6,136,128]{3,2,1,0:T(8,128)}, f32[2,6,136,128]{3,2,1,0:T(8,128)S(1)}, u32[]{:S(2)}) copy-start(f32[2,6,136,128]{3,2,1,0:T(8,128)S(1)} %collective-permute-done.2.top) | copy-start | bytes 2506756
  52.5 0.9 copy-start.11
  61.6 0.8 copy-start.15
  62.4 0.8 copy-start.16
  63.2 38.6 %all-to-all-start = ((f32[32,6,8,128]{3,2,1,0:T(8,128)}), f32[32,6,8,128]{3,2,1,0:T(8,128)}, u32[]{:S(2)}, u32[]{:S(2)}) async-start(f32[32,6,8,128]{3,2,1,0:T(8,128)} %get-tuple-element.45), calls=%async_computation | async-start | bytes 1572864 | tf_op jit(solution)/shard_map/all_to_all | solution.py:321
  88.1 29.8 %collective-permute-start.4 = (f32[2,6,128,128]{3,2,1,0:T(8,128)}, f32[2,6,128,128]{3,2,1,0:T(8,128)S(1)}, u32[]{:S(2)}, u32[]{:S(2)}) collective-permute-start(f32[2,6,128,128]{3,2,1,0:T(8,128)} %get-tuple-element.39), channel_id=1, source_target_pairs={{0,16},{16,32},{32,48},{48,64},{64,80},{80,96},{96,112},{112,128},... | collective-permute-start | bytes 2359304 | tf_op jit(solution)/shard_map/ppermute | solution.py:299
  91.7 26.3 %collective-permute-start.5 = (f32[2,6,128,128]{3,2,1,0:T(8,128)S(1)}, f32[2,6,128,128]{3,2,1,0:T(8,128)S(1)}, u32[]{:S(2)}, u32[]{:S(2)}) collective-permute-start(f32[2,6,128,128]{3,2,1,0:T(8,128)S(1)} %get-tuple-element.40), channel_id=1, source_target_pairs={{16,0},{32,16},{48,32},{64,48},{80,64},{96,80},{112,96},{128,112},... | collective-permute-start | bytes 2359304 | tf_op jit(solution)/shard_map/ppermute | solution.py:299
  103.7 23.8 %all-to-all-start.1 = ((f32[8,6,8,128]{3,2,1,0:T(8,128)}), f32[8,6,8,128]{3,2,1,0:T(8,128)}, u32[]{:S(2)}, u32[]{:S(2)}) async-start(f32[8,6,8,128]{3,2,1,0:T(8,128)} %plane_sum.1), calls=%async_computation.1 | async-start | bytes 393216 | tf_op jit(solution)/shard_map/all_to_all | solution.py:321
  117.9 0.9 copy-start.3
  118.0 1.1 copy-start.5
  121.5 16.6 %copy-start.8 = (f32[2,256,256]{2,1,0:T(8,128)S(1)}, f32[2,256,256]{2,1,0:T(8,128)}, u32[]{:S(2)}) copy-start(f32[2,256,256]{2,1,0:T(8,128)} %probe.5) | copy-start | bytes 1572868
  121.5 16.6 %copy-start.10 = (f32[2,6,136,128]{3,2,1,0:T(8,128)S(1)}, f32[2,6,136,128]{3,2,1,0:T(8,128)}, u32[]{:S(2)}) copy-start(f32[2,6,136,128]{3,2,1,0:T(8,128)} %copy-done.9) | copy-start | bytes 2506756
  121.5 20.2 %collective-permute-start.6 = (f32[2,512,128]{2,1,0:T(8,128)}, f32[2,512,128]{2,1,0:T(8,128)S(1)}, u32[]{:S(2)}, u32[]{:S(2)}) collective-permute-start(f32[2,512,128]{2,1,0:T(8,128)} %get-tuple-element.43), channel_id=1, source_target_pairs={{0,1},{1,2},{2,3},{3,4},{4,5},{5,6},{6,7},{7,8},{8,9},{9,10},{10,1... | collective-permute-start | bytes 1572872 | tf_op jit(solution)/shard_map/ppermute | solution.py:299
  125.0 25.9 %collective-permute-start.7 = (f32[2,512,128]{2,1,0:T(8,128)}, f32[2,512,128]{2,1,0:T(8,128)}, u32[]{:S(2)}, u32[]{:S(2)}) collective-permute-start(f32[2,512,128]{2,1,0:T(8,128)} %get-tuple-element.44), channel_id=1, source_target_pairs={{1,0},{2,1},{3,2},{4,3},{5,4},{6,5},{7,6},{8,7},{9,8},{10,9},{11,1... | collective-permute-start | bytes 1572872 | tf_op jit(solution)/shard_map/ppermute | solution.py:299
  129.5 26.4 %all-to-all-start.2 = ((f32[32,4,8,128]{3,2,1,0:T(8,128)}), f32[32,4,8,128]{3,2,1,0:T(8,128)S(1)}, u32[]{:S(2)}, u32[]{:S(2)}) async-start(f32[32,4,8,128]{3,2,1,0:T(8,128)} %probe_rows.1), calls=%async_computation.2 | async-start | bytes 1048576 | tf_op jit(solution)/shard_map/all_to_all | solution.py:321
  138.1 1.2 copy-start.12
  139.2 11.7 %copy-start.1 = (f32[2,512,512]{2,1,0:T(8,128)S(1)}, f32[2,512,512]{2,1,0:T(8,128)}, u32[]{:S(2)}) copy-start(f32[2,512,512]{2,1,0:T(8,128)} %tile_ref.5) | copy-start | bytes 6291460
  139.2 11.7 %copy-start.4 = (f32[2,6,128,128]{3,2,1,0:T(8,128)S(1)}, f32[2,6,128,128]{3,2,1,0:T(8,128)}, u32[]{:S(2)}) copy-start(f32[2,6,128,128]{3,2,1,0:T(8,128)} %copy-done.3) | copy-start | bytes 2359300
  139.2 11.7 %copy-start.6 = (f32[2,6,128,128]{3,2,1,0:T(8,128)S(1)}, f32[2,6,128,128]{3,2,1,0:T(8,128)}, u32[]{:S(2)}) copy-start(f32[2,6,128,128]{3,2,1,0:T(8,128)} %copy-done.5) | copy-start | bytes 2359300
  150.9 1.6 %copy-start.13 = (f32[2,4,512,128]{3,2,1,0:T(8,128)S(1)}, f32[2,4,512,128]{3,2,1,0:T(8,128)}, u32[]{:S(2)}) copy-start(f32[2,4,512,128]{3,2,1,0:T(8,128)} %get-tuple-element.38.middle) | copy-start | bytes 6291460
  155.9 0.8 copy-start.20

commit v3 on v2

--- a/solution.py
+++ b/solution.py
@@ -12,7 +12,7 @@
 LANES = 128
 VMEM = pl.BlockSpec(memory_space=pltpu.VMEM)
 SMEM = pl.BlockSpec(memory_space=pltpu.SMEM)
-ANY = pl.BlockSpec(memory_space=pl.ANY)
+HBM = pl.BlockSpec(memory_space=pltpu.HBM)
 def split_host(table):
     high = table.astype(ml_dtypes.bfloat16)
     low = (table - high.astype(np.float64)).astype(ml_dtypes.bfloat16)
@@ -118,9 +118,125 @@
         out[:, 2 : 1 + tiles, half:, :] = jnp.zeros((2, tiles - 1, 8, LANES), F32)
 
 
-def slot_kernel(
-    position, count, probe, folded, left, right, tile_ref, low, high, top, bottom,
-    margin_top, margin_bottom, side_low, side_high, middle, sums, canvas, grad, probe_sum, patch, rhs, lhs,
+def slot_stages(row, tile, offset, live, probe, measured, left, right, canvas, grad, probe_sum, patch, rhs, lhs):
+    size = probe.shape[1]
+    half = size // 2
+    near, far = slice(0, half), slice(half, size)
+    turn = jnp.bitwise_and(LANES - offset, LANES - 1)
+    kept = lax.broadcasted_iota(jnp.int32, (size, LANES), 1) < LANES - offset
+    for plane in range(2):
+        raw = [pltpu.roll(canvas[plane, tile + index, pl.ds(row, size), :], turn, 1) for index in range(3)]
+        patch[plane, 0] = jnp.where(kept, raw[0], raw[1])
+        patch[plane, 1] = jnp.where(kept, raw[1], raw[2])
+    for index, columns in enumerate((near, far)):
+        probe_re, probe_im = probe[0, :, columns], probe[1, :, columns]
+        patch_re, patch_im = patch[0, index], patch[1, index]
+        exit_re = probe_re * patch_re - probe_im * patch_im
+        exit_im = probe_re * patch_im + probe_im * patch_re
+        probe_sum[2, index] += (patch_re * patch_re + patch_im * patch_im) * live
+        put_rows(rhs.at[0], 0, columns, exit_re[:half] + exit_re[half:])
+        put_rows(rhs.at[0], half, columns, exit_im[:half] + exit_im[half:])
+        put_rows(rhs.at[1], 0, columns, exit_re[:half] - exit_re[half:])
+        put_rows(rhs.at[1], half, columns, exit_im[:half] - exit_im[half:])
+    yield
+    for parity in range(2):
+        value = matmul(left[2 * parity], rhs[parity])
+        rows = slice(parity * half, (parity + 1) * half)
+        put_columns(lhs.at[0], rows, 0, value[:half, near] + value[:half, far])
+        put_columns(lhs.at[0], rows, half, value[half:, near] + value[half:, far])
+        put_columns(lhs.at[1], rows, 0, value[:half, near] - value[:half, far])
+        put_columns(lhs.at[1], rows, half, value[half:, near] - value[half:, far])
+        yield
+    everything = slice(0, size)
+    for parity in range(2):
+        value = matmul(lhs[parity], right[2 * parity + 1])
+        wave_re, wave_im = value[:, near], value[:, far]
+        columns = slice(parity * half, (parity + 1) * half)
+        excess = (wave_re * wave_re + wave_im * wave_im - measured[:, columns]) * live
+        put_columns(lhs.at[parity], everything, 0, excess * wave_re)
+        put_columns(lhs.at[parity], everything, half, excess * wave_im)
+        yield
+    back = []
+    for parity in range(2):
+        back.append(matmul(lhs[parity], right[2 * parity]))
+    for parity in range(2):
+        rows = slice(parity * half, (parity + 1) * half)
+        put_rows(rhs.at[parity], 0, near, back[0][rows, near] + back[1][rows, near])
+        put_rows(rhs.at[parity], half, near, back[0][rows, far] + back[1][rows, far])
+        put_rows(rhs.at[parity], 0, far, back[0][rows, near] - back[1][rows, near])
+        put_rows(rhs.at[parity], half, far, back[0][rows, far] - back[1][rows, far])
+    yield
+    even = matmul(left[1], rhs[0])
+    odd = matmul(left[3], rhs[1])
+    pieces = []
+    for index, columns in enumerate((near, far)):
+        chi_re, chi_im = (
+            jnp.concatenate([even[rows, columns] + odd[rows, columns], even[rows, columns] - odd[rows, columns]], axis=0)
+            for rows in (near, far)
+        )
+        probe_re, probe_im = probe[0, :, columns], probe[1, :, columns]
+        patch_re, patch_im = patch[0, index], patch[1, index]
+        probe_sum[0, index] += patch_re * chi_re + patch_im * chi_im
+        probe_sum[1, index] += patch_re * chi_im - patch_im * chi_re
+        pieces.append((probe_re * chi_re + probe_im * chi_im, probe_re * chi_im - probe_im * chi_re))
+    for plane in range(2):
+        add_window(grad.at[plane], row, tile, offset, pieces[0][plane], pieces[1][plane])
+    yield
+
+
+def run_slots(wanted, base, position, count, probe, folded, left, right, canvas, grad, probe_sum, order, patch, rhs, lhs):
+    size = probe.shape[1]
+    half = size // 2
+    tiles = canvas.shape[1] - 2
+    reach = tiles * LANES - size
+
+    def pick(slot, found):
+        row = position[0, slot]
+        inside = (row >= 0) & (row <= reach)
+        take = inside if wanted else jnp.logical_not(inside)
+
+        @pl.when(take)
+        def keep():
+            order[found] = slot
+
+        return found + jnp.where(take, 1, 0)
+
+    total = lax.fori_loop(0, count[0], pick, 0)
+    lanes = patch.shape[0]
+
+    def step(group, carry):
+        stages = []
+        for lane in range(lanes):
+            index = lanes * group + lane
+            live = jnp.where(index < total, 1.0, 0.0)
+            slot = order[jnp.minimum(index, total - 1)]
+            row, tile, offset = place(position[0, slot] + base, position[1, slot] + half, tiles - 1)
+            stages.append(slot_stages(
+                row, tile, offset, live, probe, folded.at[slot], left, right, canvas, grad, probe_sum,
+                patch.at[lane], rhs.at[lane], lhs.at[lane],
+            ))
+        for _ in zip(*stages):
+            pass
+        return carry
+
+    lax.fori_loop(0, lax.div(total + (lanes - 1), lanes), step, 0)
+
+
+def inner_kernel(position, count, probe, folded, left, right, tile_ref, low, high, grad, probe_sum, canvas, *scratch):
+    side = tile_ref.shape[1]
+    tiles = side // LANES
+    for index in range(tiles):
+        canvas[:, 1 + index] = tile_ref[:, :, index * LANES : (index + 1) * LANES]
+    canvas[:, 0] = low[:, :side, :]
+    canvas[:, 1 + tiles] = high[:, :side, :]
+    grad[...] = jnp.zeros_like(grad)
+    probe_sum[...] = jnp.zeros_like(probe_sum)
+    run_slots(True, 0, position, count, probe, folded, left, right, canvas, grad, probe_sum, *scratch)
+
+
+def outer_kernel(
+    position, count, probe, folded, left, right, tile_ref, low, high, top, bottom, own_notes, grad_in, probe_sum_in,
+    margin_top, margin_bottom, side_low, side_high, middle, sums, places, canvas, grad, probe_sum, sems, *scratch,
 ):
     size = probe.shape[1]
     half = size // 2
@@ -133,77 +249,36 @@
     canvas[:, 1 + tiles, inner, :] = high[:, :side, :]
     canvas[:, :, :half, :] = top[:, :, :half, :]
     canvas[:, :, half + side :, :] = bottom[:, :, :half, :]
-    grad[...] = jnp.zeros_like(grad)
-    probe_sum[...] = jnp.zeros_like(probe_sum)
-    near, far = slice(0, half), slice(half, size)
-
-    def step(slot, carry):
-        row, tile, offset = place(position[0, slot] + half, position[1, slot] + half, tiles - 1)
-        turn = jnp.bitwise_and(LANES - offset, LANES - 1)
-        kept = lax.broadcasted_iota(jnp.int32, (size, LANES), 1) < LANES - offset
-        for plane in range(2):
-            raw = [pltpu.roll(canvas[plane, tile + index, pl.ds(row, size), :], turn, 1) for index in range(3)]
-            patch[plane, 0] = jnp.where(kept, raw[0], raw[1])
-            patch[plane, 1] = jnp.where(kept, raw[1], raw[2])
-        for index, columns in enumerate((near, far)):
-            probe_re, probe_im = probe[0, :, columns], probe[1, :, columns]
-            patch_re, patch_im = patch[0, index], patch[1, index]
-            exit_re = probe_re * patch_re - probe_im * patch_im
-            exit_im = probe_re * patch_im + probe_im * patch_re
-            probe_sum[2, index] += patch_re * patch_re + patch_im * patch_im
-            put_rows(rhs.at[0], 0, columns, exit_re[:half] + exit_re[half:])
-            put_rows(rhs.at[0], half, columns, exit_im[:half] + exit_im[half:])
-            put_rows(rhs.at[1], 0, columns, exit_re[:half] - exit_re[half:])
-            put_rows(rhs.at[1], half, columns, exit_im[:half] - exit_im[half:])
-        for parity_ in range(2):
-            value = matmul(left[2 * parity_], rhs[parity_])
-            rows = slice(parity_ * half, (parity_ + 1) * half)
-            put_columns(lhs.at[0], rows, 0, value[:half, near] + value[:half, far])
-            put_columns(lhs.at[0], rows, half, value[half:, near] + value[half:, far])
-            put_columns(lhs.at[1], rows, 0, value[:half, near] - value[:half, far])
-            put_columns(lhs.at[1], rows, half, value[half:, near] - value[half:, far])
-        everything = slice(0, size)
-        back = []
-        for parity_ in range(2):
-            value = matmul(lhs[parity_], right[2 * parity_ + 1])
-            wave_re, wave_im = value[:, near], value[:, far]
-            columns = slice(parity_ * half, (parity_ + 1) * half)
-            excess = wave_re * wave_re + wave_im * wave_im - folded[slot, :, columns]
-            put_columns(lhs.at[parity_], everything, 0, excess * wave_re)
-            put_columns(lhs.at[parity_], everything, half, excess * wave_im)
-            back.append(matmul(lhs[parity_], right[2 * parity_]))
-        for parity_ in range(2):
-            rows = slice(parity_ * half, (parity_ + 1) * half)
-            put_rows(rhs.at[parity_], 0, near, back[0][rows, near] + back[1][rows, near])
-            put_rows(rhs.at[parity_], half, near, back[0][rows, far] + back[1][rows, far])
-            put_rows(rhs.at[parity_], 0, far, back[0][rows, near] - back[1][rows, near])
-            put_rows(rhs.at[parity_], half, far, back[0][rows, far] - back[1][rows, far])
-        even = matmul(left[1], rhs[0])
-        odd = matmul(left[3], rhs[1])
-        pieces = []
-        for index, columns in enumerate((near, far)):
-            chi_re, chi_im = (
-                jnp.concatenate([even[rows, columns] + odd[rows, columns], even[rows, columns] - odd[rows, columns]], axis=0)
-                for rows in (near, far)
-            )
-            probe_re, probe_im = probe[0, :, columns], probe[1, :, columns]
-            patch_re, patch_im = patch[0, index], patch[1, index]
-            probe_sum[0, index] += patch_re * chi_re + patch_im * chi_im
-            probe_sum[1, index] += patch_re * chi_im - patch_im * chi_re
-            pieces.append((probe_re * chi_re + probe_im * chi_im, probe_re * chi_im - probe_im * chi_re))
-        for plane in range(2):
-            add_window(grad.at[plane], row, tile, offset, pieces[0][plane], pieces[1][plane])
-        return carry
-
-    lax.fori_loop(0, count[0], step, 0)
-    margin_top[...] = grad[:, :, :half, :]
-    margin_bottom[...] = grad[:, :, half + side :, :]
-    side_low[...] = grad[:, 0, inner, :]
-    side_high[...] = grad[:, 1 + tiles, inner, :]
-    middle[...] = grad[:, 1 : 1 + tiles, inner, :]
+    grad[:, :, :half, :] = jnp.zeros(margin_top.shape, F32)
+    grad[:, :, half + side :, :] = jnp.zeros(margin_bottom.shape, F32)
+    grad[:, :, inner, :] = grad_in[...]
+    probe_sum[...] = probe_sum_in[...]
+    run_slots(False, half, position, count, probe, folded, left, right, canvas, grad, probe_sum, *scratch)
+    ends = slice(half, half + 8)
+    notes = (
+        top[0, 0, ends], top[0, 1, ends], top[0, 1 + tiles, ends],
+        low[0, side:], own_notes[0], high[0, side:],
+        bottom[0, 0, ends], bottom[0, 1, ends], bottom[0, 1 + tiles, ends],
+    )
+    for index, value in enumerate(notes):
+        places[index] = value
+    copies = [
+        pltpu.make_async_copy(source, target, sems.at[index])
+        for index, (source, target) in enumerate((
+            (grad.at[:, :, :half, :], margin_top),
+            (grad.at[:, :, half + side :, :], margin_bottom),
+            (grad.at[:, 0, inner, :], side_low),
+            (grad.at[:, 1 + tiles, inner, :], side_high),
+            (grad.at[:, 1 : 1 + tiles, inner, :], middle),
+        ))
+    ]
+    for copy in copies:
+        copy.start()
     for plane in range(3):
         for index in range(2):
             sums[:, 2 * plane + index] = probe_sum[plane, index].reshape(size // 8, 8, LANES)
+    for copy in copies:
+        copy.wait()
 
 
 def sides_kernel(first, last, above_first, above_last, below_first, below_last, low, high):
@@ -215,24 +290,14 @@
         out[:, side - half :, :] += below[:, 0]
 
 
-def weight_kernel(probe, notes, low, high, top, bottom, scale, power, weight, numbers, sems):
+def weight_kernel(numbers, probe, scale, power, weight):
     half = LANES
     side = scale.shape[1]
     tiles = side // LANES
-    sources = (
-        top.at[0, 0, half:, :], top.at[0, 1, half:, :], top.at[0, 1 + tiles, half:, :],
-        low.at[0, side:, :], notes.at[0], high.at[0, side:, :],
-        bottom.at[0, 0, half:, :], bottom.at[0, 1, half:, :], bottom.at[0, 1 + tiles, half:, :],
-    )
-    copies = [pltpu.make_async_copy(source, numbers.at[index], sems.at[index]) for index, source in enumerate(sources)]
-    for copy in copies:
-        copy.start()
     weight[...] = jnp.zeros_like(weight)
     for index in range(2):
         columns = slice(index * LANES, (index + 1) * LANES)
         power[index] = probe[0, :, columns] * probe[0, :, columns] + probe[1, :, columns] * probe[1, :, columns]
-    for copy in copies:
-        copy.wait()
     for index in range(9):
         down, across = index // 3 - 1, index % 3 - 1
 
@@ -253,22 +318,25 @@
         scale[index] = 1.0 / (weight[2 + index, 2 * half : 2 * half + side, :] + 1.0)
 
 
-def final_kernel(tile_ref, middle, above, below, low, high, scale, out):
+def update_kernel(tile_ref, grad, above, below, scale, out):
     half = LANES
     side = tile_ref.shape[1]
-    index = pl.program_id(0)
-    is_first = (index == 0).astype(F32)
-    is_last = (index == pl.num_programs(0) - 1).astype(F32)
     for plane in range(2):
         for start in range(0, side, half):
             rows = slice(start, start + half)
-            value = middle[plane, 0, rows, :]
+            value = grad[plane, 0, rows, :]
             if start == 0:
                 value = value + above[plane, 0]
             if start + half == side:
                 value = value + below[plane, 0]
-            value = value + low[plane, rows, :] * is_first + high[plane, rows, :] * is_last
             out[plane, rows, :] = tile_ref[plane, rows, :] - value * scale[0, rows, :]
+
+
+def edge_kernel(before, low, high, scale, out):
+    is_low = (pl.program_id(0) == 0).astype(F32)
+    is_high = 1.0 - is_low
+    for plane in range(2):
+        out[plane] = before[plane] - (low[plane] * is_low + high[plane] * is_high) * scale[0]
 
 
 def plane_kernel(parts, out):
@@ -305,6 +373,10 @@
 
 def params(mib):
     return pltpu.CompilerParams(vmem_limit_bytes=mib * 2**20)
+
+
+def cost(mib):
+    return pl.CostEstimate(flops=0, bytes_accessed=mib * 2**20, transcendentals=0)
 
 
 def solution(mesh):
@@ -348,7 +420,8 @@
             in_specs=[SMEM, VMEM, VMEM, VMEM],
             out_specs=VMEM,
             scratch_shapes=[pltpu.VMEM((size, 3 * size), BF16)],
-            compiler_params=params(16),
+            compiler_params=params(8),
+            cost_estimate=cost(6),
             name="fold",
         )(count, intensity[0, 0], gather_left, gather_right)
         end = jax.ShapeDtypeStruct((2, tiles + 2, half + 8, LANES), F32)
@@ -357,40 +430,63 @@
             out_shape=(end, end),
             in_specs=[VMEM] * 4,
             out_specs=(VMEM, VMEM),
-            compiler_params=params(16),
+            compiler_params=params(8),
+            cost_estimate=cost(4),
             name="ends",
         )(object_field, low, high, notes)
         top, bottom = both_ways(first_rows, last_rows, "ty")
 
-        margin = jax.ShapeDtypeStruct((2, tiles + 2, half, LANES), F32)
+        margin = pltpu.HBM((2, tiles + 2, half, LANES), F32)
         strip = jax.ShapeDtypeStruct((2, side, LANES), F32)
         members = len(planes[0])
-        margin_top, margin_bottom, side_low, side_high, middle, sums = pl.pallas_call(
-            slot_kernel,
+        lanes = 2
+        scratch = [
+            pltpu.SMEM((slots,), jnp.int32),
+            pltpu.VMEM((lanes, 2, 2, size, LANES), F32),
+            pltpu.VMEM((lanes, 2, 3 * size, size), BF16),
+            pltpu.VMEM((lanes, 2, size, 3 * size), BF16),
+        ]
+        grad, probe_sum = pl.pallas_call(
+            inner_kernel,
             out_shape=(
-                margin, margin, strip, strip,
-                jax.ShapeDtypeStruct((2, tiles, side, LANES), F32),
-                jax.ShapeDtypeStruct((members, 6, 8, LANES), F32),
+                jax.ShapeDtypeStruct((2, tiles + 2, side, LANES), F32),
+                jax.ShapeDtypeStruct((3, 2, size, LANES), F32),
             ),
-            in_specs=[SMEM] * 2 + [VMEM] * 9,
-            out_specs=(VMEM,) * 6,
+            in_specs=[SMEM] * 2 + [VMEM] * 7,
+            out_specs=(VMEM,) * 2,
+            scratch_shapes=[pltpu.VMEM((2, tiles + 2, side, LANES), F32)] + scratch,
+            compiler_params=params(22),
+            cost_estimate=cost(16),
+            name="inner_slots",
+        )(position, count, probe, folded, left, right, object_field, low, high)
+        margin_top, margin_bottom, side_low, side_high, middle, sums, places = pl.pallas_call(
+            outer_kernel,
+            out_shape=(
+                margin, margin,
+                pltpu.HBM((2, side, LANES), F32),
+                pltpu.HBM((2, side, LANES), F32),
+                pltpu.HBM((2, tiles, side, LANES), F32),
+                pltpu.HBM((members, 6, 8, LANES), F32),
+                jax.ShapeDtypeStruct((9, 8, LANES), F32),
+            ),
+            in_specs=[SMEM] * 2 + [VMEM] * 12,
+            out_specs=(HBM,) * 5 + (VMEM, VMEM),
             scratch_shapes=[
                 pltpu.VMEM((2, tiles + 2, side + size, LANES), F32),
                 pltpu.VMEM((2, tiles + 2, side + size, LANES), F32),
                 pltpu.VMEM((3, 2, size, LANES), F32),
-                pltpu.VMEM((2, 2, size, LANES), F32),
-                pltpu.VMEM((2, 3 * size, size), BF16),
-                pltpu.VMEM((2, size, 3 * size), BF16),
-            ],
-            compiler_params=params(48),
-            name="slots",
-        )(position, count, probe, folded, left, right, object_field, low, high, top, bottom)
+                pltpu.SemaphoreType.DMA((5,)),
+            ] + scratch,
+            compiler_params=params(30),
+            cost_estimate=cost(16),
+            name="outer_slots",
+        )(position, count, probe, folded, left, right, object_field, low, high, top, bottom, notes, grad, probe_sum)
 
         above, below = both_ways(margin_top, margin_bottom, "ty")
         parts = trade(sums, planes)
-        tall = (2, 1, side, LANES)
         flat = (2, 1, half, LANES)
         whole = block((2, side, LANES), 0, 0, 0)
+
         margin_low, margin_high = pl.pallas_call(
             sides_kernel,
             out_shape=(strip, strip),
@@ -401,23 +497,29 @@
                 block(flat, 0, 0, 0, 0), block(flat, 0, tiles + 1, 0, 0),
             ],
             out_specs=(whole, whole),
+            compiler_params=params(8),
+            cost_estimate=cost(16),
             name="sides",
         )(side_low, side_high, above, above, below, below)
         from_low, from_high = both_ways(margin_low, margin_high, "tx")
 
         parts = pl.pallas_call(
             plane_kernel,
-            out_shape=jax.ShapeDtypeStruct((len(lines[0]), 6, 8, LANES), F32),
+            out_shape=pltpu.HBM((len(lines[0]), 6, 8, LANES), F32),
             in_specs=[VMEM],
             out_specs=VMEM,
+            compiler_params=params(6),
+            cost_estimate=cost(2),
             name="plane_sum",
         )(parts)
         parts = trade(parts, lines)
         pieces = pl.pallas_call(
             probe_kernel,
-            out_shape=jax.ShapeDtypeStruct((members, 4, 8, LANES), F32),
+            out_shape=pltpu.HBM((members, 4, 8, LANES), F32),
             in_specs=[SMEM, VMEM, VMEM],
             out_specs=VMEM,
+            compiler_params=params(6),
+            cost_estimate=cost(2),
             name="probe_rows",
         )(piece, parts, probe)
         probe_new = pl.pallas_call(
@@ -425,40 +527,52 @@
             out_shape=jax.ShapeDtypeStruct(probe.shape, F32),
             in_specs=[VMEM],
             out_specs=VMEM,
+            compiler_params=params(6),
+            cost_estimate=cost(2),
             name="join",
         )(trade(pieces, planes))
 
         scale = pl.pallas_call(
             weight_kernel,
             out_shape=jax.ShapeDtypeStruct((tiles, side, LANES), F32),
-            in_specs=[VMEM] + [ANY] * 5,
+            in_specs=[SMEM, VMEM],
             out_specs=VMEM,
             scratch_shapes=[
                 pltpu.VMEM((2, size, LANES), F32),
                 pltpu.VMEM((tiles + 4, side + 2 * size, LANES), F32),
-                pltpu.SMEM((9, 8, LANES), F32),
-                pltpu.SemaphoreType.DMA((9,)),
             ],
-            compiler_params=params(16),
+            compiler_params=params(8),
+            cost_estimate=cost(8),
             name="weights",
-        )(probe, notes, low, high, top, bottom)
+        )(places, probe)
+        column = pl.BlockSpec((2, side, LANES), lambda index: (0, 0, index))
         object_new = pl.pallas_call(
-            final_kernel,
+            update_kernel,
             out_shape=jax.ShapeDtypeStruct(object_field.shape, F32),
             grid=(tiles,),
             in_specs=[
-                pl.BlockSpec((2, side, LANES), lambda index: (0, 0, index)),
-                pl.BlockSpec(tall, lambda index: (0, index, 0, 0)),
+                column,
+                pl.BlockSpec((2, 1, side, LANES), lambda index: (0, index, 0, 0)),
                 pl.BlockSpec(flat, lambda index: (0, index + 1, 0, 0)),
                 pl.BlockSpec(flat, lambda index: (0, index + 1, 0, 0)),
-                block((2, side, LANES), 0, 0, 0),
-                block((2, side, LANES), 0, 0, 0),
                 pl.BlockSpec((1, side, LANES), lambda index: (index, 0, 0)),
             ],
-            out_specs=pl.BlockSpec((2, side, LANES), lambda index: (0, 0, index)),
-            compiler_params=params(24),
-            name="final",
-        )(object_field, middle, above, below, from_low, from_high, scale)
+            out_specs=column,
+            compiler_params=params(8),
+            cost_estimate=cost(8),
+            name="update",
+        )(object_field, middle, above, below, scale)
+        ends = pl.BlockSpec((2, side, LANES), lambda index: (0, 0, index * (tiles - 1)))
+        object_new = pl.pallas_call(
+            edge_kernel,
+            out_shape=jax.ShapeDtypeStruct(object_field.shape, F32),
+            grid=(2,),
+            in_specs=[ends, whole, whole, pl.BlockSpec((1, side, LANES), lambda index: (index * (tiles - 1), 0, 0))],
+            out_specs=ends,
+            input_output_aliases={0: 0},
+            compiler_params=params(8),
+            name="edges",
+        )(object_new, from_low, from_high, scale)
         return (object_new, probe_new)
 
     in_specs = (

time: 161 us -> 147 us (0.913); the launches traced: 159 us -> 147 us
  waiting for transfers between devices: 53.8 us -> 40 us
  local copies, waits for them, and re-layouts: 10 us -> 5.87 us
  Pallas kernels: 23 us -> 26.7 us
  starting transfers between devices: 69.4 us -> 72.1 us
    ppermute x8, waiting for transfers between devices: 44.4 us -> 30.9 us  [both_ways(): return (lax.ppermute(high, axis, up), lax.ppermute(low, axis, down))]
    unnamed x42 -> x22, local copies, waits for them, and re-layouts: 8.52 us -> 4.36 us
    pallas_call x4 -> x6, Pallas kernels: 15.6 us -> 18.5 us  [the longest x1 4.37 us: per_device(): pl.pallas_call(outer_kernel, out_shape=(margin, margin, pltpu.HBM((2, sid...]
    ppermute x8, starting transfers between devices: 21.8 us -> 24.3 us  [both_ways(): return (lax.ppermute(high, axis, up), lax.ppermute(low, axis, down))]
  transfers between devices with their start and end apart: 11 -> 11, of which waited for: 7 -> 6; matrix products, arithmetic and copies ran while one was open for 0% -> 0% of each run, Pallas kernels for 8% -> 14%
where the time goes in v3:
time: 147 us
  starting transfers between devices  72.1 us (49%)
  waiting for transfers between devices  40 us (27%)
  Pallas kernels  26.7 us (18%)
  local copies, waits for them, and re-layouts  5.87 us (4%)
  between operations  1.55 us (1%)
    all_to_all x3, starting transfers between devices, trade(): lax.all_to_all(pieces, ('ty', 'tx'), 0, 0, axis_index_groups=groups, tile...  47.8 us
    ppermute x8, waiting for transfers between devices, both_ways(): return (lax.ppermute(high, axis, up), lax.ppermute(low, axis, down))  30.9 us
    ppermute x8, starting transfers between devices, both_ways(): return (lax.ppermute(high, axis, up), lax.ppermute(low, axis, down))  24.3 us
    all_to_all x3, waiting for transfers between devices, trade(): lax.all_to_all(pieces, ('ty', 'tx'), 0, 0, axis_index_groups=groups, tile...  9.06 us
    pallas_call x1, Pallas kernels, per_device(): pl.pallas_call(outer_kernel, out_shape=(margin, margin, pltpu.HBM((2, sid...  4.37 us
    unnamed x22, local copies, waits for them, and re-layouts  4.36 us
    pallas_call x1, Pallas kernels, per_device(): pl.pallas_call(inner_kernel, out_shape=(jax.ShapeDtypeStruct((2, tiles +...  4.22 us
    pallas_call x1, Pallas kernels, per_device(): pl.pallas_call(update_kernel, out_shape=jax.ShapeDtypeStruct(object_field...  3.82 us
  transfers between devices with their start and end apart: 11, of which 6 were waited for; matrix products, arithmetic and copies ran while one was open for 0% of the time, Pallas kernels for 14%

profile of v3, /device:TPU:1, one launch (start us, length us, event | category | flops | bytes accessed | tf_op | source)
XLA Modules:
  0.0 146.9 jit_solution(2410041680693393434)
XLA Ops:
  1.3 0.7 convert_element_type.7
  2.0 1.4 fusion
  3.4 0.1 scatter.9
  3.5 0.1 pad_maximum_fusion
  3.6 0.0 copy-start.5
  3.6 0.0 copy-start.8
  3.6 0.0 copy-start.9
  3.6 4.7 %collective-permute-start = (f32[2,520,128]{2,1,0:T(8,128)S(1)}, f32[2,520,128]{2,1,0:T(8,128)S(1)}, u32[]{:S(2)}, u32[]{:S(2)}) collective-permute-start(f32[2,520,128]{2,1,0:T(8,128)S(1)} %get-tuple-element.55), channel_id=1, source_target_pairs={{0,1},{1,2},{2,3},{3,4},{4,5},{5,6},{6,7},{7,8},{8,9},{9,10},{10,1... | collective-permute-start | bytes 1597448 | tf_op jit(solution)/shard_map/ppermute | solution.py:367
  8.3 1.3 collective-permute-start.1
  9.6 9.4 %collective-permute-done.low = f32[2,520,128]{2,1,0:T(8,128)S(1)} collective-permute-done((f32[2,520,128]{2,1,0:T(8,128)S(1)}, f32[2,520,128]{2,1,0:T(8,128)S(1)}, u32[]{:S(2)}, u32[]{:S(2)}) %collective-permute-start) | collective-permute-done | bytes 532512 | tf_op jit(solution)/shard_map/ppermute | solution.py:367
  19.0 15.9 %collective-permute-done.1.high = f32[2,520,128]{2,1,0:T(8,128)S(1)} collective-permute-done((f32[2,520,128]{2,1,0:T(8,128)S(1)}, f32[2,520,128]{2,1,0:T(8,128)S(1)}, u32[]{:S(2)}, u32[]{:S(2)}) %collective-permute-start.1) | collective-permute-done | bytes 532512 | tf_op jit(solution)/shard_map/ppermute | solution.py:367
  34.9 0.1 ends.1
  35.0 3.6 %collective-permute-start.2 = (f32[2,6,136,128]{3,2,1,0:T(8,128)S(1)}, f32[2,6,136,128]{3,2,1,0:T(8,128)S(1)}, u32[]{:S(2)}, u32[]{:S(2)}) collective-permute-start(f32[2,6,136,128]{3,2,1,0:T(8,128)S(1)} %get-tuple-element.39), channel_id=1, source_target_pairs={{0,16},{16,32},{32,48},{48,64},{64,80},{80,96},{96,112},{112,128},... | collective-permute-start | bytes 2506760 | tf_op jit(solution)/shard_map/ppermute | solution.py:367
  38.6 1.9 %collective-permute-start.3 = (f32[2,6,136,128]{3,2,1,0:T(8,128)S(1)}, f32[2,6,136,128]{3,2,1,0:T(8,128)S(1)}, u32[]{:S(2)}, u32[]{:S(2)}) collective-permute-start(f32[2,6,136,128]{3,2,1,0:T(8,128)S(1)} %get-tuple-element.40), channel_id=1, source_target_pairs={{16,0},{32,16},{48,32},{64,48},{80,64},{96,80},{112,96},{128,112},... | collective-permute-start | bytes 2506760 | tf_op jit(solution)/shard_map/ppermute | solution.py:367
  40.6 0.0 copy-start.1
  40.6 0.0 copy-start.2
  40.6 0.0 copy-start.3
  40.6 0.0 copy-start.10
  40.6 1.3 fold.1.folded
  42.0 0.2 copy-done.2
  42.2 0.5 copy-done.3
  42.6 4.2 %inner_slots.1 = (f32[2,6,512,128]{3,2,1,0:T(8,128)S(1)}, f32[3,2,256,128]{3,2,1,0:T(8,128)S(1)}) custom-call(s32[2,8]{1,0:T(2,128)S(1)} %bitcast.12, s32[1]{0:T(128)} %bitcast.8.count, f32[2,256,256]{2,1,0:T(8,128)S(1)} %copy-done.1, f32[8,256,256]{2,1,0:T(8,128)S(1)} %fold.1.folded, bf16[4,256,768]{2,1,0:T(8,128)(2,1)S(1)} %copy-done.2, ...), custom_call_target="tpu_custom_call" | custom-call | bytes 16777216 | tf_op jit(solution)/shard_map/inner_slots/pallas_call | solution.py:449
  46.9 1.2 collective-permute-done.2.top
  48.1 4.4 %collective-permute-done.3.bottom = f32[2,6,136,128]{3,2,1,0:T(8,128)S(1)} collective-permute-done((f32[2,6,136,128]{3,2,1,0:T(8,128)S(1)}, f32[2,6,136,128]{3,2,1,0:T(8,128)S(1)}, u32[]{:S(2)}, u32[]{:S(2)}) %collective-permute-start.3) | collective-permute-done | bytes 835616 | tf_op jit(solution)/shard_map/ppermute | solution.py:367
  52.5 4.4 %outer_slots.1 = (f32[2,6,128,128]{3,2,1,0:T(8,128)}, f32[2,6,128,128]{3,2,1,0:T(8,128)}, f32[2,512,128]{2,1,0:T(8,128)}, f32[2,512,128]{2,1,0:T(8,128)}, f32[2,...) custom-call(s32[2,8]{1,0:T(2,128)S(1)} %bitcast.13, s32[1]{0:T(128)} %bitcast.9.count, ...), custom_call_target="tpu_custom_call" | custom-call | bytes 16777216 | tf_op jit(solution)/shard_map/outer_slots/pallas_call | solution.py:462
  56.8 21.2 %all-to-all-start = ((f32[32,6,8,128]{3,2,1,0:T(8,128)}), f32[32,6,8,128]{3,2,1,0:T(8,128)}, u32[]{:S(2)}, u32[]{:S(2)}) async-start(f32[32,6,8,128]{3,2,1,0:T(8,128)} %get-tuple-element.51), calls=%async_computation | async-start | bytes 1572864 | tf_op jit(solution)/shard_map/all_to_all | solution.py:393
  78.0 3.5 %collective-permute-start.4 = (f32[2,6,128,128]{3,2,1,0:T(8,128)}, f32[2,6,128,128]{3,2,1,0:T(8,128)S(1)}, u32[]{:S(2)}, u32[]{:S(2)}) collective-permute-start(f32[2,6,128,128]{3,2,1,0:T(8,128)} %get-tuple-element.44), channel_id=1, source_target_pairs={{0,16},{16,32},{32,48},{48,64},{64,80},{80,96},{96,112},{112,128},... | collective-permute-start | bytes 2359304 | tf_op jit(solution)/shard_map/ppermute | solution.py:367
  81.6 1.9 %collective-permute-start.5 = (f32[2,6,128,128]{3,2,1,0:T(8,128)}, f32[2,6,128,128]{3,2,1,0:T(8,128)}, u32[]{:S(2)}, u32[]{:S(2)}) collective-permute-start(f32[2,6,128,128]{3,2,1,0:T(8,128)} %get-tuple-element.45), channel_id=1, source_target_pairs={{16,0},{32,16},{48,32},{64,48},{80,64},{96,80},{112,96},{128,112},... | collective-permute-start | bytes 2359304 | tf_op jit(solution)/shard_map/ppermute | solution.py:367
  83.5 8.2 %all-to-all-done.parts = f32[32,6,8,128]{3,2,1,0:T(8,128)} async-done(((f32[32,6,8,128]{3,2,1,0:T(8,128)}), f32[32,6,8,128]{3,2,1,0:T(8,128)}, u32[]{:S(2)}, u32[]{:S(2)}) %all-to-all-start) | async-done | bytes 786464 | tf_op jit(solution)/shard_map/all_to_all | solution.py:393
  91.7 1.9 %plane_sum.1 = f32[8,6,8,128]{3,2,1,0:T(8,128)} custom-call(f32[32,6,8,128]{3,2,1,0:T(8,128)} %all-to-all-done.parts), custom_call_target="tpu_custom_call" | custom-call | bytes 2097152 | tf_op jit(solution)/shard_map/plane_sum/pallas_call | solution.py:506
  93.6 10.5 %all-to-all-start.1 = ((f32[8,6,8,128]{3,2,1,0:T(8,128)}), f32[8,6,8,128]{3,2,1,0:T(8,128)}, u32[]{:S(2)}, u32[]{:S(2)}) async-start(f32[8,6,8,128]{3,2,1,0:T(8,128)} %plane_sum.1), calls=%async_computation.1 | async-start | bytes 393216 | tf_op jit(solution)/shard_map/all_to_all | solution.py:393
  104.1 0.0 collective-permute-done.4.above.above_first.above_last
  104.1 0.0 collective-permute-done.5.below.below_first.below_last
  104.1 0.0 copy-start.6
  104.1 1.0 copy-done.6
  105.1 1.0 copy-done.7
  106.2 2.0 %sides.1 = (f32[2,512,128]{2,1,0:T(8,128)}, f32[2,512,128]{2,1,0:T(8,128)}) custom-call(f32[2,512,128]{2,1,0:T(8,128)S(1)} %copy-done.6, f32[2,512,128]{2,1,0:T(8,128)S(1)} %copy-done.7, f32[2,6,128,128]{3,2,1,0:T(8,128)S(1)} %collective-permute-done.4.above.above_first.above_last, ...), custom_call_target="tpu_custom_call" | custom-call | bytes 16777216 | tf_op jit(solution)/shard_map/sides/pallas_call | solution.py:490
  108.2 6.1 %collective-permute-start.6 = (f32[2,512,128]{2,1,0:T(8,128)}, f32[2,512,128]{2,1,0:T(8,128)}, u32[]{:S(2)}, u32[]{:S(2)}) collective-permute-start(f32[2,512,128]{2,1,0:T(8,128)} %get-tuple-element.49), channel_id=1, source_target_pairs={{0,1},{1,2},{2,3},{3,4},{4,5},{5,6},{6,7},{7,8},{8,9},{9,10},{10,1... | collective-permute-start | bytes 1572872 | tf_op jit(solution)/shard_map/ppermute | solution.py:367
  114.3 1.3 collective-permute-start.7
  115.6 1.8 %probe_rows.1 = f32[32,4,8,128]{3,2,1,0:T(8,128)} custom-call(s32[1]{0:T(128)} %bitcast.5.index, f32[8,6,8,128]{3,2,1,0:T(8,128)} %all-to-all-done.1.parts, f32[2,256,256]{2,1,0:T(8,128)S(1)} %copy-done.1), custom_call_target="tpu_custom_call" | custom-call | bytes 2097152 | tf_op jit(solution)/shard_map/probe_rows/pallas_call | solution.py:516
  117.5 16.2 %all-to-all-start.2 = ((f32[32,4,8,128]{3,2,1,0:T(8,128)}), f32[32,4,8,128]{3,2,1,0:T(8,128)}, u32[]{:S(2)}, u32[]{:S(2)}) async-start(f32[32,4,8,128]{3,2,1,0:T(8,128)} %probe_rows.1), calls=%async_computation.2 | async-start | bytes 1048576 | tf_op jit(solution)/shard_map/all_to_all | solution.py:393
  133.6 2.8 %weights.1.scale = f32[4,512,128]{2,1,0:T(8,128)S(1)} custom-call(f32[9,8,128]{2,1,0:T(8,128)S(1)} %get-tuple-element.46.numbers, f32[2,256,256]{2,1,0:T(8,128)S(1)} %copy-done.1), custom_call_target="tpu_custom_call" | custom-call | bytes 8388608 | tf_op jit(solution)/shard_map/weights/pallas_call | solution.py:535
  136.4 0.0 copy-start.4
  136.4 1.6 %copy-done.4 = f32[2,4,512,128]{3,2,1,0:T(8,128)S(1)} copy-done((f32[2,4,512,128]{3,2,1,0:T(8,128)S(1)}, f32[2,4,512,128]{3,2,1,0:T(8,128)}, u32[]{:S(2)}) %copy-start.4) | copy-done | bytes 2097176
  138.0 3.8 %update.1.before = f32[2,512,512]{2,1,0:T(8,128)} custom-call(f32[2,512,512]{2,1,0:T(8,128)S(1)} %copy-done, f32[2,4,512,128]{3,2,1,0:T(8,128)S(1)} %copy-done.4, f32[2,6,128,128]{3,2,1,0:T(8,128)S(1)} %collective-permute-done.4.above.above_first.above_last, f32[2,6,128,128]{3,2,1,0:T(8,128)} %collective-permute-done.5.below.below_first.below_last, ...), custom_call_target="tpu_custom_call" | custom-call | bytes 8388608 | tf_op jit(solution)/shard_map/update/pallas_call | solution.py:549
  141.8 2.4 %edges.1 = f32[2,512,512]{2,1,0:T(8,128)} custom-call(f32[2,512,512]{2,1,0:T(8,128)} %update.1.before, f32[2,512,128]{2,1,0:T(8,128)} %collective-permute-done.6.low, f32[2,512,128]{2,1,0:T(8,128)} %collective-permute-done.7.high, f32[4,512,128]{2,1,0:T(8,128)S(1)} %weights.1.scale), custom_call_target="tpu_custom_call", output_to_operand_aliasing={{}: (0, {})} | custom-call | tf_op jit(solution)/shard_map/edges/pallas_call | solution.py:566
  144.2 0.8 all-to-all-done.2.pieces
  145.1 1.9 %join.1 = f32[2,256,256]{2,1,0:T(8,128)} custom-call(f32[32,4,8,128]{3,2,1,0:T(8,128)} %all-to-all-done.2.pieces), custom_call_target="tpu_custom_call" | custom-call | bytes 2097152 | tf_op jit(solution)/shard_map/join/pallas_call | solution.py:525
  (13 shorter events, 0.0 us)
Async XLA Ops:
  2.0 33.0 %copy-start = (f32[2,512,512]{2,1,0:T(8,128)S(1)}, f32[2,512,512]{2,1,0:T(8,128)}, u32[]{:S(2)}) copy-start(f32[2,512,512]{2,1,0:T(8,128)} %tile_ref.7) | copy-start | bytes 6291460
  3.6 37.0 %copy-start.5 = (f32[1,1,8,256,256]{4,3,2,1,0:T(8,128)S(1)}, f32[1,1,8,256,256]{4,3,2,1,0:T(8,128)}, u32[]{:S(2)}) copy-start(f32[1,1,8,256,256]{4,3,2,1,0:T(8,128)} %param.15) | copy-start | bytes 6291460
  3.6 37.0 %copy-start.8 = (bf16[256,768]{1,0:T(8,128)(2,1)S(1)}, bf16[256,768]{1,0:T(8,128)(2,1)}, u32[]{:S(2)}) copy-start(bf16[256,768]{1,0:T(8,128)(2,1)} %constant.81.clone.gather_left) | copy-start | bytes 1179652
  3.6 37.0 %copy-start.9 = (bf16[768,256]{1,0:T(8,128)(2,1)S(1)}, bf16[768,256]{1,0:T(8,128)(2,1)}, u32[]{:S(2)}) copy-start(bf16[768,256]{1,0:T(8,128)(2,1)} %constant.82.clone.gather_right) | copy-start | bytes 1179652
  3.6 15.4 %collective-permute-start = (f32[2,520,128]{2,1,0:T(8,128)S(1)}, f32[2,520,128]{2,1,0:T(8,128)S(1)}, u32[]{:S(2)}, u32[]{:S(2)}) collective-permute-start(f32[2,520,128]{2,1,0:T(8,128)S(1)} %get-tuple-element.55), channel_id=1, source_target_pairs={{0,1},{1,2},{2,3},{3,4},{4,5},{5,6},{6,7},{7,8},{8,9},{9,10},{10,1... | collective-permute-start | bytes 1597448 | tf_op jit(solution)/shard_map/ppermute | solution.py:367
  8.3 26.6 %collective-permute-start.1 = (f32[2,520,128]{2,1,0:T(8,128)S(1)}, f32[2,520,128]{2,1,0:T(8,128)S(1)}, u32[]{:S(2)}, u32[]{:S(2)}) collective-permute-start(f32[2,520,128]{2,1,0:T(8,128)S(1)} %get-tuple-element.54), channel_id=1, source_target_pairs={{1,0},{2,1},{3,2},{4,3},{5,4},{6,5},{7,6},{8,7},{9,8},{10,9},{11,1... | collective-permute-start | bytes 1597448 | tf_op jit(solution)/shard_map/ppermute | solution.py:367
  35.0 13.0 %collective-permute-start.2 = (f32[2,6,136,128]{3,2,1,0:T(8,128)S(1)}, f32[2,6,136,128]{3,2,1,0:T(8,128)S(1)}, u32[]{:S(2)}, u32[]{:S(2)}) collective-permute-start(f32[2,6,136,128]{3,2,1,0:T(8,128)S(1)} %get-tuple-element.39), channel_id=1, source_target_pairs={{0,16},{16,32},{32,48},{48,64},{64,80},{80,96},{96,112},{112,128},... | collective-permute-start | bytes 2506760 | tf_op jit(solution)/shard_map/ppermute | solution.py:367
  38.6 13.8 %collective-permute-start.3 = (f32[2,6,136,128]{3,2,1,0:T(8,128)S(1)}, f32[2,6,136,128]{3,2,1,0:T(8,128)S(1)}, u32[]{:S(2)}, u32[]{:S(2)}) collective-permute-start(f32[2,6,136,128]{3,2,1,0:T(8,128)S(1)} %get-tuple-element.40), channel_id=1, source_target_pairs={{16,0},{32,16},{48,32},{64,48},{80,64},{96,80},{112,96},{128,112},... | collective-permute-start | bytes 2506760 | tf_op jit(solution)/shard_map/ppermute | solution.py:367
  40.6 1.4 copy-start.1
  40.6 1.6 %copy-start.2 = (bf16[4,256,768]{2,1,0:T(8,128)(2,1)S(1)}, bf16[4,256,768]{2,1,0:T(8,128)(2,1)}, u32[]{:S(2)}) copy-start(bf16[4,256,768]{2,1,0:T(8,128)(2,1)} %constant.79.clone.left) | copy-start | bytes 4718596
  40.6 2.0 %copy-start.3 = (bf16[4,768,256]{2,1,0:T(8,128)(2,1)S(1)}, bf16[4,768,256]{2,1,0:T(8,128)(2,1)}, u32[]{:S(2)}) copy-start(bf16[4,768,256]{2,1,0:T(8,128)(2,1)} %constant.80.clone.right) | copy-start | bytes 4718596
  40.6 2.0 %copy-start.10 = (s32[2,1,1,8]{3,2,1,0:T(1,128)S(1)}, s32[2,1,1,8]{3,2,1,0:T(1,128)}, u32[]{:S(2)}) copy-start(s32[2,1,1,8]{3,2,1,0:T(1,128)} %param.16) | copy-start | bytes 196
  56.8 34.9 %all-to-all-start = ((f32[32,6,8,128]{3,2,1,0:T(8,128)}), f32[32,6,8,128]{3,2,1,0:T(8,128)}, u32[]{:S(2)}, u32[]{:S(2)}) async-start(f32[32,6,8,128]{3,2,1,0:T(8,128)} %get-tuple-element.51), calls=%async_computation | async-start | bytes 1572864 | tf_op jit(solution)/shard_map/all_to_all | solution.py:393
  78.0 26.1 %collective-permute-start.4 = (f32[2,6,128,128]{3,2,1,0:T(8,128)}, f32[2,6,128,128]{3,2,1,0:T(8,128)S(1)}, u32[]{:S(2)}, u32[]{:S(2)}) collective-permute-start(f32[2,6,128,128]{3,2,1,0:T(8,128)} %get-tuple-element.44), channel_id=1, source_target_pairs={{0,16},{16,32},{32,48},{48,64},{64,80},{80,96},{96,112},{112,128},... | collective-permute-start | bytes 2359304 | tf_op jit(solution)/shard_map/ppermute | solution.py:367
  81.6 22.5 %collective-permute-start.5 = (f32[2,6,128,128]{3,2,1,0:T(8,128)}, f32[2,6,128,128]{3,2,1,0:T(8,128)}, u32[]{:S(2)}, u32[]{:S(2)}) collective-permute-start(f32[2,6,128,128]{3,2,1,0:T(8,128)} %get-tuple-element.45), channel_id=1, source_target_pairs={{16,0},{32,16},{48,32},{64,48},{80,64},{96,80},{112,96},{128,112},... | collective-permute-start | bytes 2359304 | tf_op jit(solution)/shard_map/ppermute | solution.py:367
  93.6 22.0 %all-to-all-start.1 = ((f32[8,6,8,128]{3,2,1,0:T(8,128)}), f32[8,6,8,128]{3,2,1,0:T(8,128)}, u32[]{:S(2)}, u32[]{:S(2)}) async-start(f32[8,6,8,128]{3,2,1,0:T(8,128)} %plane_sum.1), calls=%async_computation.1 | async-start | bytes 393216 | tf_op jit(solution)/shard_map/all_to_all | solution.py:393
  104.1 1.0 copy-start.6
  105.1 1.0 copy-start.7
  108.2 33.6 %collective-permute-start.6 = (f32[2,512,128]{2,1,0:T(8,128)}, f32[2,512,128]{2,1,0:T(8,128)}, u32[]{:S(2)}, u32[]{:S(2)}) collective-permute-start(f32[2,512,128]{2,1,0:T(8,128)} %get-tuple-element.49), channel_id=1, source_target_pairs={{0,1},{1,2},{2,3},{3,4},{4,5},{5,6},{6,7},{7,8},{8,9},{9,10},{10,1... | collective-permute-start | bytes 1572872 | tf_op jit(solution)/shard_map/ppermute | solution.py:367
  114.3 27.5 %collective-permute-start.7 = (f32[2,512,128]{2,1,0:T(8,128)}, f32[2,512,128]{2,1,0:T(8,128)}, u32[]{:S(2)}, u32[]{:S(2)}) collective-permute-start(f32[2,512,128]{2,1,0:T(8,128)} %get-tuple-element.50), channel_id=1, source_target_pairs={{1,0},{2,1},{3,2},{4,3},{5,4},{6,5},{7,6},{8,7},{9,8},{10,9},{11,1... | collective-permute-start | bytes 1572872 | tf_op jit(solution)/shard_map/ppermute | solution.py:367
  117.5 27.6 %all-to-all-start.2 = ((f32[32,4,8,128]{3,2,1,0:T(8,128)}), f32[32,4,8,128]{3,2,1,0:T(8,128)}, u32[]{:S(2)}, u32[]{:S(2)}) async-start(f32[32,4,8,128]{3,2,1,0:T(8,128)} %probe_rows.1), calls=%async_computation.2 | async-start | bytes 1048576 | tf_op jit(solution)/shard_map/all_to_all | solution.py:393
  136.4 1.6 %copy-start.4 = (f32[2,4,512,128]{3,2,1,0:T(8,128)S(1)}, f32[2,4,512,128]{3,2,1,0:T(8,128)}, u32[]{:S(2)}) copy-start(f32[2,4,512,128]{3,2,1,0:T(8,128)} %get-tuple-element.43.grad) | copy-start | bytes 6291460

commit v4 on v3

--- a/solution.py
+++ b/solution.py
@@ -103,19 +103,45 @@
     lax.fori_loop(0, count[0], step, 0)
 
 
-def ends_kernel(tile_ref, low, high, notes, top, bottom):
+def own_notes(position, count):
+    row = lax.broadcasted_iota(jnp.int32, (8, LANES), 0)
+    lane = lax.broadcasted_iota(jnp.int32, (8, LANES), 1)
+    notes = jnp.where(row == 2, count[0], 0)
+    for slot in range(position.shape[1]):
+        for axis in range(2):
+            notes = jnp.where((row == axis) & (lane == slot), position[axis, slot], notes)
+    return notes.astype(F32)
+
+
+def edge_kernel(odd, position, count, tile_ref, x_first, x_second, y_first, y_second):
     half = LANES
     side = tile_ref.shape[1]
-    tiles = side // LANES
-    for out, start in ((top, 0), (bottom, side - half)):
-        rows = slice(start, start + half)
-        for index in range(tiles):
-            out[:, 1 + index, :half, :] = tile_ref[:, rows, index * LANES : (index + 1) * LANES]
-        for index, strip in ((0, low), (1 + tiles, high)):
-            out[:, index, :half, :] = strip[:, rows, :]
-            out[:, index, half:, :] = strip[:, side:, :]
-        out[:, 1, half:, :] = notes[...]
-        out[:, 2 : 1 + tiles, half:, :] = jnp.zeros((2, tiles - 1, 8, LANES), F32)
+    odd_y, odd_x = odd[0] == 1, odd[1] == 1
+    notes = own_notes(position, count)
+    low, high = tile_ref[:, :, :half], tile_ref[:, :, side - half :]
+    x_first[:, :side, :] = jnp.where(odd_x, high, low)
+    x_second[:, :side, :] = jnp.where(odd_x, low, high)
+    for out in (x_first, x_second):
+        for plane in range(2):
+            out[plane, side:, :] = notes
+    low, high = tile_ref[:, :half, :], tile_ref[:, side - half :, :]
+    y_first[...] = jnp.where(odd_y, high, low)
+    y_second[...] = jnp.where(odd_y, low, high)
+
+
+def corner_kernel(odd, position, count, x_first, x_second, first, second):
+    half = LANES
+    side = x_first.shape[1] - 8
+    far = side - half
+    odd_x = odd[1] == 1
+    notes = own_notes(position, count)
+    for out, odd_start in ((first, far), (second, 0)):
+        rows = pl.ds(pl.multiple_of(jnp.where(odd[0] == 1, odd_start, far - odd_start), LANES), half)
+        for index, (even_ref, odd_ref) in enumerate(((x_first, x_second), (x_second, x_first))):
+            out[:, index, :half, :] = jnp.where(odd_x, odd_ref[:, rows, :], even_ref[:, rows, :])
+            out[:, index, half : half + 8, :] = jnp.where(odd_x, odd_ref[:, side:, :], even_ref[:, side:, :])
+            for plane in range(2):
+                out[plane, index, half + 8 :, :] = notes
 
 
 def slot_stages(row, tile, offset, live, probe, measured, left, right, canvas, grad, probe_sum, patch, rhs, lhs):
@@ -222,72 +248,90 @@
     lax.fori_loop(0, lax.div(total + (lanes - 1), lanes), step, 0)
 
 
-def inner_kernel(position, count, probe, folded, left, right, tile_ref, low, high, grad, probe_sum, canvas, *scratch):
+def inner_kernel(odd, position, count, probe, folded, left, right, tile_ref, x_first, x_second, grad, probe_sum, canvas, *scratch):
     side = tile_ref.shape[1]
     tiles = side // LANES
+    odd_x = odd[1] == 1
     for index in range(tiles):
         canvas[:, 1 + index] = tile_ref[:, :, index * LANES : (index + 1) * LANES]
-    canvas[:, 0] = low[:, :side, :]
-    canvas[:, 1 + tiles] = high[:, :side, :]
+    canvas[:, 0] = jnp.where(odd_x, x_second[:, :side, :], x_first[:, :side, :])
+    canvas[:, 1 + tiles] = jnp.where(odd_x, x_first[:, :side, :], x_second[:, :side, :])
     grad[...] = jnp.zeros_like(grad)
     probe_sum[...] = jnp.zeros_like(probe_sum)
     run_slots(True, 0, position, count, probe, folded, left, right, canvas, grad, probe_sum, *scratch)
 
 
 def outer_kernel(
-    position, count, probe, folded, left, right, tile_ref, low, high, top, bottom, own_notes, grad_in, probe_sum_in,
-    margin_top, margin_bottom, side_low, side_high, middle, sums, places, canvas, grad, probe_sum, sems, *scratch,
+    odd, position, count, probe, folded, left, right, tile_ref, x_first, x_second, y_first, y_second,
+    corner_first, corner_second, grad_in, probe_sum_in,
+    margin_first, margin_second, side_low, side_high, middle, sums, places,
+    canvas, grad, probe_sum, sems, *scratch,
 ):
     size = probe.shape[1]
     half = size // 2
     side = tile_ref.shape[1]
     tiles = side // LANES
     inner = slice(half, half + side)
+    odd_y, odd_x = odd[0] == 1, odd[1] == 1
     for index in range(tiles):
-        canvas[:, 1 + index, inner, :] = tile_ref[:, :, index * LANES : (index + 1) * LANES]
-    canvas[:, 0, inner, :] = low[:, :side, :]
-    canvas[:, 1 + tiles, inner, :] = high[:, :side, :]
-    canvas[:, :, :half, :] = top[:, :, :half, :]
-    canvas[:, :, half + side :, :] = bottom[:, :, :half, :]
-    grad[:, :, :half, :] = jnp.zeros(margin_top.shape, F32)
-    grad[:, :, half + side :, :] = jnp.zeros(margin_bottom.shape, F32)
+        columns = slice(index * LANES, (index + 1) * LANES)
+        canvas[:, 1 + index, inner, :] = tile_ref[:, :, columns]
+        canvas[:, 1 + index, :half, :] = jnp.where(odd_y, y_second[:, :, columns], y_first[:, :, columns])
+        canvas[:, 1 + index, half + side :, :] = jnp.where(odd_y, y_first[:, :, columns], y_second[:, :, columns])
+    canvas[:, 0, inner, :] = jnp.where(odd_x, x_second[:, :side, :], x_first[:, :side, :])
+    canvas[:, 1 + tiles, inner, :] = jnp.where(odd_x, x_first[:, :side, :], x_second[:, :side, :])
+    for index, tile in enumerate((0, 1 + tiles)):
+        above, below = corner_first[:, index, :half, :], corner_second[:, index, :half, :]
+        canvas[:, tile, :half, :] = jnp.where(odd_y, below, above)
+        canvas[:, tile, half + side :, :] = jnp.where(odd_y, above, below)
+    grad[:, :, :half, :] = jnp.zeros((2, tiles + 2, half, LANES), F32)
+    grad[:, :, half + side :, :] = jnp.zeros((2, tiles + 2, half, LANES), F32)
     grad[:, :, inner, :] = grad_in[...]
     probe_sum[...] = probe_sum_in[...]
     run_slots(False, half, position, count, probe, folded, left, right, canvas, grad, probe_sum, *scratch)
-    ends = slice(half, half + 8)
-    notes = (
-        top[0, 0, ends], top[0, 1, ends], top[0, 1 + tiles, ends],
-        low[0, side:], own_notes[0], high[0, side:],
-        bottom[0, 0, ends], bottom[0, 1, ends], bottom[0, 1 + tiles, ends],
-    )
-    for index, value in enumerate(notes):
-        places[index] = value
-    copies = [
-        pltpu.make_async_copy(source, target, sems.at[index])
-        for index, (source, target) in enumerate((
-            (grad.at[:, :, :half, :], margin_top),
-            (grad.at[:, :, half + side :, :], margin_bottom),
-            (grad.at[:, 0, inner, :], side_low),
-            (grad.at[:, 1 + tiles, inner, :], side_high),
-            (grad.at[:, 1 : 1 + tiles, inner, :], middle),
-        ))
-    ]
-    for copy in copies:
+    copies = []
+
+    def send(source, target):
+        copy = pltpu.make_async_copy(source, target, sems.at[len(copies)])
         copy.start()
+        copies.append(copy)
+
+    for out, odd_start in ((margin_first, half + side), (margin_second, 0)):
+        rows = pl.ds(pl.multiple_of(jnp.where(odd_y, odd_start, half + side - odd_start), LANES), half)
+        send(grad.at[:, :, rows, :], out)
+    send(grad.at[:, 0, inner, :], side_low)
+    send(grad.at[:, 1 + tiles, inner, :], side_high)
+    send(grad.at[:, 1 : 1 + tiles, inner, :], middle)
     for plane in range(3):
         for index in range(2):
             sums[:, 2 * plane + index] = probe_sum[plane, index].reshape(size // 8, 8, LANES)
+    beside, own = slice(half, half + 8), slice(half + 8, half + 16)
+    for start, (even_ref, odd_ref) in ((0, (corner_first, corner_second)), (6, (corner_second, corner_first))):
+        for index, (tile, rows) in enumerate(((0, beside), (0, own), (1, beside))):
+            places[start + index] = jnp.where(odd_y, odd_ref[0, tile, rows, :], even_ref[0, tile, rows, :])
+    places[3] = jnp.where(odd_x, x_second[0, side:, :], x_first[0, side:, :])
+    places[4] = own_notes(position, count)
+    places[5] = jnp.where(odd_x, x_first[0, side:, :], x_second[0, side:, :])
     for copy in copies:
         copy.wait()
 
 
-def sides_kernel(first, last, above_first, above_last, below_first, below_last, low, high):
+def sides_kernel(odd, own_low, own_high, low_first, low_second, high_first, high_second, first, second):
     half = LANES
-    side = first.shape[1]
-    for out, own, above, below in ((low, first, above_first, below_first), (high, last, above_last, below_last)):
-        out[...] = own[...]
-        out[:, :half, :] += above[:, 0]
-        out[:, side - half :, :] += below[:, 0]
+    side = own_low.shape[1]
+    odd_y, odd_x = odd[0] == 1, odd[1] == 1
+    for start in range(0, side, half):
+        rows = slice(start, start + half)
+        values = []
+        for own, y_first, y_second in ((own_low, low_first, low_second), (own_high, high_first, high_second)):
+            value = own[:, rows, :]
+            if start == 0:
+                value = value + jnp.where(odd_y, y_second[:, 0], y_first[:, 0])
+            if start + half == side:
+                value = value + jnp.where(odd_y, y_first[:, 0], y_second[:, 0])
+            values.append(value)
+        first[:, rows, :] = jnp.where(odd_x, values[1], values[0])
+        second[:, rows, :] = jnp.where(odd_x, values[0], values[1])
 
 
 def weight_kernel(numbers, probe, scale, power, weight):
@@ -318,28 +362,28 @@
         scale[index] = 1.0 / (weight[2 + index, 2 * half : 2 * half + side, :] + 1.0)
 
 
-def update_kernel(tile_ref, grad, above, below, scale, out):
+def update_kernel(odd, tile_ref, grad, y_first, y_second, scale, out):
     half = LANES
     side = tile_ref.shape[1]
+    odd_y = odd[0] == 1
     for plane in range(2):
         for start in range(0, side, half):
             rows = slice(start, start + half)
             value = grad[plane, 0, rows, :]
             if start == 0:
-                value = value + above[plane, 0]
+                value = value + jnp.where(odd_y, y_second[plane, 0], y_first[plane, 0])
             if start + half == side:
-                value = value + below[plane, 0]
+                value = value + jnp.where(odd_y, y_first[plane, 0], y_second[plane, 0])
             out[plane, rows, :] = tile_ref[plane, rows, :] - value * scale[0, rows, :]
 
 
-def edge_kernel(before, low, high, scale, out):
-    is_low = (pl.program_id(0) == 0).astype(F32)
-    is_high = 1.0 - is_low
+def column_kernel(odd, before, x_first, x_second, scale, out):
+    use_first = odd[1] == pl.program_id(0)
     for plane in range(2):
-        out[plane] = before[plane] - (low[plane] * is_low + high[plane] * is_high) * scale[0]
-
-
-def plane_kernel(parts, out):
+        out[plane] = before[plane] - jnp.where(use_first, x_first[plane], x_second[plane]) * scale[0]
+
+
+def plane_kernel(parts, after, out):
     out[...] = jnp.broadcast_to(jnp.sum(parts[...], axis=0)[None], out.shape)
 
 
@@ -360,15 +404,10 @@
             out[plane, :, tile * LANES : (tile + 1) * LANES] = value.reshape(out.shape[1], LANES)
 
 
-def both_ways(low, high, axis):
+def swap(first, second, axis):
     count = lax.axis_size(axis)
-    up = [(index, index + 1) for index in range(count - 1)]
-    down = [(index + 1, index) for index in range(count - 1)]
-    return lax.ppermute(high, axis, up), lax.ppermute(low, axis, down)
-
-
-def block(shape, *where):
-    return pl.BlockSpec(shape, lambda *_: where)
+    across = [pair for low in range(1, count - 1, 2) for pair in ((low, low + 1), (low + 1, low))]
+    return lax.ppermute(first, axis, across), lax.ppermute(second, axis, [(index, index ^ 1) for index in range(count)])
 
 
 def params(mib):
@@ -406,14 +445,21 @@
         left, right = (jnp.asarray(table) for table in half_tables(size))
         gather_left, gather_right = (jnp.asarray(table) for table in parity_tables(size))
 
-        notes = jnp.zeros((8, LANES), F32).at[:2, :slots].set(position.astype(F32))
-        notes = notes.at[2, 0].set(counts[0, 0].astype(F32))
-        notes = jnp.stack([notes, jnp.zeros_like(notes)])
-        low, high = both_ways(
-            jnp.concatenate([object_field[:, :, :half], notes], axis=1),
-            jnp.concatenate([object_field[:, :, side - half :], notes], axis=1),
-            "tx",
-        )
+        odd = jnp.bitwise_and(jnp.stack([row, col]), 1).astype(jnp.int32)
+
+        strip = jax.ShapeDtypeStruct((2, side + 8, LANES), F32)
+        edge = jax.ShapeDtypeStruct((2, half, side), F32)
+        x_first, x_second, y_first, y_second = pl.pallas_call(
+            edge_kernel,
+            out_shape=(strip, strip, edge, edge),
+            in_specs=[SMEM] * 3 + [VMEM],
+            out_specs=(VMEM,) * 4,
+            compiler_params=params(6),
+            cost_estimate=cost(4),
+            name="edges",
+        )(odd, position, count, object_field)
+        x_first, x_second = swap(x_first, x_second, "tx")
+        y_first, y_second = swap(y_first, y_second, "ty")
         folded = pl.pallas_call(
             fold_kernel,
             out_shape=jax.ShapeDtypeStruct((slots, size, size), F32),
@@ -424,20 +470,18 @@
             cost_estimate=cost(6),
             name="fold",
         )(count, intensity[0, 0], gather_left, gather_right)
-        end = jax.ShapeDtypeStruct((2, tiles + 2, half + 8, LANES), F32)
-        first_rows, last_rows = pl.pallas_call(
-            ends_kernel,
-            out_shape=(end, end),
-            in_specs=[VMEM] * 4,
+        corner = jax.ShapeDtypeStruct((2, 2, half + 16, LANES), F32)
+        corners = pl.pallas_call(
+            corner_kernel,
+            out_shape=(corner, corner),
+            in_specs=[SMEM] * 3 + [VMEM] * 2,
             out_specs=(VMEM, VMEM),
-            compiler_params=params(8),
+            compiler_params=params(4),
             cost_estimate=cost(4),
-            name="ends",
-        )(object_field, low, high, notes)
-        top, bottom = both_ways(first_rows, last_rows, "ty")
-
-        margin = pltpu.HBM((2, tiles + 2, half, LANES), F32)
-        strip = jax.ShapeDtypeStruct((2, side, LANES), F32)
+            name="corners",
+        )(odd, position, count, x_first, x_second)
+        corners = swap(*corners, "ty")
+
         members = len(planes[0])
         lanes = 2
         scratch = [
@@ -452,24 +496,24 @@
                 jax.ShapeDtypeStruct((2, tiles + 2, side, LANES), F32),
                 jax.ShapeDtypeStruct((3, 2, size, LANES), F32),
             ),
-            in_specs=[SMEM] * 2 + [VMEM] * 7,
+            in_specs=[SMEM] * 3 + [VMEM] * 7,
             out_specs=(VMEM,) * 2,
             scratch_shapes=[pltpu.VMEM((2, tiles + 2, side, LANES), F32)] + scratch,
             compiler_params=params(22),
             cost_estimate=cost(16),
             name="inner_slots",
-        )(position, count, probe, folded, left, right, object_field, low, high)
-        margin_top, margin_bottom, side_low, side_high, middle, sums, places = pl.pallas_call(
+        )(odd, position, count, probe, folded, left, right, object_field, x_first, x_second)
+        margin = pltpu.HBM((2, tiles + 2, half, LANES), F32)
+        column = pltpu.HBM((2, side, LANES), F32)
+        margin_first, margin_second, side_low, side_high, middle, sums, places = pl.pallas_call(
             outer_kernel,
             out_shape=(
-                margin, margin,
-                pltpu.HBM((2, side, LANES), F32),
-                pltpu.HBM((2, side, LANES), F32),
+                margin, margin, column, column,
                 pltpu.HBM((2, tiles, side, LANES), F32),
                 pltpu.HBM((members, 6, 8, LANES), F32),
                 jax.ShapeDtypeStruct((9, 8, LANES), F32),
             ),
-            in_specs=[SMEM] * 2 + [VMEM] * 12,
+            in_specs=[SMEM] * 3 + [VMEM] * 13,
             out_specs=(HBM,) * 5 + (VMEM, VMEM),
             scratch_shapes=[
                 pltpu.VMEM((2, tiles + 2, side + size, LANES), F32),
@@ -480,38 +524,51 @@
             compiler_params=params(30),
             cost_estimate=cost(16),
             name="outer_slots",
-        )(position, count, probe, folded, left, right, object_field, low, high, top, bottom, notes, grad, probe_sum)
-
-        above, below = both_ways(margin_top, margin_bottom, "ty")
+        )(
+            odd, position, count, probe, folded, left, right, object_field, x_first, x_second, y_first, y_second,
+            *corners, grad, probe_sum,
+        )
+
+        margin_first, margin_second = swap(margin_first, margin_second, "ty")
+        scale = pl.pallas_call(
+            weight_kernel,
+            out_shape=jax.ShapeDtypeStruct((tiles, side, LANES), F32),
+            in_specs=[SMEM, VMEM],
+            out_specs=VMEM,
+            scratch_shapes=[
+                pltpu.VMEM((2, size, LANES), F32),
+                pltpu.VMEM((tiles + 4, side + 2 * size, LANES), F32),
+            ],
+            compiler_params=params(8),
+            cost_estimate=cost(8),
+            name="weights",
+        )(places, probe)
         parts = trade(sums, planes)
-        flat = (2, 1, half, LANES)
-        whole = block((2, side, LANES), 0, 0, 0)
-
-        margin_low, margin_high = pl.pallas_call(
+        strip = jax.ShapeDtypeStruct((2, side, LANES), F32)
+        whole = pl.BlockSpec((2, side, LANES), lambda index: (0, 0, 0))
+        first_tile = pl.BlockSpec((2, 1, half, LANES), lambda index: (0, 0, 0, 0))
+        last_tile = pl.BlockSpec((2, 1, half, LANES), lambda index: (0, tiles + 1, 0, 0))
+        x_first, x_second = pl.pallas_call(
             sides_kernel,
             out_shape=(strip, strip),
             grid=(1,),
-            in_specs=[
-                whole, whole,
-                block(flat, 0, 0, 0, 0), block(flat, 0, tiles + 1, 0, 0),
-                block(flat, 0, 0, 0, 0), block(flat, 0, tiles + 1, 0, 0),
-            ],
+            in_specs=[SMEM, whole, whole, first_tile, first_tile, last_tile, last_tile],
             out_specs=(whole, whole),
             compiler_params=params(8),
             cost_estimate=cost(16),
             name="sides",
-        )(side_low, side_high, above, above, below, below)
-        from_low, from_high = both_ways(margin_low, margin_high, "tx")
+        )(odd, side_low, side_high, margin_first, margin_second, margin_first, margin_second)
+        x_first, x_second = swap(x_first, x_second, "tx")
 
         parts = pl.pallas_call(
             plane_kernel,
             out_shape=pltpu.HBM((len(lines[0]), 6, 8, LANES), F32),
-            in_specs=[VMEM],
+            in_specs=[VMEM, HBM],
             out_specs=VMEM,
             compiler_params=params(6),
             cost_estimate=cost(2),
             name="plane_sum",
-        )(parts)
+        )(parts, scale)
         parts = trade(parts, lines)
         pieces = pl.pallas_call(
             probe_kernel,
@@ -532,47 +589,32 @@
             name="join",
         )(trade(pieces, planes))
 
-        scale = pl.pallas_call(
-            weight_kernel,
-            out_shape=jax.ShapeDtypeStruct((tiles, side, LANES), F32),
-            in_specs=[SMEM, VMEM],
-            out_specs=VMEM,
-            scratch_shapes=[
-                pltpu.VMEM((2, size, LANES), F32),
-                pltpu.VMEM((tiles + 4, side + 2 * size, LANES), F32),
-            ],
-            compiler_params=params(8),
-            cost_estimate=cost(8),
-            name="weights",
-        )(places, probe)
         column = pl.BlockSpec((2, side, LANES), lambda index: (0, 0, index))
+        flat = pl.BlockSpec((2, 1, half, LANES), lambda index: (0, index + 1, 0, 0))
         object_new = pl.pallas_call(
             update_kernel,
             out_shape=jax.ShapeDtypeStruct(object_field.shape, F32),
             grid=(tiles,),
             in_specs=[
-                column,
-                pl.BlockSpec((2, 1, side, LANES), lambda index: (0, index, 0, 0)),
-                pl.BlockSpec(flat, lambda index: (0, index + 1, 0, 0)),
-                pl.BlockSpec(flat, lambda index: (0, index + 1, 0, 0)),
+                SMEM, column, pl.BlockSpec((2, 1, side, LANES), lambda index: (0, index, 0, 0)), flat, flat,
                 pl.BlockSpec((1, side, LANES), lambda index: (index, 0, 0)),
             ],
             out_specs=column,
             compiler_params=params(8),
             cost_estimate=cost(8),
             name="update",
-        )(object_field, middle, above, below, scale)
+        )(odd, object_field, middle, margin_first, margin_second, scale)
         ends = pl.BlockSpec((2, side, LANES), lambda index: (0, 0, index * (tiles - 1)))
         object_new = pl.pallas_call(
-            edge_kernel,
+            column_kernel,
             out_shape=jax.ShapeDtypeStruct(object_field.shape, F32),
             grid=(2,),
-            in_specs=[ends, whole, whole, pl.BlockSpec((1, side, LANES), lambda index: (index * (tiles - 1), 0, 0))],
+            in_specs=[SMEM, ends, whole, whole, pl.BlockSpec((1, side, LANES), lambda index: (index * (tiles - 1), 0, 0))],
             out_specs=ends,
-            input_output_aliases={0: 0},
+            input_output_aliases={1: 0},
             compiler_params=params(8),
-            name="edges",
-        )(object_new, from_low, from_high, scale)
+            name="columns",
+        )(odd, object_new, x_first, x_second, scale)
         return (object_new, probe_new)
 
     in_specs = (

time: 147 us -> 137 us (0.932)
  waiting for transfers between devices: 40 us -> 32.5 us
  starting transfers between devices: 72.1 us -> 65.9 us
  local copies, waits for them, and re-layouts: 5.87 us -> 10.8 us
    ppermute x8 -> x10, waiting for transfers between devices: 30.9 us -> 18.6 us  [the longest x5 18.6 us: swap(): lax.ppermute(second, axis, [(index, index ^ 1) for index in range(count)])]
    unnamed x22 -> x30, local copies, waits for them, and re-layouts: 4.36 us -> 10.8 us
    all_to_all x3, starting transfers between devices: 47.8 us -> 42.4 us  [trade(): lax.all_to_all(pieces, ('ty', 'tx'), 0, 0, axis_index_groups=groups, tile...]
    all_to_all x3, waiting for transfers between devices: 9.06 us -> 13.9 us  [trade(): lax.all_to_all(pieces, ('ty', 'tx'), 0, 0, axis_index_groups=groups, tile...]
    pallas_call x3 -> x4, Pallas kernels: 6.93 us -> 8.33 us  [the longest x1 4.55 us: per_device(): pl.pallas_call(outer_kernel, out_shape=(margin, margin, column, column, p...]
    ppermute x8 -> x10, starting transfers between devices: 24.3 us -> 23.5 us  [the longest x5 14.6 us: swap(): lax.ppermute(first, axis, across)]
  transfers between devices with their start and end apart: 11 -> 13, of which waited for: 6 -> 4; matrix products, arithmetic and copies ran while one was open for 0% -> 0% of each run, Pallas kernels for 14% -> 15%
where the time goes in v4:
time: 137 us; the launch traced here: 138 us
  starting transfers between devices  65.9 us (48%)
  waiting for transfers between devices  32.5 us (24%)
  Pallas kernels  27.4 us (20%)
  local copies, waits for them, and re-layouts  10.8 us (8%)
  between operations  1.52 us (1%)
    all_to_all x3, starting transfers between devices, trade(): lax.all_to_all(pieces, ('ty', 'tx'), 0, 0, axis_index_groups=groups, tile...  42.4 us
    ppermute x5, waiting for transfers between devices, swap(): lax.ppermute(second, axis, [(index, index ^ 1) for index in range(count)])  18.6 us
    ppermute x5, starting transfers between devices, swap(): lax.ppermute(first, axis, across)  14.6 us
    all_to_all x3, waiting for transfers between devices, trade(): lax.all_to_all(pieces, ('ty', 'tx'), 0, 0, axis_index_groups=groups, tile...  13.9 us
    unnamed x30, local copies, waits for them, and re-layouts  10.8 us
    ppermute x5, starting transfers between devices, swap(): lax.ppermute(second, axis, [(index, index ^ 1) for index in range(count)])  8.94 us
    pallas_call x1, Pallas kernels, per_device(): pl.pallas_call(outer_kernel, out_shape=(margin, margin, column, column, p...  4.55 us
    pallas_call x1, Pallas kernels, per_device(): pl.pallas_call(inner_kernel, out_shape=(jax.ShapeDtypeStruct((2, tiles +...  4.26 us
  transfers between devices with their start and end apart: 13, of which 4 were waited for; matrix products, arithmetic and copies ran while one was open for 0% of the time, Pallas kernels for 15%

profile of v4, /device:TPU:1, one launch (start us, length us, event | category | flops | bytes accessed | tf_op | source)
XLA Modules:
  0.0 138.3 jit_solution(13855976976180152366)
XLA Ops:
  1.3 0.1 add_and_fusion.odd
  1.4 1.6 %copy-done = f32[2,512,512]{2,1,0:T(8,128)S(1)} copy-done((f32[2,512,512]{2,1,0:T(8,128)S(1)}, f32[2,512,512]{2,1,0:T(8,128)}, u32[]{:S(2)}) %copy-start) | copy-done | bytes 2097176
  3.0 0.7 copy-done.13
  3.6 0.7 edges.1
  4.3 0.7 collective-permute-start
  5.0 5.4 %collective-permute-start.1 = (f32[2,520,128]{2,1,0:T(8,128)S(1)}, f32[2,520,128]{2,1,0:T(8,128)S(1)}, u32[]{:S(2)}, u32[]{:S(2)}) collective-permute-start(f32[2,520,128]{2,1,0:T(8,128)S(1)} %get-tuple-element.20), channel_id=1, source_target_pairs={{0,1},{1,0},{2,3},{3,2},{4,5},{5,4},{6,7},{7,6},{8,9},{9,8},{10,11... | collective-permute-start | bytes 1597448 | tf_op jit(solution)/shard_map/ppermute | solution.py:410
  10.4 4.3 %collective-permute-start.2 = (f32[2,128,512]{2,1,0:T(8,128)S(1)}, f32[2,128,512]{2,1,0:T(8,128)S(1)}, u32[]{:S(2)}, u32[]{:S(2)}) collective-permute-start(f32[2,128,512]{2,1,0:T(8,128)S(1)} %get-tuple-element.21), channel_id=1, source_target_pairs={{16,32},{32,16},{48,64},{64,48},{80,96},{96,80},{112,128},{128,112... | collective-permute-start | bytes 1572872 | tf_op jit(solution)/shard_map/ppermute | solution.py:410
  14.8 0.1 collective-permute-start.3
  14.9 0.0 collective-permute-done.x_first
  14.9 18.5 %collective-permute-done.1.x_second = f32[2,520,128]{2,1,0:T(8,128)S(1)} collective-permute-done((f32[2,520,128]{2,1,0:T(8,128)S(1)}, f32[2,520,128]{2,1,0:T(8,128)S(1)}, u32[]{:S(2)}, u32[]{:S(2)}) %collective-permute-start.1) | collective-permute-done | bytes 532512 | tf_op jit(solution)/shard_map/ppermute | solution.py:410
  33.4 0.6 corners.1
  34.0 4.6 %collective-permute-start.4 = (f32[2,2,144,128]{3,2,1,0:T(8,128)S(1)}, f32[2,2,144,128]{3,2,1,0:T(8,128)S(1)}, u32[]{:S(2)}, u32[]{:S(2)}) collective-permute-start(f32[2,2,144,128]{3,2,1,0:T(8,128)S(1)} %get-tuple-element.23), channel_id=1, source_target_pairs={{16,32},{32,16},{48,64},{64,48},{80,96},{96,80},{112,128},{128,112... | collective-permute-start | bytes 884744 | tf_op jit(solution)/shard_map/ppermute | solution.py:410
  38.6 0.1 collective-permute-start.5
  38.7 0.0 copy-start.11
  38.7 1.0 copy-done.11
  39.7 1.0 copy-done.12
  40.7 1.3 fold.1.folded
  42.1 0.2 copy-done.1
  42.3 0.1 copy-done.2
  42.4 0.5 copy-done.5
  42.9 4.3 %inner_slots.1 = (f32[2,6,512,128]{3,2,1,0:T(8,128)S(1)}, f32[3,2,256,128]{3,2,1,0:T(8,128)S(1)}) custom-call(s32[2]{0:T(128)S(1)} %add_and_fusion.odd, s32[2,8]{1,0:T(2,128)S(1)} %bitcast.14, s32[1]{0:T(128)} %bitcast.9.count, f32[2,256,256]{2,1,0:T(8,128)S(1)} %copy-done.2, f32[8,256,256]{2,1,0:T(8,128)S(1)} %fold.1.folded, ...), custom_call_target="tpu_custom_call" | custom-call | bytes 16777216 | tf_op jit(solution)/shard_map/inner_slots/pallas_call | solution.py:493
  47.2 0.0 collective-permute-done.2.y_first
  47.2 4.5 %outer_slots.1 = (f32[2,6,128,128]{3,2,1,0:T(8,128)}, f32[2,6,128,128]{3,2,1,0:T(8,128)}, f32[2,512,128]{2,1,0:T(8,128)}, f32[2,512,128]{2,1,0:T(8,128)}, f32[2,...) custom-call(s32[2]{0:T(128)S(1)} %add_and_fusion.odd, s32[2,8]{1,0:T(2,128)S(1)} %bitcast.15, ...), custom_call_target="tpu_custom_call" | custom-call | bytes 16777216 | tf_op jit(solution)/shard_map/outer_slots/pallas_call | solution.py:508
  51.8 24.2 %all-to-all-start = ((f32[32,6,8,128]{3,2,1,0:T(8,128)}), f32[32,6,8,128]{3,2,1,0:T(8,128)}, u32[]{:S(2)}, u32[]{:S(2)}) async-start(f32[32,6,8,128]{3,2,1,0:T(8,128)} %get-tuple-element.35), calls=%async_computation | async-start | bytes 1572864 | tf_op jit(solution)/shard_map/all_to_all | solution.py:432
  76.0 3.5 %collective-permute-start.6 = (f32[2,6,128,128]{3,2,1,0:T(8,128)}, f32[2,6,128,128]{3,2,1,0:T(8,128)}, u32[]{:S(2)}, u32[]{:S(2)}) collective-permute-start(f32[2,6,128,128]{3,2,1,0:T(8,128)} %get-tuple-element.28), channel_id=1, source_target_pairs={{16,32},{32,16},{48,64},{64,48},{80,96},{96,80},{112,128},{128,112... | collective-permute-start | bytes 2359304 | tf_op jit(solution)/shard_map/ppermute | solution.py:410
  79.5 0.1 collective-permute-start.7
  79.6 0.0 copy-start.3
  79.6 1.0 copy-done.3
  80.7 2.6 %weights.1.scale.after = f32[4,512,128]{2,1,0:T(8,128)S(1)} custom-call(f32[9,8,128]{2,1,0:T(8,128)S(1)} %get-tuple-element.30.numbers, f32[2,256,256]{2,1,0:T(8,128)S(1)} %copy-done.3), custom_call_target="tpu_custom_call" | custom-call | bytes 8388608 | tf_op jit(solution)/shard_map/weights/pallas_call | solution.py:533
  83.3 6.4 %all-to-all-done.parts = f32[32,6,8,128]{3,2,1,0:T(8,128)} async-done(((f32[32,6,8,128]{3,2,1,0:T(8,128)}), f32[32,6,8,128]{3,2,1,0:T(8,128)}, u32[]{:S(2)}, u32[]{:S(2)}) %all-to-all-start) | async-done | bytes 786464 | tf_op jit(solution)/shard_map/all_to_all | solution.py:432
  89.7 1.9 %plane_sum.1 = f32[8,6,8,128]{3,2,1,0:T(8,128)} custom-call(f32[32,6,8,128]{3,2,1,0:T(8,128)} %all-to-all-done.parts, f32[4,512,128]{2,1,0:T(8,128)S(1)} %weights.1.scale.after), custom_call_target="tpu_custom_call" | custom-call | bytes 2097152 | tf_op jit(solution)/shard_map/plane_sum/pallas_call | solution.py:563
  91.6 4.5 %all-to-all-start.1 = ((f32[8,6,8,128]{3,2,1,0:T(8,128)}), f32[8,6,8,128]{3,2,1,0:T(8,128)S(1)}, u32[]{:S(2)}, u32[]{:S(2)}) async-start(f32[8,6,8,128]{3,2,1,0:T(8,128)} %plane_sum.1), calls=%async_computation.1 | async-start | bytes 393216 | tf_op jit(solution)/shard_map/all_to_all | solution.py:432
  96.1 0.0 copy-start.9
  96.1 1.0 copy-done.9
  97.1 1.0 copy-done.10
  98.2 2.2 %sides.1 = (f32[2,512,128]{2,1,0:T(8,128)}, f32[2,512,128]{2,1,0:T(8,128)}) custom-call(s32[2]{0:T(128)S(1)} %add_and_fusion.odd, f32[2,512,128]{2,1,0:T(8,128)S(1)} %copy-done.9, f32[2,512,128]{2,1,0:T(8,128)S(1)} %copy-done.10, f32[2,6,128,128]{3,2,1,0:T(8,128)} %collective-permute-done.6.y_first.low_first.high_first, ...), custom_call_target="tpu_custom_call" | custom-call | bytes 16777216 | tf_op jit(solution)/shard_map/sides/pallas_call | solution.py:551
  100.4 1.5 %collective-permute-start.8 = (f32[2,512,128]{2,1,0:T(8,128)}, f32[2,512,128]{2,1,0:T(8,128)}, u32[]{:S(2)}, u32[]{:S(2)}) collective-permute-start(f32[2,512,128]{2,1,0:T(8,128)} %get-tuple-element.33), channel_id=1, source_target_pairs={{1,2},{2,1},{3,4},{4,3},{5,6},{6,5},{7,8},{8,7},{9,10},{10,9},{11,... | collective-permute-start | bytes 1572872 | tf_op jit(solution)/shard_map/ppermute | solution.py:410
  101.9 3.3 %collective-permute-start.9 = (f32[2,512,128]{2,1,0:T(8,128)}, f32[2,512,128]{2,1,0:T(8,128)}, u32[]{:S(2)}, u32[]{:S(2)}) collective-permute-start(f32[2,512,128]{2,1,0:T(8,128)} %get-tuple-element.34), channel_id=1, source_target_pairs={{0,1},{1,0},{2,3},{3,2},{4,5},{5,4},{6,7},{7,6},{8,9},{9,8},{10,11... | collective-permute-start | bytes 1572872 | tf_op jit(solution)/shard_map/ppermute | solution.py:410
  105.1 4.2 %all-to-all-done.1.parts = f32[8,6,8,128]{3,2,1,0:T(8,128)S(1)} async-done(((f32[8,6,8,128]{3,2,1,0:T(8,128)}), f32[8,6,8,128]{3,2,1,0:T(8,128)S(1)}, u32[]{:S(2)}, u32[]{:S(2)}) %all-to-all-start.1) | async-done | bytes 196640 | tf_op jit(solution)/shard_map/all_to_all | solution.py:432
  109.3 1.0 copy-done.4
  110.3 0.9 probe_rows.1
  111.2 13.7 %all-to-all-start.2 = ((f32[32,4,8,128]{3,2,1,0:T(8,128)}), f32[32,4,8,128]{3,2,1,0:T(8,128)}, u32[]{:S(2)}, u32[]{:S(2)}) async-start(f32[32,4,8,128]{3,2,1,0:T(8,128)} %probe_rows.1), calls=%async_computation.2 | async-start | bytes 1048576 | tf_op jit(solution)/shard_map/all_to_all | solution.py:432
  125.0 0.0 copy-start.7
  125.0 1.6 %copy-done.7 = f32[2,4,512,128]{3,2,1,0:T(8,128)S(1)} copy-done((f32[2,4,512,128]{3,2,1,0:T(8,128)S(1)}, f32[2,4,512,128]{3,2,1,0:T(8,128)}, u32[]{:S(2)}) %copy-start.7) | copy-done | bytes 2097176
  126.6 4.0 %update.1.before = f32[2,512,512]{2,1,0:T(8,128)} custom-call(s32[2]{0:T(128)S(1)} %add_and_fusion.odd, f32[2,512,512]{2,1,0:T(8,128)S(1)} %copy-done.1, f32[2,4,512,128]{3,2,1,0:T(8,128)S(1)} %copy-done.7, f32[2,6,128,128]{3,2,1,0:T(8,128)} %collective-permute-done.6.y_first.low_first.high_first, ...), custom_call_target="tpu_custom_call" | custom-call | bytes 8388608 | tf_op jit(solution)/shard_map/update/pallas_call | solution.py:594
  130.6 2.5 %columns.1 = f32[2,512,512]{2,1,0:T(8,128)} custom-call(s32[2]{0:T(128)S(1)} %add_and_fusion.odd, f32[2,512,512]{2,1,0:T(8,128)} %update.1.before, f32[2,512,128]{2,1,0:T(8,128)} %collective-permute-done.8.x_first, f32[2,512,128]{2,1,0:T(8,128)} %collective-permute-done.9.x_second, f32[4,512,128]{2,1,0:T(8,128)S(1)} %weights.1.scale.after), custom_call_target="tpu_custom_call", output_to_operand_aliasing={{}: (1, {})} | custom-call | tf_op jit(solution)/shard_map/columns/pallas_call | solution.py:608
  133.1 3.3 %all-to-all-done.2.pieces = f32[32,4,8,128]{3,2,1,0:T(8,128)} async-done(((f32[32,4,8,128]{3,2,1,0:T(8,128)}), f32[32,4,8,128]{3,2,1,0:T(8,128)}, u32[]{:S(2)}, u32[]{:S(2)}) %all-to-all-start.2) | async-done | bytes 524320 | tf_op jit(solution)/shard_map/all_to_all | solution.py:432
  136.4 1.9 %join.1 = f32[2,256,256]{2,1,0:T(8,128)} custom-call(f32[32,4,8,128]{3,2,1,0:T(8,128)} %all-to-all-done.2.pieces), custom_call_target="tpu_custom_call" | custom-call | bytes 2097152 | tf_op jit(solution)/shard_map/join/pallas_call | solution.py:582
  (21 shorter events, 0.0 us)
Async XLA Ops:
  1.4 1.6 %copy-start = (f32[2,512,512]{2,1,0:T(8,128)S(1)}, f32[2,512,512]{2,1,0:T(8,128)}, u32[]{:S(2)}) copy-start(f32[2,512,512]{2,1,0:T(8,128)} %tile_ref.7) | copy-start | bytes 6291460
  3.0 0.7 copy-start.13
  3.6 35.1 %copy-start.8 = (f32[1,1,8,256,256]{4,3,2,1,0:T(8,128)S(1)}, f32[1,1,8,256,256]{4,3,2,1,0:T(8,128)}, u32[]{:S(2)}) copy-start(f32[1,1,8,256,256]{4,3,2,1,0:T(8,128)} %param.11) | copy-start | bytes 6291460
  4.3 10.5 %collective-permute-start = (f32[2,520,128]{2,1,0:T(8,128)S(1)}, f32[2,520,128]{2,1,0:T(8,128)S(1)}, u32[]{:S(2)}, u32[]{:S(2)}) collective-permute-start(f32[2,520,128]{2,1,0:T(8,128)S(1)} %get-tuple-element.19), channel_id=1, source_target_pairs={{1,2},{2,1},{3,4},{4,3},{5,6},{6,5},{7,8},{8,7},{9,10},{10,9},{11,... | collective-permute-start | bytes 1597448 | tf_op jit(solution)/shard_map/ppermute | solution.py:410
  5.0 28.4 %collective-permute-start.1 = (f32[2,520,128]{2,1,0:T(8,128)S(1)}, f32[2,520,128]{2,1,0:T(8,128)S(1)}, u32[]{:S(2)}, u32[]{:S(2)}) collective-permute-start(f32[2,520,128]{2,1,0:T(8,128)S(1)} %get-tuple-element.20), channel_id=1, source_target_pairs={{0,1},{1,0},{2,3},{3,2},{4,5},{5,4},{6,7},{7,6},{8,9},{9,8},{10,11... | collective-permute-start | bytes 1597448 | tf_op jit(solution)/shard_map/ppermute | solution.py:410
  10.4 36.7 %collective-permute-start.2 = (f32[2,128,512]{2,1,0:T(8,128)S(1)}, f32[2,128,512]{2,1,0:T(8,128)S(1)}, u32[]{:S(2)}, u32[]{:S(2)}) collective-permute-start(f32[2,128,512]{2,1,0:T(8,128)S(1)} %get-tuple-element.21), channel_id=1, source_target_pairs={{16,32},{32,16},{48,64},{64,48},{80,96},{96,80},{112,128},{128,112... | collective-permute-start | bytes 1572872 | tf_op jit(solution)/shard_map/ppermute | solution.py:410
  14.8 32.4 %collective-permute-start.3 = (f32[2,128,512]{2,1,0:T(8,128)S(1)}, f32[2,128,512]{2,1,0:T(8,128)S(1)}, u32[]{:S(2)}, u32[]{:S(2)}) collective-permute-start(f32[2,128,512]{2,1,0:T(8,128)S(1)} %get-tuple-element.22), channel_id=1, source_target_pairs={{0,16},{16,0},{32,48},{48,32},{64,80},{80,64},{96,112},{112,96},{1... | collective-permute-start | bytes 1572872 | tf_op jit(solution)/shard_map/ppermute | solution.py:410
  33.4 8.7 %copy-start.6 = (bf16[4,256,768]{2,1,0:T(8,128)(2,1)S(1)}, bf16[4,256,768]{2,1,0:T(8,128)(2,1)}, u32[]{:S(2)}) copy-start(bf16[4,256,768]{2,1,0:T(8,128)(2,1)} %constant.23.clone.left) | copy-start | bytes 4718596
  34.0 13.2 %collective-permute-start.4 = (f32[2,2,144,128]{3,2,1,0:T(8,128)S(1)}, f32[2,2,144,128]{3,2,1,0:T(8,128)S(1)}, u32[]{:S(2)}, u32[]{:S(2)}) collective-permute-start(f32[2,2,144,128]{3,2,1,0:T(8,128)S(1)} %get-tuple-element.23), channel_id=1, source_target_pairs={{16,32},{32,16},{48,64},{64,48},{80,96},{96,80},{112,128},{128,112... | collective-permute-start | bytes 884744 | tf_op jit(solution)/shard_map/ppermute | solution.py:410
  38.6 8.6 %collective-permute-start.5 = (f32[2,2,144,128]{3,2,1,0:T(8,128)S(1)}, f32[2,2,144,128]{3,2,1,0:T(8,128)S(1)}, u32[]{:S(2)}, u32[]{:S(2)}) collective-permute-start(f32[2,2,144,128]{3,2,1,0:T(8,128)S(1)} %get-tuple-element.24), channel_id=1, source_target_pairs={{0,16},{16,0},{32,48},{48,32},{64,80},{80,64},{96,112},{112,96},{1... | collective-permute-start | bytes 884744 | tf_op jit(solution)/shard_map/ppermute | solution.py:410
  38.7 1.0 copy-start.11
  39.7 1.0 copy-start.12
  40.7 1.6 %copy-start.1 = (f32[2,512,512]{2,1,0:T(8,128)S(1)}, f32[2,512,512]{2,1,0:T(8,128)}, u32[]{:S(2)}) copy-start(f32[2,512,512]{2,1,0:T(8,128)} %tile_ref.7) | copy-start | bytes 6291460
  40.7 1.7 %copy-start.2 = (f32[2,256,256]{2,1,0:T(8,128)S(1)}, f32[2,256,256]{2,1,0:T(8,128)}, u32[]{:S(2)}) copy-start(f32[2,256,256]{2,1,0:T(8,128)} %probe.7) | copy-start | bytes 1572868
  40.7 2.2 %copy-start.5 = (bf16[4,768,256]{2,1,0:T(8,128)(2,1)S(1)}, bf16[4,768,256]{2,1,0:T(8,128)(2,1)}, u32[]{:S(2)}) copy-start(bf16[4,768,256]{2,1,0:T(8,128)(2,1)} %constant.24.clone.right) | copy-start | bytes 4718596
  40.7 2.2 %copy-start.14 = (s32[2,1,1,8]{3,2,1,0:T(1,128)S(1)}, s32[2,1,1,8]{3,2,1,0:T(1,128)}, u32[]{:S(2)}) copy-start(s32[2,1,1,8]{3,2,1,0:T(1,128)} %param.12) | copy-start | bytes 196
  51.8 37.9 %all-to-all-start = ((f32[32,6,8,128]{3,2,1,0:T(8,128)}), f32[32,6,8,128]{3,2,1,0:T(8,128)}, u32[]{:S(2)}, u32[]{:S(2)}) async-start(f32[32,6,8,128]{3,2,1,0:T(8,128)} %get-tuple-element.35), calls=%async_computation | async-start | bytes 1572864 | tf_op jit(solution)/shard_map/all_to_all | solution.py:432
  76.0 20.1 %collective-permute-start.6 = (f32[2,6,128,128]{3,2,1,0:T(8,128)}, f32[2,6,128,128]{3,2,1,0:T(8,128)}, u32[]{:S(2)}, u32[]{:S(2)}) collective-permute-start(f32[2,6,128,128]{3,2,1,0:T(8,128)} %get-tuple-element.28), channel_id=1, source_target_pairs={{16,32},{32,16},{48,64},{64,48},{80,96},{96,80},{112,128},{128,112... | collective-permute-start | bytes 2359304 | tf_op jit(solution)/shard_map/ppermute | solution.py:410
  79.5 16.5 %collective-permute-start.7 = (f32[2,6,128,128]{3,2,1,0:T(8,128)}, f32[2,6,128,128]{3,2,1,0:T(8,128)}, u32[]{:S(2)}, u32[]{:S(2)}) collective-permute-start(f32[2,6,128,128]{3,2,1,0:T(8,128)} %get-tuple-element.29), channel_id=1, source_target_pairs={{0,16},{16,0},{32,48},{48,32},{64,80},{80,64},{96,112},{112,96},{1... | collective-permute-start | bytes 2359304 | tf_op jit(solution)/shard_map/ppermute | solution.py:410
  79.6 1.0 copy-start.3
  91.6 17.7 %all-to-all-start.1 = ((f32[8,6,8,128]{3,2,1,0:T(8,128)}), f32[8,6,8,128]{3,2,1,0:T(8,128)S(1)}, u32[]{:S(2)}, u32[]{:S(2)}) async-start(f32[8,6,8,128]{3,2,1,0:T(8,128)} %plane_sum.1), calls=%async_computation.1 | async-start | bytes 393216 | tf_op jit(solution)/shard_map/all_to_all | solution.py:432
  96.1 1.0 copy-start.9
  97.1 1.0 copy-start.10
  100.4 30.2 %collective-permute-start.8 = (f32[2,512,128]{2,1,0:T(8,128)}, f32[2,512,128]{2,1,0:T(8,128)}, u32[]{:S(2)}, u32[]{:S(2)}) collective-permute-start(f32[2,512,128]{2,1,0:T(8,128)} %get-tuple-element.33), channel_id=1, source_target_pairs={{1,2},{2,1},{3,4},{4,3},{5,6},{6,5},{7,8},{8,7},{9,10},{10,9},{11,... | collective-permute-start | bytes 1572872 | tf_op jit(solution)/shard_map/ppermute | solution.py:410
  101.9 28.7 %collective-permute-start.9 = (f32[2,512,128]{2,1,0:T(8,128)}, f32[2,512,128]{2,1,0:T(8,128)}, u32[]{:S(2)}, u32[]{:S(2)}) collective-permute-start(f32[2,512,128]{2,1,0:T(8,128)} %get-tuple-element.34), channel_id=1, source_target_pairs={{0,1},{1,0},{2,3},{3,2},{4,5},{5,4},{6,7},{7,6},{8,9},{9,8},{10,11... | collective-permute-start | bytes 1572872 | tf_op jit(solution)/shard_map/ppermute | solution.py:410
  109.3 1.0 copy-start.4
  111.2 25.2 %all-to-all-start.2 = ((f32[32,4,8,128]{3,2,1,0:T(8,128)}), f32[32,4,8,128]{3,2,1,0:T(8,128)}, u32[]{:S(2)}, u32[]{:S(2)}) async-start(f32[32,4,8,128]{3,2,1,0:T(8,128)} %probe_rows.1), calls=%async_computation.2 | async-start | bytes 1048576 | tf_op jit(solution)/shard_map/all_to_all | solution.py:432
  125.0 1.6 %copy-start.7 = (f32[2,4,512,128]{3,2,1,0:T(8,128)S(1)}, f32[2,4,512,128]{3,2,1,0:T(8,128)}, u32[]{:S(2)}) copy-start(f32[2,4,512,128]{3,2,1,0:T(8,128)} %get-tuple-element.27.grad) | copy-start | bytes 6291460

commit v5 on v4

--- a/solution.py
+++ b/solution.py
@@ -129,7 +129,7 @@
     y_second[...] = jnp.where(odd_y, low, high)
 
 
-def corner_kernel(odd, position, count, x_first, x_second, first, second):
+def corner_kernel(odd, position, count, x_first, x_second, after, first, second):
     half = LANES
     side = x_first.shape[1] - 8
     far = side - half
@@ -316,7 +316,7 @@
         copy.wait()
 
 
-def sides_kernel(odd, own_low, own_high, low_first, low_second, high_first, high_second, first, second):
+def sides_kernel(odd, own_low, own_high, low_first, low_second, high_first, high_second, first, second, token):
     half = LANES
     side = own_low.shape[1]
     odd_y, odd_x = odd[0] == 1, odd[1] == 1
@@ -332,6 +332,7 @@
             values.append(value)
         first[:, rows, :] = jnp.where(odd_x, values[1], values[0])
         second[:, rows, :] = jnp.where(odd_x, values[0], values[1])
+    token[...] = jnp.zeros_like(token)
 
 
 def weight_kernel(numbers, probe, scale, power, weight):
@@ -383,7 +384,7 @@
         out[plane] = before[plane] - jnp.where(use_first, x_first[plane], x_second[plane]) * scale[0]
 
 
-def plane_kernel(parts, after, out):
+def plane_kernel(parts, after, later, out):
     out[...] = jnp.broadcast_to(jnp.sum(parts[...], axis=0)[None], out.shape)
 
 
@@ -408,6 +409,10 @@
     count = lax.axis_size(axis)
     across = [pair for low in range(1, count - 1, 2) for pair in ((low, low + 1), (low + 1, low))]
     return lax.ppermute(first, axis, across), lax.ppermute(second, axis, [(index, index ^ 1) for index in range(count)])
+
+
+def keep(value):
+    return pltpu.with_memory_space_constraint(value, pltpu.HBM)
 
 
 def params(mib):
@@ -474,12 +479,12 @@
         corners = pl.pallas_call(
             corner_kernel,
             out_shape=(corner, corner),
-            in_specs=[SMEM] * 3 + [VMEM] * 2,
+            in_specs=[SMEM] * 3 + [VMEM] * 2 + [HBM],
             out_specs=(VMEM, VMEM),
             compiler_params=params(4),
             cost_estimate=cost(4),
             name="corners",
-        )(odd, position, count, x_first, x_second)
+        )(odd, position, count, x_first, x_second, folded)
         corners = swap(*corners, "ty")
 
         members = len(planes[0])
@@ -542,33 +547,33 @@
             compiler_params=params(8),
             cost_estimate=cost(8),
             name="weights",
-        )(places, probe)
+        )(places, keep(probe))
         parts = trade(sums, planes)
-        strip = jax.ShapeDtypeStruct((2, side, LANES), F32)
+        strip = pltpu.HBM((2, side, LANES), F32)
         whole = pl.BlockSpec((2, side, LANES), lambda index: (0, 0, 0))
         first_tile = pl.BlockSpec((2, 1, half, LANES), lambda index: (0, 0, 0, 0))
         last_tile = pl.BlockSpec((2, 1, half, LANES), lambda index: (0, tiles + 1, 0, 0))
-        x_first, x_second = pl.pallas_call(
+        *margins, token = pl.pallas_call(
             sides_kernel,
-            out_shape=(strip, strip),
+            out_shape=(strip, strip, jax.ShapeDtypeStruct((8, LANES), F32)),
             grid=(1,),
             in_specs=[SMEM, whole, whole, first_tile, first_tile, last_tile, last_tile],
-            out_specs=(whole, whole),
+            out_specs=(whole, whole, pl.BlockSpec((8, LANES), lambda index: (0, 0))),
             compiler_params=params(8),
             cost_estimate=cost(16),
             name="sides",
-        )(odd, side_low, side_high, margin_first, margin_second, margin_first, margin_second)
-        x_first, x_second = swap(x_first, x_second, "tx")
+        )(odd, keep(side_low), keep(side_high), margin_first, margin_second, margin_first, margin_second)
+        x_first, x_second = swap(*margins, "tx")
 
         parts = pl.pallas_call(
             plane_kernel,
             out_shape=pltpu.HBM((len(lines[0]), 6, 8, LANES), F32),
-            in_specs=[VMEM, HBM],
+            in_specs=[VMEM, HBM, HBM],
             out_specs=VMEM,
             compiler_params=params(6),
             cost_estimate=cost(2),
             name="plane_sum",
-        )(parts, scale)
+        )(parts, scale, token)
         parts = trade(parts, lines)
         pieces = pl.pallas_call(
             probe_kernel,
@@ -578,7 +583,7 @@
             compiler_params=params(6),
             cost_estimate=cost(2),
             name="probe_rows",
-        )(piece, parts, probe)
+        )(piece, parts, keep(probe))
         probe_new = pl.pallas_call(
             join_kernel,
             out_shape=jax.ShapeDtypeStruct(probe.shape, F32),
@@ -603,7 +608,7 @@
             compiler_params=params(8),
             cost_estimate=cost(8),
             name="update",
-        )(odd, object_field, middle, margin_first, margin_second, scale)
+        )(odd, keep(object_field), keep(middle), margin_first, margin_second, scale)
         ends = pl.BlockSpec((2, side, LANES), lambda index: (0, 0, index * (tiles - 1)))
         object_new = pl.pallas_call(
             column_kernel,

time: 137 us -> 145 us (1.058)
  the two profiles are of different devices: /device:TPU:1 before, /device:TPU:33 now
where the time goes in v5:
time: 145 us; the launch traced here: 143 us
  starting transfers between devices  73.7 us (51%)
  waiting for transfers between devices  33.3 us (23%)
  Pallas kernels  30.1 us (21%)
  local copies, waits for them, and re-layouts  4.28 us (3%)
  between operations  1.55 us (1%)
    all_to_all x3, starting transfers between devices, trade(): lax.all_to_all(pieces, ('ty', 'tx'), 0, 0, axis_index_groups=groups, tile...  56.2 us
    all_to_all x3, waiting for transfers between devices, trade(): lax.all_to_all(pieces, ('ty', 'tx'), 0, 0, axis_index_groups=groups, tile...  17.8 us
    ppermute x5, starting transfers between devices, swap(): lax.ppermute(first, axis, across)  17 us
    ppermute x5, waiting for transfers between devices, swap(): lax.ppermute(first, axis, across)  15.5 us
    pallas_call x1, Pallas kernels, per_device(): pl.pallas_call(outer_kernel, out_shape=(margin, margin, column, column, p...  7.77 us
    pallas_call x1, Pallas kernels, per_device(): pl.pallas_call(update_kernel, out_shape=jax.ShapeDtypeStruct(object_field...  4.34 us
    pallas_call x1, Pallas kernels, per_device(): pl.pallas_call(inner_kernel, out_shape=(jax.ShapeDtypeStruct((2, tiles +...  4.31 us
    unnamed x20, local copies, waits for them, and re-layouts  4.28 us
  transfers between devices with their start and end apart: 13, of which 4 were waited for; matrix products, arithmetic and copies ran while one was open for 0% of the time, Pallas kernels for 14%

profile of v5, /device:TPU:33, one launch (start us, length us, event | category | flops | bytes accessed | tf_op | source)
XLA Modules:
  0.0 143.0 jit_solution(10112349453636963276)
XLA Ops:
  1.3 0.1 add_and_fusion.odd
  1.4 1.6 %copy-done = f32[2,512,512]{2,1,0:T(8,128)S(1)} copy-done((f32[2,512,512]{2,1,0:T(8,128)S(1)}, f32[2,512,512]{2,1,0:T(8,128)}, u32[]{:S(2)}) %copy-start) | copy-done | bytes 2097176
  3.0 0.7 copy-done.8
  3.6 0.7 edges.1
  4.3 3.5 %collective-permute-start = (f32[2,520,128]{2,1,0:T(8,128)S(1)}, f32[2,520,128]{2,1,0:T(8,128)S(1)}, u32[]{:S(2)}, u32[]{:S(2)}) collective-permute-start(f32[2,520,128]{2,1,0:T(8,128)S(1)} %get-tuple-element.20), channel_id=1, source_target_pairs={{1,2},{2,1},{3,4},{4,3},{5,6},{6,5},{7,8},{8,7},{9,10},{10,9},{11,... | collective-permute-start | bytes 1597448 | tf_op jit(solution)/shard_map/ppermute | solution.py:411
  7.9 0.1 collective-permute-start.1
  8.0 4.0 %collective-permute-start.2 = (f32[2,128,512]{2,1,0:T(8,128)S(1)}, f32[2,128,512]{2,1,0:T(8,128)S(1)}, u32[]{:S(2)}, u32[]{:S(2)}) collective-permute-start(f32[2,128,512]{2,1,0:T(8,128)S(1)} %get-tuple-element.22), channel_id=1, source_target_pairs={{16,32},{32,16},{48,64},{64,48},{80,96},{96,80},{112,128},{128,112... | collective-permute-start | bytes 1572872 | tf_op jit(solution)/shard_map/ppermute | solution.py:411
  12.0 0.1 collective-permute-start.3
  12.1 0.0 copy-done.5
  12.2 0.0 copy-start.6
  12.2 1.0 copy-done.6
  13.2 1.0 copy-done.7
  14.2 1.3 fold.1.after.folded
  15.5 0.0 copy-start.1
  15.5 0.0 copy-start.2
  15.5 15.5 %collective-permute-done.x_first = f32[2,520,128]{2,1,0:T(8,128)S(1)} collective-permute-done((f32[2,520,128]{2,1,0:T(8,128)S(1)}, f32[2,520,128]{2,1,0:T(8,128)S(1)}, u32[]{:S(2)}, u32[]{:S(2)}) %collective-permute-start) | collective-permute-done | bytes 532512 | tf_op jit(solution)/shard_map/ppermute | solution.py:411
  31.0 0.0 collective-permute-done.1.x_second
  31.0 0.0 copy-done.9
  31.0 0.6 corners.1
  31.6 4.4 %collective-permute-start.4 = (f32[2,2,144,128]{3,2,1,0:T(8,128)S(1)}, f32[2,2,144,128]{3,2,1,0:T(8,128)S(1)}, u32[]{:S(2)}, u32[]{:S(2)}) collective-permute-start(f32[2,2,144,128]{3,2,1,0:T(8,128)S(1)} %get-tuple-element.24), channel_id=1, source_target_pairs={{16,32},{32,16},{48,64},{64,48},{80,96},{96,80},{112,128},{128,112... | collective-permute-start | bytes 884744 | tf_op jit(solution)/shard_map/ppermute | solution.py:411
  36.0 0.1 collective-permute-start.5
  36.2 4.3 %inner_slots.1 = (f32[2,6,512,128]{3,2,1,0:T(8,128)S(1)}, f32[3,2,256,128]{3,2,1,0:T(8,128)S(1)}) custom-call(s32[2]{0:T(128)S(1)} %add_and_fusion.odd, s32[2,8]{1,0:T(2,128)S(1)} %bitcast.14, s32[1]{0:T(128)} %bitcast.9.count, f32[2,256,256]{2,1,0:T(8,128)S(1)} %copy-done.2, f32[8,256,256]{2,1,0:T(8,128)S(1)} %fold.1.after.folded, ...), custom_call_target="tpu_custom_call" | custom-call | bytes 16777216 | tf_op jit(solution)/shard_map/inner_slots/pallas_call | solution.py:498
  40.5 0.0 collective-permute-done.2.y_first
  40.5 0.0 collective-permute-done.3.y_second
  40.5 0.0 collective-permute-done.4.corner_first
  40.5 0.0 collective-permute-done.5.corner_second
  40.5 7.8 %outer_slots.1 = (f32[2,6,128,128]{3,2,1,0:T(8,128)}, f32[2,6,128,128]{3,2,1,0:T(8,128)}, f32[2,512,128]{2,1,0:T(8,128)}, f32[2,512,128]{2,1,0:T(8,128)}, f32[2,...) custom-call(s32[2]{0:T(128)S(1)} %add_and_fusion.odd, s32[2,8]{1,0:T(2,128)S(1)} %bitcast.15, ...), custom_call_target="tpu_custom_call" | custom-call | bytes 16777216 | tf_op jit(solution)/shard_map/outer_slots/pallas_call | solution.py:513
  48.3 1.9 %collective-permute-start.6 = (f32[2,6,128,128]{3,2,1,0:T(8,128)}, f32[2,6,128,128]{3,2,1,0:T(8,128)S(1)}, u32[]{:S(2)}, u32[]{:S(2)}) collective-permute-start(f32[2,6,128,128]{3,2,1,0:T(8,128)} %get-tuple-element.29), channel_id=1, source_target_pairs={{16,32},{32,16},{48,64},{64,48},{80,96},{96,80},{112,128},{128,112... | collective-permute-start | bytes 2359304 | tf_op jit(solution)/shard_map/ppermute | solution.py:411
  50.3 0.1 collective-permute-start.7
  50.4 28.5 %all-to-all-start = ((f32[32,6,8,128]{3,2,1,0:T(8,128)}), f32[32,6,8,128]{3,2,1,0:T(8,128)S(1)}, u32[]{:S(2)}, u32[]{:S(2)}) async-start(f32[32,6,8,128]{3,2,1,0:T(8,128)} %get-tuple-element.36), calls=%async_computation | async-start | bytes 1572864 | tf_op jit(solution)/shard_map/all_to_all | solution.py:437
  78.9 2.7 %weights.1.scale.after = f32[4,512,128]{2,1,0:T(8,128)S(1)} custom-call(f32[9,8,128]{2,1,0:T(8,128)S(1)} %get-tuple-element.31.numbers, f32[2,256,256]{2,1,0:T(8,128)} %probe.7), custom_call_target="tpu_custom_call" | custom-call | bytes 8388608 | tf_op jit(solution)/shard_map/weights/pallas_call | solution.py:538
  81.6 0.0 collective-permute-done.6.y_first.low_first.high_first
  81.6 0.0 collective-permute-done.7.y_second.low_second.high_second
  81.6 2.3 %sides.1 = (f32[2,512,128]{2,1,0:T(8,128)}, f32[2,512,128]{2,1,0:T(8,128)}, f32[8,128]{1,0:T(8,128)S(1)}) custom-call(s32[2]{0:T(128)S(1)} %add_and_fusion.odd, f32[2,512,128]{2,1,0:T(8,128)} %get-tuple-element.32.own_low, f32[2,512,128]{2,1,0:T(8,128)} %get-tuple-element.33.own_high, ...), custom_call_target="tpu_custom_call" | custom-call | bytes 16777216 | tf_op jit(solution)/shard_map/sides/pallas_call | solution.py:556
  84.0 8.9 %all-to-all-done.parts = f32[32,6,8,128]{3,2,1,0:T(8,128)S(1)} async-done(((f32[32,6,8,128]{3,2,1,0:T(8,128)}), f32[32,6,8,128]{3,2,1,0:T(8,128)S(1)}, u32[]{:S(2)}, u32[]{:S(2)}) %all-to-all-start) | async-done | bytes 786464 | tf_op jit(solution)/shard_map/all_to_all | solution.py:437
  92.9 0.7 plane_sum.1
  93.6 6.9 %all-to-all-start.1 = ((f32[8,6,8,128]{3,2,1,0:T(8,128)}), f32[8,6,8,128]{3,2,1,0:T(8,128)S(1)}, u32[]{:S(2)}, u32[]{:S(2)}) async-start(f32[8,6,8,128]{3,2,1,0:T(8,128)} %plane_sum.1), calls=%async_computation.1 | async-start | bytes 393216 | tf_op jit(solution)/shard_map/all_to_all | solution.py:437
  100.6 3.1 %collective-permute-start.8 = (f32[2,512,128]{2,1,0:T(8,128)}, f32[2,512,128]{2,1,0:T(8,128)}, u32[]{:S(2)}, u32[]{:S(2)}) collective-permute-start(f32[2,512,128]{2,1,0:T(8,128)} %get-tuple-element.34), channel_id=1, source_target_pairs={{1,2},{2,1},{3,4},{4,3},{5,6},{6,5},{7,8},{8,7},{9,10},{10,9},{11,... | collective-permute-start | bytes 1572872 | tf_op jit(solution)/shard_map/ppermute | solution.py:411
  103.7 0.1 collective-permute-start.9
  103.8 4.3 %all-to-all-done.1.parts = f32[8,6,8,128]{3,2,1,0:T(8,128)S(1)} async-done(((f32[8,6,8,128]{3,2,1,0:T(8,128)}), f32[8,6,8,128]{3,2,1,0:T(8,128)S(1)}, u32[]{:S(2)}, u32[]{:S(2)}) %all-to-all-start.1) | async-done | bytes 196640 | tf_op jit(solution)/shard_map/all_to_all | solution.py:437
  108.0 1.9 %probe_rows.1 = f32[32,4,8,128]{3,2,1,0:T(8,128)} custom-call(s32[1]{0:T(128)} %bitcast.5.index, f32[8,6,8,128]{3,2,1,0:T(8,128)S(1)} %all-to-all-done.1.parts, f32[2,256,256]{2,1,0:T(8,128)} %probe.7), custom_call_target="tpu_custom_call" | custom-call | bytes 2097152 | tf_op jit(solution)/shard_map/probe_rows/pallas_call | solution.py:578
  110.0 20.8 %all-to-all-start.2 = ((f32[32,4,8,128]{3,2,1,0:T(8,128)}), f32[32,4,8,128]{3,2,1,0:T(8,128)S(1)}, u32[]{:S(2)}, u32[]{:S(2)}) async-start(f32[32,4,8,128]{3,2,1,0:T(8,128)} %probe_rows.1), calls=%async_computation.2 | async-start | bytes 1048576 | tf_op jit(solution)/shard_map/all_to_all | solution.py:437
  130.7 4.3 %update.1.before = f32[2,512,512]{2,1,0:T(8,128)} custom-call(s32[2]{0:T(128)S(1)} %add_and_fusion.odd, f32[2,512,512]{2,1,0:T(8,128)} %tile_ref.7, f32[2,4,512,128]{3,2,1,0:T(8,128)} %get-tuple-element.28.grad, f32[2,6,128,128]{3,2,1,0:T(8,128)S(1)} %collective-permute-done.6.y_first.low_first.high_first, ...), custom_call_target="tpu_custom_call" | custom-call | bytes 8388608 | tf_op jit(solution)/shard_map/update/pallas_call | solution.py:599
  135.1 0.0 collective-permute-done.8.x_first
  135.1 0.0 collective-permute-done.9.x_second
  135.1 2.5 %columns.1 = f32[2,512,512]{2,1,0:T(8,128)} custom-call(s32[2]{0:T(128)S(1)} %add_and_fusion.odd, f32[2,512,512]{2,1,0:T(8,128)} %update.1.before, f32[2,512,128]{2,1,0:T(8,128)} %collective-permute-done.8.x_first, f32[2,512,128]{2,1,0:T(8,128)} %collective-permute-done.9.x_second, f32[4,512,128]{2,1,0:T(8,128)S(1)} %weights.1.scale.after), custom_call_target="tpu_custom_call", output_to_operand_aliasing={{}: (1, {})} | custom-call | tf_op jit(solution)/shard_map/columns/pallas_call | solution.py:613
  137.6 4.6 %all-to-all-done.2.pieces = f32[32,4,8,128]{3,2,1,0:T(8,128)S(1)} async-done(((f32[32,4,8,128]{3,2,1,0:T(8,128)}), f32[32,4,8,128]{3,2,1,0:T(8,128)S(1)}, u32[]{:S(2)}, u32[]{:S(2)}) %all-to-all-start.2) | async-done | bytes 524320 | tf_op jit(solution)/shard_map/all_to_all | solution.py:437
  142.1 0.8 join.1
  (11 shorter events, 0.0 us)
Async XLA Ops:
  1.4 1.6 %copy-start = (f32[2,512,512]{2,1,0:T(8,128)S(1)}, f32[2,512,512]{2,1,0:T(8,128)}, u32[]{:S(2)}) copy-start(f32[2,512,512]{2,1,0:T(8,128)} %tile_ref.7) | copy-start | bytes 6291460
  3.0 0.7 copy-start.8
  3.6 8.5 %copy-start.5 = (f32[1,1,8,256,256]{4,3,2,1,0:T(8,128)S(1)}, f32[1,1,8,256,256]{4,3,2,1,0:T(8,128)}, u32[]{:S(2)}) copy-start(f32[1,1,8,256,256]{4,3,2,1,0:T(8,128)} %param.11) | copy-start | bytes 6291460
  4.3 26.7 %collective-permute-start = (f32[2,520,128]{2,1,0:T(8,128)S(1)}, f32[2,520,128]{2,1,0:T(8,128)S(1)}, u32[]{:S(2)}, u32[]{:S(2)}) collective-permute-start(f32[2,520,128]{2,1,0:T(8,128)S(1)} %get-tuple-element.20), channel_id=1, source_target_pairs={{1,2},{2,1},{3,4},{4,3},{5,6},{6,5},{7,8},{8,7},{9,10},{10,9},{11,... | collective-permute-start | bytes 1597448 | tf_op jit(solution)/shard_map/ppermute | solution.py:411
  7.9 23.1 %collective-permute-start.1 = (f32[2,520,128]{2,1,0:T(8,128)S(1)}, f32[2,520,128]{2,1,0:T(8,128)S(1)}, u32[]{:S(2)}, u32[]{:S(2)}) collective-permute-start(f32[2,520,128]{2,1,0:T(8,128)S(1)} %get-tuple-element.21), channel_id=1, source_target_pairs={{0,1},{1,0},{2,3},{3,2},{4,5},{5,4},{6,7},{7,6},{8,9},{9,8},{10,11... | collective-permute-start | bytes 1597448 | tf_op jit(solution)/shard_map/ppermute | solution.py:411
  8.0 32.5 %collective-permute-start.2 = (f32[2,128,512]{2,1,0:T(8,128)S(1)}, f32[2,128,512]{2,1,0:T(8,128)S(1)}, u32[]{:S(2)}, u32[]{:S(2)}) collective-permute-start(f32[2,128,512]{2,1,0:T(8,128)S(1)} %get-tuple-element.22), channel_id=1, source_target_pairs={{16,32},{32,16},{48,64},{64,48},{80,96},{96,80},{112,128},{128,112... | collective-permute-start | bytes 1572872 | tf_op jit(solution)/shard_map/ppermute | solution.py:411
  12.0 28.5 %collective-permute-start.3 = (f32[2,128,512]{2,1,0:T(8,128)S(1)}, f32[2,128,512]{2,1,0:T(8,128)S(1)}, u32[]{:S(2)}, u32[]{:S(2)}) collective-permute-start(f32[2,128,512]{2,1,0:T(8,128)S(1)} %get-tuple-element.23), channel_id=1, source_target_pairs={{0,16},{16,0},{32,48},{48,32},{64,80},{80,64},{96,112},{112,96},{1... | collective-permute-start | bytes 1572872 | tf_op jit(solution)/shard_map/ppermute | solution.py:411
  12.2 1.0 copy-start.6
  13.2 1.0 copy-start.7
  14.1 16.9 %copy-start.9 = (s32[2,1,1,8]{3,2,1,0:T(1,128)S(1)}, s32[2,1,1,8]{3,2,1,0:T(1,128)}, u32[]{:S(2)}) copy-start(s32[2,1,1,8]{3,2,1,0:T(1,128)} %param.12) | copy-start | bytes 196
  14.1 22.0 %copy-start.3 = (bf16[4,768,256]{2,1,0:T(8,128)(2,1)S(1)}, bf16[4,768,256]{2,1,0:T(8,128)(2,1)}, u32[]{:S(2)}) copy-start(bf16[4,768,256]{2,1,0:T(8,128)(2,1)} %constant.24.clone.right) | copy-start | bytes 4718596
  14.2 22.0 %copy-start.4 = (bf16[4,256,768]{2,1,0:T(8,128)(2,1)S(1)}, bf16[4,256,768]{2,1,0:T(8,128)(2,1)}, u32[]{:S(2)}) copy-start(bf16[4,256,768]{2,1,0:T(8,128)(2,1)} %constant.23.clone.left) | copy-start | bytes 4718596
  15.5 20.7 %copy-start.1 = (f32[2,512,512]{2,1,0:T(8,128)S(1)}, f32[2,512,512]{2,1,0:T(8,128)}, u32[]{:S(2)}) copy-start(f32[2,512,512]{2,1,0:T(8,128)} %tile_ref.7) | copy-start | bytes 6291460
  15.5 20.7 %copy-start.2 = (f32[2,256,256]{2,1,0:T(8,128)S(1)}, f32[2,256,256]{2,1,0:T(8,128)}, u32[]{:S(2)}) copy-start(f32[2,256,256]{2,1,0:T(8,128)} %probe.7) | copy-start | bytes 1572868
  31.6 8.9 %collective-permute-start.4 = (f32[2,2,144,128]{3,2,1,0:T(8,128)S(1)}, f32[2,2,144,128]{3,2,1,0:T(8,128)S(1)}, u32[]{:S(2)}, u32[]{:S(2)}) collective-permute-start(f32[2,2,144,128]{3,2,1,0:T(8,128)S(1)} %get-tuple-element.24), channel_id=1, source_target_pairs={{16,32},{32,16},{48,64},{64,48},{80,96},{96,80},{112,128},{128,112... | collective-permute-start | bytes 884744 | tf_op jit(solution)/shard_map/ppermute | solution.py:411
  36.0 4.5 %collective-permute-start.5 = (f32[2,2,144,128]{3,2,1,0:T(8,128)S(1)}, f32[2,2,144,128]{3,2,1,0:T(8,128)S(1)}, u32[]{:S(2)}, u32[]{:S(2)}) collective-permute-start(f32[2,2,144,128]{3,2,1,0:T(8,128)S(1)} %get-tuple-element.25), channel_id=1, source_target_pairs={{0,16},{16,0},{32,48},{48,32},{64,80},{80,64},{96,112},{112,96},{1... | collective-permute-start | bytes 884744 | tf_op jit(solution)/shard_map/ppermute | solution.py:411
  48.3 33.3 %collective-permute-start.6 = (f32[2,6,128,128]{3,2,1,0:T(8,128)}, f32[2,6,128,128]{3,2,1,0:T(8,128)S(1)}, u32[]{:S(2)}, u32[]{:S(2)}) collective-permute-start(f32[2,6,128,128]{3,2,1,0:T(8,128)} %get-tuple-element.29), channel_id=1, source_target_pairs={{16,32},{32,16},{48,64},{64,48},{80,96},{96,80},{112,128},{128,112... | collective-permute-start | bytes 2359304 | tf_op jit(solution)/shard_map/ppermute | solution.py:411
  50.3 31.4 %collective-permute-start.7 = (f32[2,6,128,128]{3,2,1,0:T(8,128)}, f32[2,6,128,128]{3,2,1,0:T(8,128)S(1)}, u32[]{:S(2)}, u32[]{:S(2)}) collective-permute-start(f32[2,6,128,128]{3,2,1,0:T(8,128)} %get-tuple-element.30), channel_id=1, source_target_pairs={{0,16},{16,0},{32,48},{48,32},{64,80},{80,64},{96,112},{112,96},{1... | collective-permute-start | bytes 2359304 | tf_op jit(solution)/shard_map/ppermute | solution.py:411
  50.4 42.5 %all-to-all-start = ((f32[32,6,8,128]{3,2,1,0:T(8,128)}), f32[32,6,8,128]{3,2,1,0:T(8,128)S(1)}, u32[]{:S(2)}, u32[]{:S(2)}) async-start(f32[32,6,8,128]{3,2,1,0:T(8,128)} %get-tuple-element.36), calls=%async_computation | async-start | bytes 1572864 | tf_op jit(solution)/shard_map/all_to_all | solution.py:437
  93.6 14.4 %all-to-all-start.1 = ((f32[8,6,8,128]{3,2,1,0:T(8,128)}), f32[8,6,8,128]{3,2,1,0:T(8,128)S(1)}, u32[]{:S(2)}, u32[]{:S(2)}) async-start(f32[8,6,8,128]{3,2,1,0:T(8,128)} %plane_sum.1), calls=%async_computation.1 | async-start | bytes 393216 | tf_op jit(solution)/shard_map/all_to_all | solution.py:437
  100.6 34.5 %collective-permute-start.8 = (f32[2,512,128]{2,1,0:T(8,128)}, f32[2,512,128]{2,1,0:T(8,128)}, u32[]{:S(2)}, u32[]{:S(2)}) collective-permute-start(f32[2,512,128]{2,1,0:T(8,128)} %get-tuple-element.34), channel_id=1, source_target_pairs={{1,2},{2,1},{3,4},{4,3},{5,6},{6,5},{7,8},{8,7},{9,10},{10,9},{11,... | collective-permute-start | bytes 1572872 | tf_op jit(solution)/shard_map/ppermute | solution.py:411
  103.7 31.4 %collective-permute-start.9 = (f32[2,512,128]{2,1,0:T(8,128)}, f32[2,512,128]{2,1,0:T(8,128)}, u32[]{:S(2)}, u32[]{:S(2)}) collective-permute-start(f32[2,512,128]{2,1,0:T(8,128)} %get-tuple-element.35), channel_id=1, source_target_pairs={{0,1},{1,0},{2,3},{3,2},{4,5},{5,4},{6,7},{7,6},{8,9},{9,8},{10,11... | collective-permute-start | bytes 1572872 | tf_op jit(solution)/shard_map/ppermute | solution.py:411
  110.0 32.2 %all-to-all-start.2 = ((f32[32,4,8,128]{3,2,1,0:T(8,128)}), f32[32,4,8,128]{3,2,1,0:T(8,128)S(1)}, u32[]{:S(2)}, u32[]{:S(2)}) async-start(f32[32,4,8,128]{3,2,1,0:T(8,128)} %probe_rows.1), calls=%async_computation.2 | async-start | bytes 1048576 | tf_op jit(solution)/shard_map/all_to_all | solution.py:437
